TPU v7x, 32 devices: a whole 2x2x4 slice. The times are simulated.
32 devices in a mesh: dp: 8 (over z, core), fsdp: 4 (over y, x).
Axes of the slice: x: 2, y: 2, z: 4, core: 2. Of those that a mesh axis runs over, the one named last changes fastest.
Arguments:
- tokens: bfloat16 [32, 512, 1024], P(('dp', 'fsdp')), may hold values from -6 to 6
- segment_ids: int32 [32, 512], P(('dp', 'fsdp')), may hold values from 0 to 7, never falling along the last dimension, each value on 1 to 256 neighbouring positions
- rel_bucket: int32 [1023], replicated, may hold values from 0 to 511, as said below
- query_weight: float32 [1024, 1024], P(('dp', 'fsdp')), may hold values from -0.25 to 0.25
- query_bias: float32 [1024], P(('dp', 'fsdp')), may hold values from -3 to 3
- key_weight: float32 [1024, 1024], P(('dp', 'fsdp')), may hold values from -0.25 to 0.25
- key_bias: float32 [1024], P(('dp', 'fsdp')), may hold values from -3 to 3
- value_weight: float32 [1024, 1024], P(('dp', 'fsdp')), may hold values from -0.1875 to 0.1875
- value_bias: float32 [1024], P(('dp', 'fsdp')), may hold values from -3 to 3
- out_weight: float32 [1024, 1024], P(None, ('dp', 'fsdp')), may hold values from -0.75 to 0.75
- out_bias: float32 [1024], P(('dp', 'fsdp')), may hold values from -3 to 3
- attention_gain: float32 [1024], P(('dp', 'fsdp')), may hold values from 0.1 to 1.9
- attention_shift: float32 [1024], P(('dp', 'fsdp')), may hold values from -2 to 2
- up_weight: float32 [1024, 4096], P(('dp', 'fsdp')), may hold values from -0.1875 to 0.1875
- up_bias: float32 [4096], P(('dp', 'fsdp')), may hold values from -3 to 3
- down_weight: float32 [4096, 1024], P(None, ('dp', 'fsdp')), may hold values from -0.125 to 0.125
- down_bias: float32 [1024], P(('dp', 'fsdp')), may hold values from -3 to 3
- output_gain: float32 [1024], P(('dp', 'fsdp')), may hold values from 0.1 to 1.9
- output_shift: float32 [1024], P(('dp', 'fsdp')), may hold values from -2 to 2
- position_table: float32 [512, 1024], P(None, ('dp', 'fsdp')), may hold values from -6 to 6
- cotangent: bfloat16 [32, 512, 1024], P(('dp', 'fsdp')), may hold values from -8 to 8
Outputs:
- layer_out: bfloat16 [32, 512, 1024], P(('dp', 'fsdp'))
- tokens_grad: bfloat16 [32, 512, 1024], P(('dp', 'fsdp'))
- query_weight_grad: float32 [1024, 1024], P(('dp', 'fsdp'))
- query_bias_grad: float32 [1024], P(('dp', 'fsdp'))
- key_weight_grad: float32 [1024, 1024], P(('dp', 'fsdp'))
- key_bias_grad: float32 [1024], P(('dp', 'fsdp'))
- value_weight_grad: float32 [1024, 1024], P(('dp', 'fsdp'))
- value_bias_grad: float32 [1024], P(('dp', 'fsdp'))
- out_weight_grad: float32 [1024, 1024], P(None, ('dp', 'fsdp'))
- out_bias_grad: float32 [1024], P(('dp', 'fsdp'))
- attention_gain_grad: float32 [1024], P(('dp', 'fsdp'))
- attention_shift_grad: float32 [1024], P(('dp', 'fsdp'))
- up_weight_grad: float32 [1024, 4096], P(('dp', 'fsdp'))
- up_bias_grad: float32 [4096], P(('dp', 'fsdp'))
- down_weight_grad: float32 [4096, 1024], P(None, ('dp', 'fsdp'))
- down_bias_grad: float32 [1024], P(('dp', 'fsdp'))
- output_gain_grad: float32 [1024], P(('dp', 'fsdp'))
- output_shift_grad: float32 [1024], P(('dp', 'fsdp'))
- position_table_grad: float32 [512, 1024], P(None, ('dp', 'fsdp'))
Inputs may be any that keep to these rules, and one draw needn't show every extreme that they name: `segment_ids`: within each sequence the document numbers never fall; a document spans 1 to half of 512 tokens, and in each sequence one spans exactly that many. `rel_bucket`: never falls along its length; the entry for distance zero is half of 512, the first entry is 0 and the last is 511.
All inputs are finite; a program needn't handle non-finite values.
Results may differ from a plain program's by a relative error of at most 0.023.
Values may be sent and summed in bfloat16 or wider, within the bound.
No kernel may reach another device: no remote copies, remote signals or barrier semaphores. Data moves between devices by JAX's collectives and lax.ppermute only.
A program may use at most 384 MiB of HBM per device.

v0:
```python
import math

import jax
import jax.numpy as jnp
from jax import lax
from jax.sharding import PartitionSpec as P

HEADS = 16


NORM_EPS = 1e-07
SHARD_DIMS = (0, 0, 0, 0, 0, 0, 1, 0, 0, 0, 0, 0, 1, 0, 0, 0, 1)
MATRIX_SLOTS = (0, 2, 4, 6, 10, 12, 16)


def dense(left, right):
    return jnp.dot(left, right, preferred_element_type=jnp.float32)


def dense_transposed(left, right):
    return lax.dot_general(
        left, right, (((1,), (1,)), ((), ())), preferred_element_type=jnp.float32
    )


def inner_rows(left, right):
    return lax.dot_general(
        left, right, (((0,), (0,)), ((), ())), preferred_element_type=jnp.float32
    )


def column_sums(matrix):
    return jnp.sum(matrix.astype(jnp.float32), axis=0)


def layer_norm(values_in, gain_vec, shift_vec):
    row_mean = jnp.mean(values_in, axis=-1, keepdims=True)
    centered = values_in - row_mean
    row_variance = jnp.mean(centered * centered, axis=-1, keepdims=True)
    return centered * lax.rsqrt(row_variance + NORM_EPS) * gain_vec + shift_vec


def gelu_exact(values_in):
    return jax.nn.gelu(values_in, approximate=False)


def skew_rows(table, rows, cols):
    heads = table.shape[0]
    span = table.shape[2]
    flat = table.reshape(heads, rows * span)
    part = flat[:, rows - 1 : rows - 1 + rows * (span - 1)]
    return part.reshape(heads, rows, span - 1)[:, :, :cols]


def unskew_rows(values, rows, span):
    heads = values.shape[0]
    cols = values.shape[2]
    widened = jnp.pad(values, ((0, 0), (0, 0), (0, span - 1 - cols)))
    flat = widened.reshape(heads, rows * (span - 1))
    return jnp.pad(flat, ((0, 0), (rows - 1, 1))).reshape(heads, rows, span)


def sequence_pass(weight_list, token_rows, segment_row, cot_rows, bucket_table):
    (
        query_weight,
        query_bias,
        key_weight,
        key_bias,
        value_weight,
        value_bias,
        out_weight,
        out_bias,
        attention_gain,
        attention_shift,
        up_weight,
        up_bias,
        down_weight,
        down_bias,
        output_gain,
        output_shift,
        position_table,
    ) = weight_list
    low_type = jnp.bfloat16
    seq_len = token_rows.shape[0]
    width = token_rows.shape[1]
    head_size = width // HEADS
    bucket_count = position_table.shape[0]
    score_scale = 1.0 / math.sqrt(3.0 * head_size)
    inputs = token_rows.astype(jnp.float32)
    queries = (dense(token_rows, query_weight) + query_bias.astype(jnp.float32)).astype(low_type)
    keys_all = (dense(token_rows, key_weight) + key_bias.astype(jnp.float32)).astype(low_type)
    values_all = (dense(token_rows, value_weight) + value_bias.astype(jnp.float32)).astype(low_type)
    pos_keys = (dense(position_table, key_weight) + key_bias.astype(jnp.float32)).astype(low_type)
    pos_queries = (dense(position_table, query_weight) + query_bias.astype(jnp.float32)).astype(
        low_type
    )
    query_split_heads = queries.reshape(seq_len, HEADS, head_size)
    key_heads = keys_all.reshape(seq_len, HEADS, head_size)
    value_heads = values_all.reshape(seq_len, HEADS, head_size)
    position_key_split = pos_keys.reshape(bucket_count, HEADS, head_size)
    pos_query_heads = pos_queries.reshape(bucket_count, HEADS, head_size)
    block_rows = min(512, seq_len)
    span = seq_len + block_rows - 1
    offsets = jnp.arange(span, dtype=jnp.int32)
    bucket_ids = jnp.arange(bucket_count, dtype=jnp.int32)
    block_starts = list(range(0, seq_len, block_rows))

    def block_scores(start):
        pick_query = jnp.take(bucket_table, start + block_rows - 1 - offsets + seq_len - 1)
        pick_key = jnp.take(bucket_table, 2 * seq_len - 2 - start - offsets)
        near_keys = jnp.take(position_key_split, pick_query, axis=0)
        to_table = jnp.einsum(
            "rhe,whe->hrw", query_split_heads, near_keys, preferred_element_type=jnp.float32
        )
        to_content = skew_rows(to_table, block_rows, seq_len)
        near_queries = jnp.take(pos_query_heads, pick_key, axis=0)
        from_table = jnp.einsum(
            "jhe,whe->hjw", key_heads, near_queries, preferred_element_type=jnp.float32
        )
        from_content = skew_rows(from_table, seq_len, block_rows)
        content = jnp.einsum(
            "ihe,jhe->hij", query_split_heads, key_heads, preferred_element_type=jnp.float32
        )
        raw_scores = (content + to_content + from_content.transpose(0, 2, 1)) * score_scale
        same_doc = segment_row[:, None] == segment_row[None, :]
        masked_scores = jnp.where(same_doc[None], raw_scores, -1e30)
        return (masked_scores, pick_query, pick_key)

    context_blocks = []
    log_totals = []
    for start in block_starts:
        masked_scores, _, _ = block_scores(start)
        soft = jax.nn.softmax(masked_scores, axis=-1)
        log_totals.append(jax.nn.logsumexp(masked_scores, axis=-1, keepdims=True))
        context_blocks.append(
            jnp.einsum(
                "hij,jhe->ihe",
                soft.astype(low_type),
                value_heads,
                preferred_element_type=jnp.float32,
            )
        )
    context = context_blocks[0].reshape(seq_len, width).astype(low_type)
    attn_out = dense(context, out_weight) + out_bias.astype(jnp.float32)
    mixed, first_norm_back = jax.vjp(
        layer_norm,
        inputs + attn_out,
        attention_gain.astype(jnp.float32),
        attention_shift.astype(jnp.float32),
    )
    mixed_low = mixed.astype(low_type)
    up_proj = dense(mixed_low, up_weight) + up_bias.astype(jnp.float32)
    activated_full, gelu_back = jax.vjp(gelu_exact, up_proj)
    activated = activated_full.astype(low_type)
    ffn_out = dense(activated, down_weight) + down_bias.astype(jnp.float32)
    layer_out, second_norm_back = jax.vjp(
        layer_norm,
        mixed + ffn_out,
        output_gain.astype(jnp.float32),
        output_shift.astype(jnp.float32),
    )
    grad_sum, output_gain_grad, output_shift_grad = second_norm_back(cot_rows.astype(jnp.float32))
    grad_ffn = grad_sum.astype(low_type)
    down_bias_grad = column_sums(grad_ffn)
    down_weight_grad = inner_rows(activated, grad_ffn)
    (grad_up_full,) = gelu_back(dense_transposed(grad_ffn, down_weight))
    grad_up = grad_up_full.astype(low_type)
    up_bias_grad = column_sums(grad_up)
    up_weight_grad = inner_rows(mixed_low, grad_up)
    grad_mixed = grad_sum + dense_transposed(grad_up, up_weight)
    grad_first, attention_gain_grad, attention_shift_grad = first_norm_back(grad_mixed)
    grad_attn = grad_first.astype(low_type)
    out_bias_grad = column_sums(grad_attn)
    out_weight_grad = inner_rows(context, grad_attn)
    grad_context = dense_transposed(grad_attn, out_weight).astype(low_type)
    context_heads = grad_context.reshape(seq_len, HEADS, head_size)
    grad_key_pos = jnp.zeros((HEADS, seq_len, bucket_count), jnp.float32)
    grad_key_content = jnp.zeros((seq_len, HEADS, head_size), jnp.float32)
    grad_value_sum = jnp.zeros((seq_len, HEADS, head_size), jnp.float32)
    query_content_parts = []
    query_pos_parts = []
    for block_number, start in enumerate(block_starts):
        masked_scores, pick_query, pick_key = block_scores(start)
        soft = jnp.exp(masked_scores - log_totals[block_number])
        grad_value_sum = jnp.einsum(
            "hij,ihe->jhe", soft.astype(low_type), context_heads, preferred_element_type=jnp.float32
        )
        grad_soft = jnp.einsum(
            "ihe,jhe->hij", context_heads, value_heads, preferred_element_type=jnp.float32
        )
        grad_scores = (
            soft * (grad_soft - jnp.sum(soft * grad_soft, axis=-1, keepdims=True))
        ).astype(low_type)
        query_content_parts.append(
            jnp.einsum("hij,jhe->ihe", grad_scores, key_heads, preferred_element_type=jnp.float32)
            * score_scale
        )
        grad_key_content = (
            jnp.einsum(
                "hij,ihe->jhe", grad_scores, query_split_heads, preferred_element_type=jnp.float32
            )
            * score_scale
        )
        onehot_query = (pick_query[:, None] == bucket_ids[None, :]).astype(low_type)
        onehot_key = (pick_key[:, None] == bucket_ids[None, :]).astype(low_type)
        spread_query = unskew_rows(grad_scores, block_rows, span)
        query_pos_parts.append(
            jnp.einsum(
                "hrw,wb->hrb", spread_query, onehot_query, preferred_element_type=jnp.float32
            )
            * score_scale
        )
        spread_key = unskew_rows(grad_scores.transpose(0, 2, 1), seq_len, span)
        grad_key_pos = (
            jnp.einsum("hjw,wb->hjb", spread_key, onehot_key, preferred_element_type=jnp.float32)
            * score_scale
        )
    query_position_gradient = query_pos_parts[0].astype(low_type)
    grad_key_pos_low = grad_key_pos.astype(low_type)
    grad_queries = (
        (
            query_content_parts[0]
            + jnp.einsum(
                "vyz,zvp->yvp",
                query_position_gradient,
                position_key_split,
                preferred_element_type=jnp.float32,
            )
        )
        .reshape(seq_len, width)
        .astype(low_type)
    )
    grad_pos_keys = (
        jnp.einsum(
            "npz,pnv->znv",
            query_position_gradient,
            query_split_heads,
            preferred_element_type=jnp.float32,
        )
        .reshape(bucket_count, width)
        .astype(low_type)
    )
    grad_keys = (
        (
            grad_key_content
            + jnp.einsum(
                "hjb,bhe->jhe",
                grad_key_pos_low,
                pos_query_heads,
                preferred_element_type=jnp.float32,
            )
        )
        .reshape(seq_len, width)
        .astype(low_type)
    )
    grad_pos_queries = (
        jnp.einsum("hjb,jhe->bhe", grad_key_pos_low, key_heads, preferred_element_type=jnp.float32)
        .reshape(bucket_count, width)
        .astype(low_type)
    )
    grad_values = grad_value_sum.reshape(seq_len, width).astype(low_type)
    query_weight_grad = inner_rows(token_rows, grad_queries) + inner_rows(
        position_table, grad_pos_queries
    )
    query_bias_grad = column_sums(grad_queries) + column_sums(grad_pos_queries)
    key_weight_grad = inner_rows(token_rows, grad_keys) + inner_rows(position_table, grad_pos_keys)
    key_bias_grad = column_sums(grad_keys) + column_sums(grad_pos_keys)
    value_weight_grad = inner_rows(token_rows, grad_values)
    value_bias_grad = column_sums(grad_values)
    position_table_grad = dense_transposed(grad_pos_keys, key_weight) + dense_transposed(
        grad_pos_queries, query_weight
    )
    input_grad = (
        grad_first
        + dense_transposed(grad_queries, query_weight)
        + dense_transposed(grad_keys, key_weight)
        + dense_transposed(grad_values, value_weight)
    )
    grads = (
        query_weight_grad,
        query_bias_grad,
        key_weight_grad,
        key_bias_grad,
        value_weight_grad,
        value_bias_grad,
        out_weight_grad,
        out_bias_grad,
        attention_gain_grad,
        attention_shift_grad,
        up_weight_grad,
        up_bias_grad,
        down_weight_grad,
        down_bias_grad,
        output_gain_grad,
        output_shift_grad,
        position_table_grad,
    )
    return (layer_out.astype(low_type), input_grad.astype(low_type), grads)


def owner_layout(totals, parts):
    laid = []
    for slot, member in enumerate(totals):
        if slot in MATRIX_SLOTS:
            oriented = member.T if SHARD_DIMS[slot] == 1 else member
            laid.append(oriented.reshape(8 * parts, -1))
        else:
            laid.append(member)
    return laid


def restore_layout(owned, totals):
    restored = []
    for slot, member in enumerate(owned):
        if slot in MATRIX_SLOTS:
            whole = totals[slot]
            columns = whole.shape[0] if SHARD_DIMS[slot] == 1 else whole.shape[1]
            piece = member.reshape(-1, columns)
            restored.append(piece.T if SHARD_DIMS[slot] == 1 else piece)
        else:
            restored.append(member)
    return restored


def per_device(
    tokens,
    segment_ids,
    rel_bucket,
    query_weight,
    query_bias,
    key_weight,
    key_bias,
    value_weight,
    value_bias,
    out_weight,
    out_bias,
    attention_gain,
    attention_shift,
    up_weight,
    up_bias,
    down_weight,
    down_bias,
    output_gain,
    output_shift,
    position_table,
    cotangent,
):
    low_type = jnp.bfloat16
    gathered = (
        lax.all_gather(query_weight.astype(low_type), ("dp", "fsdp"), axis=0, tiled=True),
        lax.all_gather(query_bias.astype(low_type), ("dp", "fsdp"), axis=0, tiled=True),
        lax.all_gather(key_weight.astype(low_type), ("dp", "fsdp"), axis=0, tiled=True),
        lax.all_gather(key_bias.astype(low_type), ("dp", "fsdp"), axis=0, tiled=True),
        lax.all_gather(value_weight.astype(low_type), ("dp", "fsdp"), axis=0, tiled=True),
        lax.all_gather(value_bias.astype(low_type), ("dp", "fsdp"), axis=0, tiled=True),
        lax.all_gather(out_weight.astype(low_type), ("dp", "fsdp"), axis=1, tiled=True),
        lax.all_gather(out_bias.astype(low_type), ("dp", "fsdp"), axis=0, tiled=True),
        lax.all_gather(attention_gain.astype(low_type), ("dp", "fsdp"), axis=0, tiled=True),
        lax.all_gather(attention_shift.astype(low_type), ("dp", "fsdp"), axis=0, tiled=True),
        lax.all_gather(up_weight.astype(low_type), ("dp", "fsdp"), axis=0, tiled=True),
        lax.all_gather(up_bias.astype(low_type), ("dp", "fsdp"), axis=0, tiled=True),
        lax.all_gather(down_weight.astype(low_type), ("dp", "fsdp"), axis=1, tiled=True),
        lax.all_gather(down_bias.astype(low_type), ("dp", "fsdp"), axis=0, tiled=True),
        lax.all_gather(output_gain.astype(low_type), ("dp", "fsdp"), axis=0, tiled=True),
        lax.all_gather(output_shift.astype(low_type), ("dp", "fsdp"), axis=0, tiled=True),
        lax.all_gather(position_table.astype(low_type), ("dp", "fsdp"), axis=1, tiled=True),
    )
    weight_list = tuple(gathered)
    layer_out, input_grad, totals = sequence_pass(
        weight_list, tokens[0], segment_ids[0], cotangent[0], rel_bucket
    )
    parts = lax.axis_size("dp") * lax.axis_size("fsdp")
    laid = owner_layout(totals, parts)
    owned = (
        lax.psum_scatter(laid[0], ("dp", "fsdp"), scatter_dimension=0, tiled=True),
        lax.psum_scatter(laid[1], ("dp", "fsdp"), scatter_dimension=0, tiled=True),
        lax.psum_scatter(laid[2], ("dp", "fsdp"), scatter_dimension=0, tiled=True),
        lax.psum_scatter(laid[3], ("dp", "fsdp"), scatter_dimension=0, tiled=True),
        lax.psum_scatter(laid[4], ("dp", "fsdp"), scatter_dimension=0, tiled=True),
        lax.psum_scatter(laid[5], ("dp", "fsdp"), scatter_dimension=0, tiled=True),
        lax.psum_scatter(laid[6], ("dp", "fsdp"), scatter_dimension=0, tiled=True),
        lax.psum_scatter(laid[7], ("dp", "fsdp"), scatter_dimension=0, tiled=True),
        lax.psum_scatter(laid[8], ("dp", "fsdp"), scatter_dimension=0, tiled=True),
        lax.psum_scatter(laid[9], ("dp", "fsdp"), scatter_dimension=0, tiled=True),
        lax.psum_scatter(laid[10], ("dp", "fsdp"), scatter_dimension=0, tiled=True),
        lax.psum_scatter(laid[11], ("dp", "fsdp"), scatter_dimension=0, tiled=True),
        lax.psum_scatter(laid[12], ("dp", "fsdp"), scatter_dimension=0, tiled=True),
        lax.psum_scatter(laid[13], ("dp", "fsdp"), scatter_dimension=0, tiled=True),
        lax.psum_scatter(laid[14], ("dp", "fsdp"), scatter_dimension=0, tiled=True),
        lax.psum_scatter(laid[15], ("dp", "fsdp"), scatter_dimension=0, tiled=True),
        lax.psum_scatter(laid[16], ("dp", "fsdp"), scatter_dimension=0, tiled=True),
    )
    restored = restore_layout(tuple(owned), totals)
    return (layer_out[None], input_grad[None]) + tuple(restored)


def solution(mesh):
    return jax.shard_map(
        per_device,
        mesh=mesh,
        in_specs=(
            P(("dp", "fsdp"), None, None),
            P(("dp", "fsdp"), None),
            P(),
            P(("dp", "fsdp"), None),
            P(("dp", "fsdp")),
            P(("dp", "fsdp"), None),
            P(("dp", "fsdp")),
            P(("dp", "fsdp"), None),
            P(("dp", "fsdp")),
            P(None, ("dp", "fsdp")),
            P(("dp", "fsdp")),
            P(("dp", "fsdp")),
            P(("dp", "fsdp")),
            P(("dp", "fsdp"), None),
            P(("dp", "fsdp")),
            P(None, ("dp", "fsdp")),
            P(("dp", "fsdp")),
            P(("dp", "fsdp")),
            P(("dp", "fsdp")),
            P(None, ("dp", "fsdp")),
            P(("dp", "fsdp"), None, None),
        ),
        out_specs=(
            P(("dp", "fsdp"), None, None),
            P(("dp", "fsdp"), None, None),
            P(("dp", "fsdp"), None),
            P(("dp", "fsdp")),
            P(("dp", "fsdp"), None),
            P(("dp", "fsdp")),
            P(("dp", "fsdp"), None),
            P(("dp", "fsdp")),
            P(None, ("dp", "fsdp")),
            P(("dp", "fsdp")),
            P(("dp", "fsdp")),
            P(("dp", "fsdp")),
            P(("dp", "fsdp"), None),
            P(("dp", "fsdp")),
            P(None, ("dp", "fsdp")),
            P(("dp", "fsdp")),
            P(("dp", "fsdp")),
            P(("dp", "fsdp")),
            P(None, ("dp", "fsdp")),
        ),
        check_vma=False,
    )
```

profile of v0, /device:TPU:0, one launch (start us, length us, event | category | flops | bytes accessed | tf_op | source)
XLA Modules:
  0.0 2395.2 jit_solution(9984242923094970024)
XLA Ops:
  26.3 42.3 %all-reduce.24 = (bf16[1024]{0:T(1024)(128)(2,1)S(1)}, bf16[1024]{0:T(1024)(128)(2,1)S(1)}, bf16[1024]{0:T(1024)(128)(2,1)S(1)}, bf16[1024]{0:T(1024)(128)(2,1)S...) all-reduce(bf16[1024]{0:T(1024)(128)(2,1)S(1)} %dynamic-update-slic, ...), channel_id=1, replica_groups=mesh['dp'=8,'fsdp'=4] {'dp','fsdp'}, use_global_device_ids=true, to_apply=%add.4 | all-reduce | flops 9216 | bytes 36864
  72.0 65.8 %all-gather = bf16[32,1,128]{2,1,0:T(2,128)(2,1)S(1)} all-gather(bf16[1,1,128]{2,1,0:T(2,128)(2,1)S(1)} %convert_bitcast_fusion.1), channel_id=1, replica_groups=mesh['dp'=8,'fsdp'=4] {'dp','fsdp'}, dimensions={0}, use_global_device_ids=true | all-gather | bytes 8448 | tf_op jit(solution)/shard_map/all_gather | solution.py:361
  147.8 38.1 %all-gather.11.cloned.1.call-done = bf16[1024,1024]{1,0:T(8,128)(2,1)} async-done(((bf16[32,1024]{1,0:T(8,128)(2,1)}), bf16[1024,1024]{1,0:T(8,128)(2,1)}) %all-gather.11.cloned.1.call-update) | async-done | bytes 2097168 | tf_op jit(solution)/shard_map/all_gather | solution.py:350
  262.0 40.7 %reshape.284 = f32[16,523776]{1,0:T(8,128)} reshape(f32[16,512,1023]{2,1,0:T(8,128)} %fusion.17) | data formatting | bytes 67043328 | tf_op jit(solution)/shard_map/reshape | solution.py:50
  302.7 25.6 %slice.26 = f32[16,523264]{1,0:T(8,128)} slice(f32[16,523776]{1,0:T(8,128)} %reshape.284), slice={[0:16], [511:523775]} | slice | bytes 66977792 | tf_op jit(solution)/shard_map/slice | solution.py:51
  328.3 53.1 %reshape.285 = f32[16,512,1022]{2,1,0:T(8,128)} reshape(f32[16,523264]{1,0:T(8,128)} %slice.26) | data formatting | bytes 66977792 | tf_op jit(solution)/shard_map/reshape | solution.py:52
  410.8 41.8 %reshape.287 = f32[16,523776]{1,0:T(8,128)} reshape(f32[16,512,1023]{2,1,0:T(8,128)} %fusion.15) | data formatting | bytes 67043328 | tf_op jit(solution)/shard_map/reshape | solution.py:50
  452.6 25.7 %slice.28 = f32[16,523264]{1,0:T(8,128)} slice(f32[16,523776]{1,0:T(8,128)} %reshape.287), slice={[0:16], [511:523775]} | slice | bytes 66977792 | tf_op jit(solution)/shard_map/slice | solution.py:51
  478.3 51.6 %reshape.288 = f32[16,512,1022]{2,1,0:T(8,128)} reshape(f32[16,523264]{1,0:T(8,128)} %slice.28) | data formatting | bytes 66977792 | tf_op jit(solution)/shard_map/reshape | solution.py:52
  535.4 19.7 fusion.54
  574.6 28.1 %multiply_convert_fusion.3 = (bf16[512,4096]{1,0:T(8,128)(2,1)}, f32[512,4096]{1,0:T(8,128)}, f32[512,4096]{1,0:T(8,128)}) fusion(f32[4096]{0:T(1024)S(1)} %bitcast.184, bf16[1024,4096]{1,0:T(8,128)(2,1)} %all-gather.19.cloned.1.call-done, f32[512,1024]{1,0:T(8,128)S(1)} %get-tuple-element.67, f32[1024]{0:T(1024)S(1)} %copy-done.58, ...), kind=kOutput, calls=%fused_computation.23 | convolution fusion | flops 4436000768 | bytes 31485952 | tf_op jit(solution)/shard_map/dot_general | solution.py:17
  693.5 43.6 %reshape.290 = bf16[16,523264]{1,0:T(8,128)(2,1)} reshape(bf16[16,512,1022]{2,1,0:T(8,128)(2,1)} %pad.14.clone) | data formatting | bytes 33488896 | tf_op jit(solution)/shard_map/reshape | solution.py:59
  752.4 45.4 %reshape.291 = bf16[16,512,1023]{2,1,0:T(8,128)(2,1)} reshape(bf16[16,523776]{1,0:T(8,128)(2,1)} %pad.15) | data formatting | bytes 33521664 | tf_op jit(solution)/shard_map/reshape | solution.py:60
  829.2 43.6 %reshape.292 = bf16[16,523264]{1,0:T(8,128)(2,1)} reshape(bf16[16,512,1022]{2,1,0:T(8,128)(2,1)} %pad.16) | data formatting | bytes 33488896 | tf_op jit(solution)/shard_map/reshape | solution.py:59
  888.1 45.6 %reshape.293 = bf16[16,512,1023]{2,1,0:T(8,128)(2,1)} reshape(bf16[16,523776]{1,0:T(8,128)(2,1)} %pad.17) | data formatting | bytes 33521664 | tf_op jit(solution)/shard_map/reshape | solution.py:60
  1066.1 20.4 reshape.304
  1098.6 20.4 reshape.302
  1120.6 40.9 %all-reduce.23 = (f32[1024]{0:T(1024)S(1)}, f32[1024]{0:T(1024)S(1)}, f32[1024]{0:T(1024)S(1)}, f32[1024]{0:T(1024)S(1)}, f32[1024]{0:T(1024)S(1)}, /*index=5*/f...) all-reduce(f32[1024]{0:T(1024)S(1)} %add.262, ...), channel_id=3, replica_groups=mesh['dp'=8,'fsdp'=4] {'dp','fsdp'}, use_global_device_ids=true, to_apply=%region_15.18.clone | all-reduce | flops 13312 | bytes 106496
  1177.0 65.5 %reduce-scatter.14.cloned.1.call-done = f32[8,4096]{1,0:T(8,128)} async-done(((f32[256,4096]{1,0:T(8,128)}), f32[8,4096]{1,0:T(8,128)}) %reduce-scatter.14.cloned.1.call-update) | async-done | bytes 131088 | tf_op jit(solution)/shard_map/reduce_scatter | solution.py:381
  1244.0 139.4 %reduce-scatter.10.cloned.1.call-done = f32[8,4096]{1,0:T(8,128)} async-done(((f32[256,4096]{1,0:T(8,128)}), f32[8,4096]{1,0:T(8,128)}) %reduce-scatter.10.cloned.1.call-update) | async-done | bytes 131088 | tf_op jit(solution)/shard_map/reduce_scatter | solution.py:377
  1385.0 140.5 %reduce-scatter.8.cloned.1.call-done = f32[8,4096]{1,0:T(8,128)} async-done(((f32[256,4096]{1,0:T(8,128)}), f32[8,4096]{1,0:T(8,128)}) %reduce-scatter.8.cloned.1.call-update) | async-done | bytes 131088 | tf_op jit(solution)/shard_map/reduce_scatter | solution.py:375
  1527.1 139.9 %reduce-scatter.12.cloned.1.call-done = f32[8,4096]{1,0:T(8,128)} async-done(((f32[256,4096]{1,0:T(8,128)}), f32[8,4096]{1,0:T(8,128)}) %reduce-scatter.12.cloned.1.call-update) | async-done | bytes 131088 | tf_op jit(solution)/shard_map/reduce_scatter | solution.py:379
  1668.6 356.5 %reduce-scatter.18.cloned.1.call-done = f32[8,16384]{1,0:T(8,128)} async-done(((f32[256,16384]{1,0:T(8,128)}), f32[8,16384]{1,0:T(8,128)}) %reduce-scatter.18.cloned.1.call-update) | async-done | bytes 524304 | tf_op jit(solution)/shard_map/reduce_scatter | solution.py:387
  2027.0 359.4 %reduce-scatter.16.cloned.1.call-done = f32[8,16384]{1,0:T(8,128)} async-done(((f32[256,16384]{1,0:T(8,128)}), f32[8,16384]{1,0:T(8,128)}) %reduce-scatter.16.cloned.1.call-update) | async-done | bytes 524304 | tf_op jit(solution)/shard_map/reduce_scatter | solution.py:385
  (368 shorter events, 486.3 us)
Async XLA Ops:
  7.3 61.4 %copy-start.52 = (s32[1,512]{1,0:T(1,128)S(1)}, s32[1,512]{1,0:T(1,128)}, u32[]{:S(2)}) copy-start(s32[1,512]{1,0:T(1,128)} %param.26) | copy-start | bytes 6148
  7.3 64.7 %copy-start.80 = (f32[128]{0:T(128)S(1)}, f32[128]{0:T(128)}, u32[]{:S(2)}) copy-start(f32[128]{0:T(128)} %param.39) | copy-start | bytes 1540
  7.3 132.9 %all-gather.15.cloned.1.call-start = ((), (), s32[]{:S(2)}) async-start(), calls=%async_computation.10 | async-start | bytes 1081344 | tf_op jit(solution)/shard_map/all_gather | solution.py:366
  8.9 131.3 %all-gather.13.cloned.1.call-start = ((), (), s32[]{:S(2)}) async-start(), calls=%async_computation.9 | async-start | bytes 2162688 | tf_op jit(solution)/shard_map/all_gather | solution.py:352
  10.5 175.4 %all-gather.11.cloned.1.call-start = ((), (), s32[]{:S(2)}) async-start(), calls=%async_computation.8 | async-start | bytes 2162688 | tf_op jit(solution)/shard_map/all_gather | solution.py:350
  12.1 517.8 %all-gather.9.cloned.1.call-start = ((), (), s32[]{:S(2)}) async-start(), calls=%async_computation.7 | async-start | bytes 2162688 | tf_op jit(solution)/shard_map/all_gather | solution.py:354
  13.7 555.9 %all-gather.17.cloned.1.call-start = ((), (), s32[]{:S(2)}) async-start(), calls=%async_computation.11 | async-start | bytes 2162688 | tf_op jit(solution)/shard_map/all_gather | solution.py:356
  15.3 559.2 %all-gather.19.cloned.1.call-start = ((), (), s32[]{:S(2)}) async-start(), calls=%async_computation.12 | async-start | bytes 8650752 | tf_op jit(solution)/shard_map/all_gather | solution.py:360
  17.2 585.5 %all-gather.21.cloned.1.call-start = ((), (), s32[]{:S(2)}) async-start(), calls=%async_computation.13 | async-start | bytes 8650752 | tf_op jit(solution)/shard_map/all_gather | solution.py:362
  19.0 1156.4 %reduce-scatter.20.cloned.1.call-start = ((), (), s32[]{:S(2)}) async-start(), calls=%async_computation.20 | async-start | bytes 2162688 | tf_op jit(solution)/shard_map/reduce_scatter | solution.py:391
  219.7 315.7 %copy-start.3 = (bf16[512,1024]{0,1:T(8,128)(2,1)}, bf16[512,1024]{0,1:T(8,128)(2,1)S(1)}, u32[]{:S(2)}) copy-start(bf16[512,1024]{0,1:T(8,128)(2,1)S(1)} %copy.92) | copy-start | bytes 3145732
  478.3 51.6 %copy-start.62 = (f32[1024]{0:T(1024)S(1)}, f32[1024]{0:T(1024)}, u32[]{:S(2)}) copy-start(f32[1024]{0:T(1024)} %convert_element_type.255) | copy-start | bytes 12292
  478.3 51.6 %copy-start.67 = (bf16[1,512,1024]{2,1,0:T(8,128)(2,1)S(1)}, bf16[1,512,1024]{2,1,0:T(8,128)(2,1)}, u32[]{:S(2)}) copy-start(bf16[1,512,1024]{2,1,0:T(8,128)(2,1)} %param.25) | copy-start | bytes 3145732
  573.3 66.6 %copy-start.19 = (f32[512,1024]{1,0:T(8,128)}, f32[512,1024]{1,0:T(8,128)S(1)}, u32[]{:S(2)}) copy-start(f32[512,1024]{1,0:T(8,128)S(1)} %get-tuple-element.67) | copy-start | bytes 6291460
  573.3 66.6 %copy-start.42 = (f32[512]{0:T(512)}, f32[512]{0:T(512)S(1)}, u32[]{:S(2)}) copy-start(f32[512]{0:T(512)S(1)} %broadcast_multiply_fusion.1) | copy-start | bytes 6148
  573.7 66.2 %copy-start.53 = (f32[512]{0:T(512)}, f32[512]{0:T(512)S(1)}, u32[]{:S(2)}) copy-start(f32[512]{0:T(512)S(1)} %fusion.45) | copy-start | bytes 6148
  819.4 135.6 %copy-start.23 = (bf16[16,64,512]{2,1,0:T(8,128)(2,1)}, bf16[16,64,512]{2,1,0:T(8,128)(2,1)S(1)}, u32[]{:S(2)}) copy-start(bf16[16,64,512]{2,1,0:T(8,128)(2,1)S(1)} %get-tuple-element.81) | copy-start | bytes 3145732
  965.8 276.6 %reduce-scatter.14.cloned.1.call-start = ((), (), s32[]{:S(2)}) async-start(), calls=%async_computation.17 | async-start | bytes 4325376 | tf_op jit(solution)/shard_map/reduce_scatter | solution.py:381
  976.2 407.2 %reduce-scatter.10.cloned.1.call-start = ((), (), s32[]{:S(2)}) async-start(), calls=%async_computation.15 | async-start | bytes 4325376 | tf_op jit(solution)/shard_map/reduce_scatter | solution.py:377
  1004.0 521.5 %reduce-scatter.8.cloned.1.call-start = ((), (), s32[]{:S(2)}) async-start(), calls=%async_computation.14 | async-start | bytes 4325376 | tf_op jit(solution)/shard_map/reduce_scatter | solution.py:375
  1030.2 636.7 %reduce-scatter.12.cloned.1.call-start = ((), (), s32[]{:S(2)}) async-start(), calls=%async_computation.16 | async-start | bytes 4325376 | tf_op jit(solution)/shard_map/reduce_scatter | solution.py:379
  1054.5 970.6 %reduce-scatter.18.cloned.1.call-start = ((), (), s32[]{:S(2)}) async-start(), calls=%async_computation.19 | async-start | bytes 17301504 | tf_op jit(solution)/shard_map/reduce_scatter | solution.py:387
  1086.5 1299.9 %reduce-scatter.16.cloned.1.call-start = ((), (), s32[]{:S(2)}) async-start(), calls=%async_computation.18 | async-start | bytes 17301504 | tf_op jit(solution)/shard_map/reduce_scatter | solution.py:385
  1172.8 1215.6 %copy-start.1 = (s32[1023]{0:T(1024)S(1)}, s32[1023]{0:T(1024)}, u32[]{:S(2)}) copy-start(s32[1023]{0:T(1024)} %param.27) | copy-start | bytes 12280
  (77 other events, 709.0 us)
Sparse Core Ops, SparseCore 0:
  11.7 56.4 all-gather.14
  71.7 55.3 all-gather.12
  130.6 55.2 all-gather.10
  189.2 55.2 all-gather.8
  247.7 55.2 all-gather.16
  306.3 76.3 all-gather.18
  386.2 76.1 all-gather.20
  966.0 135.9 reduce-scatter.19
  1104.4 138.0 reduce-scatter.13
  1244.6 138.7 reduce-scatter.9
  1385.8 139.6 reduce-scatter.7
  1527.7 139.1 reduce-scatter.11
  1669.4 355.6 reduce-scatter.17
  2027.3 359.0 reduce-scatter.15
where the time goes:
time: 2400 us
  waiting for transfers between devices  1240 us (52%)
  local copies, waits for them, and re-layouts  662 us (28%)
  matrix products  275 us (11%)
  blocking collectives  149 us (6%)
  other arithmetic  53.6 us (2%)
    reduce_scatter x1, waiting for transfers between devices, per_device(): lax.psum_scatter(laid[10], ('dp', 'fsdp'), scatter_dimension=0, tiled=True)  359 us
    reduce_scatter x1, waiting for transfers between devices, per_device(): lax.psum_scatter(laid[12], ('dp', 'fsdp'), scatter_dimension=0, tiled=True)  357 us
    reduce_scatter x1, waiting for transfers between devices, per_device(): lax.psum_scatter(laid[0], ('dp', 'fsdp'), scatter_dimension=0, tiled=True)  141 us
    reduce_scatter x1, waiting for transfers between devices, per_device(): lax.psum_scatter(laid[4], ('dp', 'fsdp'), scatter_dimension=0, tiled=True)  140 us
    reduce_scatter x1, waiting for transfers between devices, per_device(): lax.psum_scatter(laid[2], ('dp', 'fsdp'), scatter_dimension=0, tiled=True)  139 us
    reshape x2, local copies, waits for them, and re-layouts, skew_rows(): return part.reshape(heads, rows, span - 1)[:, :, :cols]  105 us
    reshape x2, local copies, waits for them, and re-layouts, unskew_rows(): return jnp.pad(flat, ((0, 0), (rows - 1, 1))).reshape(heads, rows, span)  91.1 us
    reshape x2, local copies, waits for them, and re-layouts, unskew_rows(): flat = widened.reshape(heads, rows * (span - 1))  87.2 us
  transfers between devices with their start and end apart: 14, of which 7 were waited for; matrix products, arithmetic and copies ran while one was open for 26% of the time, Pallas kernels for 0%

commit v1 on v0

v1 whole, which is shorter than its diff:
```python
import math
import jax, jax.numpy as jnp
from jax import lax
from jax.sharding import PartitionSpec as P
import jax.experimental.pallas as pl, jax.experimental.pallas.tpu as pltpu
HEADS=16
BF=jnp.bfloat16
F32=jnp.float32

def mm(a,b,ca,cb):
    return lax.dot_general(a,b,(((ca,),(cb,)),((),())),preferred_element_type=F32)

def attend_kernel(scale, q_ref,k_ref,v_ref,ek_ref,eq_ref,segc_ref,segr_ref,ctx_ref,p_ref):
    t=q_ref.shape[0]; half=t//2
    hd=q_ref.shape[1]//2
    same=segc_ref[...]==segr_ref[...]
    lane=lax.broadcasted_iota(jnp.int32,q_ref.shape,1)
    ctx=None
    for h in range(2):
        mine=(lane>=h*hd)&(lane<(h+1)*hd)
        pick=lambda r: jnp.where(mine,r[...],jnp.zeros((),BF))
        q=pick(q_ref); k=pick(k_ref)
        s=mm(q,k_ref[...],1,1)
        to=pltpu.roll(mm(q,ek_ref[...],1,1),half,1,stride=1,stride_axis=0)
        fr=pltpu.roll(mm(k,eq_ref[...],1,1),half,1,stride=1,stride_axis=0)
        s=jnp.where(same,s+to+fr.T,-1e30)
        top=jnp.max(s,axis=1,keepdims=True)
        e=jnp.exp((s-top)*scale)
        p=(e*(1.0/jnp.sum(e,axis=1,keepdims=True))).astype(BF)
        p_ref[h]=p
        part=mm(p,pick(v_ref),1,0)
        ctx=part if ctx is None else ctx+part
    ctx_ref[...]=ctx.astype(BF)

def attend(q,k,v,ek,eq,seg,scale):
    t,d=q.shape
    w=2*d//HEADS
    col=pl.BlockSpec((t,w),lambda i:(0,i))
    return pl.pallas_call(
        lambda *r: attend_kernel(scale,*r),
        grid=(HEADS//2,),
        in_specs=[col]*5+[pl.BlockSpec((t,1),lambda i:(0,0)),pl.BlockSpec((1,t),lambda i:(0,0))],
        out_specs=[col,pl.BlockSpec((2,t,t),lambda i:(i,0,0))],
        out_shape=[jax.ShapeDtypeStruct((t,d),BF),jax.ShapeDtypeStruct((HEADS,t,t),BF)],
        compiler_params=pltpu.CompilerParams(vmem_limit_bytes=48*2**20),
    )(q,k,v,ek,eq,seg.reshape(t,1),seg.reshape(1,t))

def attend_back_kernel(scale,q_ref,k_ref,v_ref,ek_ref,eq_ref,dc_ref,p_ref,dq_ref,dk_ref,dv_ref,dek_ref,deq_ref):
    t=q_ref.shape[0]; half=t//2
    hd=q_ref.shape[1]//2
    r=lax.broadcasted_iota(jnp.int32,(half,half),0); c=lax.broadcasted_iota(jnp.int32,(half,half),1)
    flip=(r+c==half-1).astype(BF)
    lane=lax.broadcasted_iota(jnp.int32,q_ref.shape,1)
    def turn(x):
        return jnp.concatenate([mm(flip,x[:half],1,0),mm(flip,x[half:],1,0)],0)
    def turn_t(x):
        return jnp.concatenate([mm(flip,x[:,:half],1,1),mm(flip,x[:,half:],1,1)],0)
    def unroll(x):
        return jnp.concatenate([pltpu.roll(x[:half],1,1,stride=1,stride_axis=0),pltpu.roll(x[half:],half+1,1,stride=1,stride_axis=0)],0)
    q_turned=turn(q_ref[...]).astype(BF); k_turned=turn(k_ref[...]).astype(BF)
    dqt=dkt=dv=dek=deq=None
    plus=lambda a,b: b if a is None else a+b
    for h in range(2):
        mine=(lane>=h*hd)&(lane<(h+1)*hd)
        pick=lambda x: jnp.where(mine,x,jnp.zeros((),BF))
        p=p_ref[h]; dc=pick(dc_ref[...])
        dp=mm(dc,v_ref[...],1,1)
        pf=p.astype(F32)
        w=pf*dp
        ds=(w-pf*jnp.sum(w,axis=1,keepdims=True)).astype(BF)
        dv=plus(dv,mm(p,dc,0,0))
        a=turn(ds).astype(BF); au=unroll(a)
        b=turn_t(ds).astype(BF); bu=unroll(b)
        dqt=plus(dqt,mm(a,pick(k_ref[...]),1,0)+mm(au,pick(ek_ref[...]),1,0))
        dkt=plus(dkt,mm(b,pick(q_ref[...]),1,0)+mm(bu,pick(eq_ref[...]),1,0))
        dek=plus(dek,mm(au,pick(q_turned),0,0))
        deq=plus(deq,mm(bu,pick(k_turned),0,0))
    dq_ref[...]=turn((dqt*scale).astype(BF)).astype(BF)
    dk_ref[...]=turn((dkt*scale).astype(BF)).astype(BF)
    dv_ref[...]=dv.astype(BF)
    dek_ref[...]=(dek*scale).astype(BF)
    deq_ref[...]=(deq*scale).astype(BF)

def attend_back(q,k,v,ek,eq,dc,p,scale):
    t,d=q.shape
    w=2*d//HEADS
    col=pl.BlockSpec((t,w),lambda i:(0,i))
    return pl.pallas_call(
        lambda *r: attend_back_kernel(scale,*r),
        grid=(HEADS//2,),
        in_specs=[col]*6+[pl.BlockSpec((2,t,t),lambda i:(i,0,0))],
        out_specs=[col]*5,
        out_shape=[jax.ShapeDtypeStruct((t,d),BF)]*5,
        compiler_params=pltpu.CompilerParams(vmem_limit_bytes=48*2**20),
    )(q,k,v,ek,eq,dc,p)


NORM_EPS = 1e-7
SPLIT = 9


def norm_parts(v):
    mean = jnp.mean(v, axis=-1, keepdims=True)
    c = v - mean
    r = lax.rsqrt(jnp.mean(c * c, axis=-1, keepdims=True) + NORM_EPS)
    return c * r, r


def norm_back(g, gain, n, r):
    u = g * gain
    d = r * (u - jnp.mean(u, -1, keepdims=True) - n * jnp.mean(u * n, -1, keepdims=True))
    return d, jnp.sum(g * n, 0), jnp.sum(g, 0)


class Tree:
    def __init__(self, width):
        self.nf, self.ndp = lax.axis_size("fsdp"), lax.axis_size("dp")
        self.n = self.nf * self.ndp
        self.nz = self.ndp // 2
        self.rows = width // self.n
        self.width = width

    def place(self):
        me = lax.axis_index("dp") * self.nf + lax.axis_index("fsdp")
        d = lax.broadcasted_iota(jnp.int32, (self.width, self.width), 0)
        j = lax.broadcasted_iota(jnp.int32, (self.width, self.width), 1)
        rel = (d // self.rows) ^ me
        f = rel % self.nf
        core = (rel // self.nf) % 2
        z = rel // (2 * self.nf)
        at = ((core * self.nf + f) * self.nz + z) * self.rows + d % self.rows
        return (at == j).astype(BF)

    def swap(self, a, axis, bit):
        size = self.nf if axis == "fsdp" else self.ndp
        return lax.ppermute(a, axis, [(i, i ^ bit) for i in range(size)])

    def finish(self, mine, flipped):
        step = self.nz * self.rows
        parts = [mine[i * step : (i + 1) * step] for i in range(self.nf)]
        bits = [1 << b for b in range(self.nf.bit_length() - 1)]
        for bit in bits[::-1] if flipped else bits:
            live = [i for i in range(len(parts)) if parts[i] is not None]
            for i in live:
                if i & bit:
                    got = self.swap(parts[i], "fsdp", bit)
                    parts[i ^ bit] = (parts[i ^ bit].astype(F32) + got.astype(F32)).astype(BF)
                    parts[i] = None
        total = parts[0]
        bit = self.nz // 2
        while bit:
            h = total.shape[0] // 2
            got = self.swap(total[h:], "dp", 2 * bit)
            total = total[:h].astype(F32) + got.astype(F32)
            bit //= 2
            if bit:
                total = total.astype(BF)
        return total

    def core_sum(self, pairs):
        h = self.width // 2
        cat = lambda xs: xs[0] if len(xs) == 1 else jnp.concatenate(xs, 1)
        away = cat([mm(a[:, h:], b, 0, cb).astype(BF) for a, b, cb in pairs])
        got = self.swap(away, "dp", 1)
        mine = cat([mm(a[:, :h], b, 0, cb) for a, b, cb in pairs])
        return (mine + got.astype(F32)).astype(BF)


def per_device(
    tokens, segment_ids, rel_bucket, query_weight, query_bias, key_weight, key_bias, value_weight, value_bias,
    out_weight, out_bias, attention_gain, attention_shift, up_weight, up_bias, down_weight, down_bias,
    output_gain, output_shift, position_table, cotangent,
):
    x = tokens[0]
    t, d = x.shape
    seg = segment_ids[0]
    tree = Tree(d)
    rows = tree.rows
    ff = up_weight.shape[1]
    spread = ff // d
    buckets = position_table.shape[0]
    scale = 1.0 / math.sqrt(3.0 * (d // HEADS))
    vectors = (query_bias, key_bias, value_bias, out_bias, attention_gain, attention_shift, down_bias, output_gain, output_shift)
    small = jnp.concatenate([v[:, None] for v in vectors] + [up_bias.reshape(spread, rows).T], axis=1).astype(BF)
    small = jnp.pad(small, ((0, 0), (0, 128 - small.shape[1])))
    first = jnp.concatenate(
        [query_weight.astype(BF), key_weight.astype(BF), value_weight.astype(BF), position_table.T.astype(BF), small], axis=1
    )
    second = jnp.concatenate([out_weight.T.astype(BF), up_weight.astype(BF), down_weight.T.astype(BF)], axis=1)
    w1 = lax.all_gather(first, ("dp", "fsdp"), axis=0, tiled=True)
    w2 = lax.all_gather(second, ("dp", "fsdp"), axis=0, tiled=True)
    wq, wk, wv = w1[:, :d], w1[:, d : 2 * d], w1[:, 2 * d : 3 * d]
    table_t = w1[:, 3 * d : 3 * d + buckets]
    vec = w1[:, 3 * d + buckets :].T.astype(F32)
    bq, bk, bv, bo, gain1, shift1, bd, gain2, shift2 = [vec[i] for i in range(SPLIT)]
    bu = vec[SPLIT : SPLIT + spread].reshape(spread, tree.n, rows).transpose(1, 0, 2).reshape(ff)
    wo_t, wu, wd_t = w2[:, :d], w2[:, d : d + ff], w2[:, d + ff :]

    half = t // 2
    picked = lax.rev(rel_bucket[t - half : 2 * t - half], (0,))
    onehot = (picked[:, None] == lax.broadcasted_iota(jnp.int32, (t, buckets), 1)).astype(BF)
    q = (mm(x, wq, 1, 0) + bq).astype(BF)
    k = (mm(x, wk, 1, 0) + bk).astype(BF)
    v = (mm(x, wv, 1, 0) + bv).astype(BF)
    spread_table = mm(onehot, table_t, 1, 1).astype(BF)
    ek = (mm(spread_table, wk, 1, 0) + bk).astype(BF)
    eq = (mm(spread_table, wq, 1, 0) + bq).astype(BF)
    context, probs = attend(q, k, v, ek, eq, seg, scale)

    place = tree.place()
    n1, r1 = norm_parts(x.astype(F32) + mm(context, wo_t, 1, 1) + bo)
    mixed = n1 * gain1 + shift1
    mixed_low = mixed.astype(BF)
    up = mm(mixed_low, wu, 1, 0) + bu
    cdf = 0.5 * (1.0 + lax.erf(up * math.sqrt(0.5)))
    act = (up * cdf).astype(BF)
    slope = cdf + up * (jnp.exp(-0.5 * up * up) * (1.0 / math.sqrt(2.0 * math.pi)))
    n2, r2 = norm_parts(mixed + mm(act, wd_t, 1, 1) + bd)
    layer_out = (n2 * gain2 + shift2).astype(BF)
    d_sum, d_gain2, d_shift2 = norm_back(cotangent[0].astype(F32), gain2, n2, r2)
    d_ffn = d_sum.astype(BF)
    d_bd = jnp.sum(d_ffn.astype(F32), 0)
    arrange = lambda m: mm(m, place, 1, 0).astype(BF)
    down_mine = tree.core_sum([(arrange(d_ffn), act, 0)])
    d_up = (mm(d_ffn, wd_t, 1, 0) * slope).astype(BF)
    d_bu = jnp.sum(d_up.astype(F32), 0)
    up_mine = tree.core_sum([(arrange(mixed_low), d_up, 0)])
    d_mixed = d_sum + mm(d_up, wu, 1, 1)
    d_first, d_gain1, d_shift1 = norm_back(d_mixed, gain1, n1, r1)
    d_attn = d_first.astype(BF)
    d_bo = jnp.sum(d_attn.astype(F32), 0)
    d_context = mm(d_attn, wo_t, 1, 0).astype(BF)
    out_mine = tree.core_sum([(arrange(d_attn), context, 0)])
    down_grad = tree.finish(down_mine, True)
    up_grad = tree.finish(up_mine, False)
    out_grad = tree.finish(out_mine, True)

    dq, dk, dv, dek, deq = attend_back(q, k, v, ek, eq, d_context, probs, scale)
    d_pos_keys = mm(onehot, dek, 0, 0).astype(BF)
    d_pos_queries = mm(onehot, deq, 0, 0).astype(BF)
    colsum = lambda m: jnp.sum(m.astype(F32), 0)
    d_bq = colsum(dq) + colsum(d_pos_queries)
    d_bk = colsum(dk) + colsum(d_pos_keys)
    d_bv = colsum(dv)
    x_arranged = arrange(x)
    table_arranged = mm(table_t, place, 0, 0).astype(BF)
    left = jnp.concatenate([x_arranged, table_arranged], 0)
    d_table = (mm(d_pos_keys, wk, 1, 1) + mm(d_pos_queries, wq, 1, 1)).astype(BF)
    lines = jnp.stack([d_bq, d_bk, d_bv, d_bo, d_gain1, d_shift1, d_bd, d_gain2, d_shift2])
    lines = jnp.concatenate([lines, d_bu.reshape(tree.n, spread, rows).transpose(1, 0, 2).reshape(spread, d)], 0)
    lines = jnp.pad(lines, ((0, 128 - lines.shape[0]), (0, 0))).astype(BF)
    rest_mine = tree.core_sum([
        (left, jnp.concatenate([dq, d_pos_queries], 0), 0),
        (left, jnp.concatenate([dk, d_pos_keys], 0), 0),
        (x_arranged, dv, 0),
        (place, d_table, 1),
        (place, lines, 1),
    ])
    rest = tree.finish(rest_mine, False)
    input_grad = (d_first + mm(dq, wq, 1, 1) + mm(dk, wk, 1, 1) + mm(dv, wv, 1, 1)).astype(BF)
    tail = rest[:, 3 * d + buckets :]
    vecs = [tail[:, i] for i in range(SPLIT)]
    d_up_bias = tail[:, SPLIT : SPLIT + spread].T.reshape(-1)
    return (
        layer_out[None], input_grad[None],
        rest[:, :d], vecs[0], rest[:, d : 2 * d], vecs[1], rest[:, 2 * d : 3 * d], vecs[2],
        out_grad.T, vecs[3], vecs[4], vecs[5], up_grad, d_up_bias, down_grad.T, vecs[6], vecs[7], vecs[8],
        rest[:, 3 * d : 3 * d + buckets].T,
    )


def solution(mesh):
    both = ("dp", "fsdp")
    row, col, vec = P(both, None), P(None, both), P(both)
    seq = P(both, None, None)
    params = (row, vec, row, vec, row, vec, col, vec, vec, vec, row, vec, col, vec, vec, vec, col)
    return jax.shard_map(
        per_device, mesh=mesh, in_specs=(seq, row, P()) + params + (seq,), out_specs=(seq, seq) + params, check_vma=False
    )
```

time: 2400 us -> 559 us (0.23)
  waiting for transfers between devices: 1240 us -> 281 us
  local copies, waits for them, and re-layouts: 662 us -> 11.9 us
  matrix products: 275 us -> 126 us
  blocking collectives: 149 us -> 0 us
  Pallas kernels: 0 us -> 66.3 us
    reduce_scatter x7 -> x0, waiting for transfers between devices: 1200 us -> none  [the longest x1 359 us: per_device(): lax.psum_scatter(laid[10], ('dp', 'fsdp'), scatter_dimension=0, tiled=True)]
    reshape x24 -> x5, local copies, waits for them, and re-layouts: 450 us -> 1.14 us  [the longest x1 0.6 us: per_device(): d_up_bias = tail[:, SPLIT:SPLIT + spread].T.reshape(-1)]
    dot_general x38 -> x40, matrix products: 275 us -> 126 us  [mm(): lax.dot_general(a, b, (((ca,), (cb,)), ((), ())), preferred_element_type=...]
    ppermute x0 -> x24, waiting for transfers between devices: none -> 142 us  [swap(): return lax.ppermute(a, axis, [(i, i ^ bit) for i in range(size)])]
    all_gather x7 -> x2, waiting for transfers between devices: 38.1 us -> 139 us  [the longest x1 75.3 us: per_device(): w2 = lax.all_gather(second, ('dp', 'fsdp'), axis=0, tiled=True)]
    unnamed x2 -> x0, blocking collectives: 83.2 us -> none
    pallas_call x0 -> x2, Pallas kernels: none -> 66.3 us  [the longest x1 33.4 us: attend(): pl.pallas_call(lambda *r: attend_kernel(scale, *r), grid=(HEADS // 2,), i...]
    all_gather x1 -> x0, blocking collectives: 65.8 us -> none  [per_device(): lax.all_gather(up_bias.astype(low_type), ('dp', 'fsdp'), axis=0, tiled=True)]
  transfers between devices with their start and end apart: 14 -> 26, of which waited for: 7 -> 16; matrix products, arithmetic and copies ran while one was open for 26% -> 14% of each run, Pallas kernels for 0% -> 6%
where the time goes in v1:
time: 559 us; the launch traced here: 555 us
  waiting for transfers between devices  281 us (50%)
  matrix products  126 us (23%)
  Pallas kernels  66.3 us (12%)
  other arithmetic  33 us (6%)
  starting transfers between devices  22 us (4%)
  between operations  15.3 us (3%)
  local copies, waits for them, and re-layouts  11.9 us (2%)
    ppermute x24, waiting for transfers between devices, swap(): return lax.ppermute(a, axis, [(i, i ^ bit) for i in range(size)])  142 us
    dot_general x40, matrix products, mm(): lax.dot_general(a, b, (((ca,), (cb,)), ((), ())), preferred_element_type=...  126 us
    all_gather x1, waiting for transfers between devices, per_device(): w2 = lax.all_gather(second, ('dp', 'fsdp'), axis=0, tiled=True)  75.3 us
    all_gather x1, waiting for transfers between devices, per_device(): w1 = lax.all_gather(first, ('dp', 'fsdp'), axis=0, tiled=True)  64.2 us
    pallas_call x1, Pallas kernels, attend(): pl.pallas_call(lambda *r: attend_kernel(scale, *r), grid=(HEADS // 2,), i...  33.4 us
    pallas_call x1, Pallas kernels, attend_back(): pl.pallas_call(lambda *r: attend_back_kernel(scale, *r), grid=(HEADS // 2...  33 us
    ppermute x24, starting transfers between devices, swap(): return lax.ppermute(a, axis, [(i, i ^ bit) for i in range(size)])  21.9 us
  transfers between devices with their start and end apart: 26, of which 16 were waited for; matrix products, arithmetic and copies ran while one was open for 14% of the time, Pallas kernels for 6%

profile of v1, /device:TPU:0, one launch (start us, length us, event | category | flops | bytes accessed | tf_op | source)
XLA Modules:
  0.0 555.3 jit_solution(9594872507011301236)
XLA Ops:
  24.5 4.7 fusion.21
  29.1 64.2 %all-gather.3.cloned.1.call-done = bf16[1024,3712]{1,0:T(8,128)(2,1)} async-done(((bf16[32,3712]{1,0:T(8,128)(2,1)}), bf16[1024,3712]{1,0:T(8,128)(2,1)}) %all-gather.3.cloned.1.call-update) | async-done | bytes 7602192 | tf_op jit(solution)/shard_map/all_gather | solution.py:190
  107.9 33.4 %shard_map.348 = (bf16[512,1024]{1,0:T(8,128)(2,1)S(1)}, bf16[16,512,512]{2,1,0:T(8,128)(2,1)}) custom-call(bf16[512,1024]{1,0:T(8,128)(2,1)S(1)} %fusion.62.r_0_, bf16[512,1024]{1,0:T(8,128)(2,1)S(1)} %fusion.63.r_1_, bf16[512,1024]{1,0:T(8,128)(2,1)S(1)} %fusion.64.r_2_, bf16[512,1024]{1,0:T(8,128)(2,1)S(1)} %add_convert_fusion.14.r_3_, ...), custom_call_target="tpu_custom_call" | custom-call | tf_op jit(solution)/shard_map/pallas_call | solution.py:39
  144.7 75.3 %all-gather.5.cloned.1.call-done = bf16[1024,9216]{1,0:T(8,128)(2,1)} async-done(((bf16[32,9216]{1,0:T(8,128)(2,1)}), bf16[1024,9216]{1,0:T(8,128)(2,1)}) %all-gather.5.cloned.1.call-update) | async-done | bytes 18874384 | tf_op jit(solution)/shard_map/all_gather | solution.py:191
  227.4 9.8 %multiply_convert_fusion = (bf16[512,4096]{1,0:T(8,128)(2,1)S(1)}, f32[512,4096]{1,0:T(8,128)}) fusion(f32[4096]{0:T(1024)S(1)} %add.299, bf16[1024,9216]{1,0:T(8,128)(2,1)} %all-gather.5.cloned.1.call-done, f32[512,1024]{1,0:T(8,128)S(1)} %get-tuple-element.75, f32[1024]{0:T(1024)S(1)} %get-tuple-element.43, f32[1024]{0:T(1024)S(1)} %get-tuple-element.44, ...), kind=kOutput, calls=%fused_computation.9 | convolution fusion | flops 4310171648 | bytes 23097344 | tf_op jit(solution)/shard_map/dot_general | solution.py:11
  237.1 9.4 %fusion.144 = (f32[512]{0:T(512)S(1)}, f32[512,1024]{1,0:T(8,128)S(1)}) fusion(f32[1024]{0:T(1024)S(1)} %get-tuple-element.42, bf16[512,4096]{1,0:T(8,128)(2,1)S(1)} %get-tuple-element.76, bf16[1024,9216]{1,0:T(8,128)(2,1)} %all-gather.5.cloned.1.call-done, f32[1024]{0:T(1024)S(1)} %get-tuple-element.43, f32[1024]{0:T(1024)S(1)} %get-tuple-element.44, ...), kind=kOutput, calls=%fused_computation.261 | convolution fusion | flops 4298636800 | bytes 16795648 | tf_op jit(solution)/shard_map/dot_general | solution.py:11
  252.9 10.6 %fusion.145 = (bf16[4096]{0:T(1024)(128)(2,1)S(1)}, bf16[512,4096]{1,0:T(8,128)(2,1)S(1)}) fusion(f32[512,4096]{1,0:T(8,128)} %get-tuple-element.77, f32[4096]{0:T(1024)S(1)} %add.299, bf16[1024,9216]{1,0:T(8,128)(2,1)} %all-gather.5.cloned.1.call-done, f32[512,1024]{1,0:T(8,128)S(1)} %get-tuple-element.59), kind=kOutput, calls=%fused_computation.262 | convolution fusion | flops 4320653312 | bytes 23093248 | tf_op jit(solution)/shard_map/dot_general | solution.py:11
  263.5 9.6 %multiply_reduce_fusion = (bf16[1024]{0:T(1024)(128)(2,1)S(1)}, f32[512]{0:T(512)S(1)}, f32[512]{0:T(512)S(1)}, bf16[1024]{0:T(1024)(128)(2,1)S(1)}, f32[512,1024]{1,0:T(8,128)S(1)}) fusion(f32[512,1024]{1,0:T(8,128)S(1)} %get-tuple-element.75, f32[512]{0:T(512)S(1)} %add_rsqrt_fusion.1, f32[512]{0:T(512)S(1)} %broadcast_multiply_fusion.5, ...), kind=kOutput, calls=%fused_computation.69 | convolution fusion | flops 4300207104 | bytes 18890752 | tf_op jit(solution)/shard_map/dot_general | solution.py:11
  281.2 33.0 %shard_map.349 = (bf16[512,1024]{1,0:T(8,128)(2,1)S(1)}, bf16[512,1024]{1,0:T(8,128)(2,1)S(1)}, bf16[512,1024]{1,0:T(8,128)(2,1)S(1)}, bf16[512,1024]{1,0:T(8,128)(2,1)S(1)}, bf16[512,1024]{1,0:T(8,128)(2,1)S(1)}) custom-call(bf16[512,1024]{1,0:T(8,128)(2,1)} %copy-done, bf16[512,1024]{1,0:T(8,128)(2,1)} %copy-done.1, bf16[512,1024]{1,0:T(8,128)(2,1)} %copy-done.3, ...), custom_call_target="tpu_custom_call" | custom-call | tf_op jit(solution)/shard_map/pallas_call | solution.py:88
  318.8 4.0 fusion.55
  337.5 4.4 convolution_convert_fusion.1
  342.2 4.7 convolution_convert_fusion
  360.1 4.0 collective-permute-done.8
  373.8 4.7 collective-permute-done.10
  383.5 5.0 add_convert_fusion.2
  390.7 4.9 add_convert_fusion.1
  397.9 4.6 add_convert_fusion
  404.3 8.3 %collective-permute-done.2 = bf16[128,3712]{1,0:T(8,128)(2,1)S(1)} collective-permute-done((bf16[128,3712]{1,0:T(8,128)(2,1)S(1)}, bf16[128,3712]{1,0:T(8,128)(2,1)S(1)}, u32[]{:S(2)}, u32[]{:S(2)}) %collective-permute-start.2) | collective-permute-done | bytes 950304 | tf_op jit(solution)/shard_map/ppermute | solution.py:136
  414.3 41.2 %collective-permute-done.14 = bf16[128,4096]{1,0:T(8,128)(2,1)S(1)} collective-permute-done((bf16[128,4096]{1,0:T(8,128)(2,1)S(1)}, bf16[128,4096]{1,0:T(8,128)(2,1)S(1)}, u32[]{:S(2)}, u32[]{:S(2)}) %collective-permute-start.14) | collective-permute-done | bytes 1048608 | tf_op jit(solution)/shard_map/ppermute | solution.py:136
  457.8 21.6 %collective-permute-done.3 = bf16[128,3712]{1,0:T(8,128)(2,1)S(1)} collective-permute-done((bf16[128,3712]{1,0:T(8,128)(2,1)S(1)}, bf16[128,3712]{1,0:T(8,128)(2,1)S(1)}, u32[]{:S(2)}, u32[]{:S(2)}) %collective-permute-start.3) | collective-permute-done | bytes 950304 | tf_op jit(solution)/shard_map/ppermute | solution.py:136
  482.9 27.8 %collective-permute-done.4 = bf16[64,3712]{1,0:T(8,128)(2,1)S(1)} collective-permute-done((bf16[64,3712]{1,0:T(8,128)(2,1)S(1)}, bf16[64,3712]{1,0:T(8,128)(2,1)S(1)}, u32[]{:S(2)}, u32[]{:S(2)}) %collective-permute-start.4) | collective-permute-done | bytes 475168 | tf_op jit(solution)/shard_map/ppermute | solution.py:136
  516.4 10.6 %collective-permute-done.5 = bf16[32,3712]{1,0:T(8,128)(2,1)S(1)} collective-permute-done((bf16[32,3712]{1,0:T(8,128)(2,1)S(1)}, bf16[32,3712]{1,0:T(8,128)(2,1)S(1)}, u32[]{:S(2)}, u32[]{:S(2)}) %collective-permute-start.5) | collective-permute-done | bytes 237600 | tf_op jit(solution)/shard_map/ppermute | solution.py:136
  534.2 5.6 %collective-permute-done.22 = bf16[64,4096]{1,0:T(8,128)(2,1)} collective-permute-done((bf16[64,4096]{1,0:T(8,128)(2,1)}, bf16[64,4096]{1,0:T(8,128)(2,1)}, u32[]{:S(2)}, u32[]{:S(2)}) %collective-permute-start.22) | collective-permute-done | bytes 524320 | tf_op jit(solution)/shard_map/ppermute | solution.py:136
  543.2 4.2 collective-permute-done.23
  (259 shorter events, 134.5 us)
Async XLA Ops:
  7.2 86.1 %all-gather.3.cloned.1.call-start = ((), (), s32[]{:S(2)}) async-start(), calls=%async_computation | async-start | bytes 7839744 | tf_op jit(solution)/shard_map/all_gather | solution.py:190
  15.9 204.1 %all-gather.5.cloned.1.call-start = ((), (), s32[]{:S(2)}) async-start(), calls=%async_computation.1 | async-start | bytes 19464192 | tf_op jit(solution)/shard_map/all_gather | solution.py:191
  334.8 48.7 %collective-permute-start = (bf16[512,3712]{1,0:T(8,128)(2,1)}, bf16[512,3712]{1,0:T(8,128)(2,1)}, u32[]{:S(2)}, u32[]{:S(2)}) collective-permute-start(bf16[512,3712]{1,0:T(8,128)(2,1)} %fusion.81), channel_id=1, source_target_pairs={{0,4},{4,0},{8,12},{12,8},{16,20},{20,16},{24,28},{28,24},{1,5},{5... | collective-permute-start | bytes 11403272 | tf_op jit(solution)/shard_map/ppermute | solution.py:136
  337.2 16.9 %collective-permute-start.6 = (bf16[512,1024]{1,0:T(8,128)(2,1)S(1)}, bf16[512,1024]{1,0:T(8,128)(2,1)S(1)}, u32[]{:S(2)}, u32[]{:S(2)}) collective-permute-start(bf16[512,1024]{1,0:T(8,128)(2,1)S(1)} %convolution_convert_fusion.12), channel_id=1, source_target_pairs={{0,4},{4,0},{8,12},{12,8},{16,20},{20,16},{24,28},{28,24},{1,5},{5... | collective-permute-start | bytes 3145736 | tf_op jit(solution)/shard_map/ppermute | solution.py:136
  341.9 48.7 %collective-permute-start.12 = (bf16[512,4096]{1,0:T(8,128)(2,1)}, bf16[512,4096]{1,0:T(8,128)(2,1)}, u32[]{:S(2)}, u32[]{:S(2)}) collective-permute-start(bf16[512,4096]{1,0:T(8,128)(2,1)} %convolution_convert_fusion.1), channel_id=1, source_target_pairs={{0,4},{4,0},{8,12},{12,8},{16,20},{20,16},{24,28},{28,24},{1,5},{5... | collective-permute-start | bytes 12582920 | tf_op jit(solution)/shard_map/ppermute | solution.py:136
  346.9 51.0 %collective-permute-start.18 = (bf16[512,4096]{1,0:T(8,128)(2,1)}, bf16[512,4096]{1,0:T(8,128)(2,1)}, u32[]{:S(2)}, u32[]{:S(2)}) collective-permute-start(bf16[512,4096]{1,0:T(8,128)(2,1)} %convolution_convert_fusion), channel_id=1, source_target_pairs={{0,4},{4,0},{8,12},{12,8},{16,20},{20,16},{24,28},{28,24},{1,5},{5... | collective-permute-start | bytes 12582920 | tf_op jit(solution)/shard_map/ppermute | solution.py:136
  354.9 9.2 %collective-permute-start.8 = (bf16[128,1024]{1,0:T(8,128)(2,1)S(1)}, bf16[128,1024]{1,0:T(8,128)(2,1)S(1)}, u32[]{:S(2)}, u32[]{:S(2)}) collective-permute-start(bf16[128,1024]{1,0:T(8,128)(2,1)S(1)} %get-tuple-element.70), channel_id=1, source_target_pairs={{0,2},{1,3},{2,0},{3,1},{4,6},{5,7},{6,4},{7,5},{8,10},{9,11},{10,... | collective-permute-start | bytes 786440 | tf_op jit(solution)/shard_map/ppermute | solution.py:136
  359.1 10.0 %collective-permute-start.7 = (bf16[128,1024]{1,0:T(8,128)(2,1)S(1)}, bf16[128,1024]{1,0:T(8,128)(2,1)S(1)}, u32[]{:S(2)}, u32[]{:S(2)}) collective-permute-start(bf16[128,1024]{1,0:T(8,128)(2,1)S(1)} %get-tuple-element.69), channel_id=1, source_target_pairs={{0,2},{1,3},{2,0},{3,1},{4,6},{5,7},{6,4},{7,5},{8,10},{9,11},{10,... | collective-permute-start | bytes 786440 | tf_op jit(solution)/shard_map/ppermute | solution.py:136
  364.2 7.1 %collective-permute-start.9 = (bf16[128,1024]{1,0:T(8,128)(2,1)S(1)}, bf16[128,1024]{1,0:T(8,128)(2,1)S(1)}, u32[]{:S(2)}, u32[]{:S(2)}) collective-permute-start(bf16[128,1024]{1,0:T(8,128)(2,1)S(1)} %add_convert_fusion.25), channel_id=1, source_target_pairs={{0,1},{1,0},{2,3},{3,2},{4,5},{5,4},{6,7},{7,6},{8,9},{9,8},{10,11... | collective-permute-start | bytes 786440 | tf_op jit(solution)/shard_map/ppermute | solution.py:136
  371.4 7.0 %collective-permute-start.10 = (bf16[64,1024]{1,0:T(8,128)(2,1)S(1)}, bf16[64,1024]{1,0:T(8,128)(2,1)S(1)}, u32[]{:S(2)}, u32[]{:S(2)}) collective-permute-start(bf16[64,1024]{1,0:T(8,128)(2,1)S(1)} %slice.368), channel_id=1, source_target_pairs={{0,16},{4,20},{8,24},{12,28},{16,0},{20,4},{24,8},{28,12},{1,17},{... | collective-permute-start | bytes 393224 | tf_op jit(solution)/shard_map/ppermute | solution.py:136
  388.6 24.1 %collective-permute-start.2 = (bf16[128,3712]{1,0:T(8,128)(2,1)S(1)}, bf16[128,3712]{1,0:T(8,128)(2,1)S(1)}, u32[]{:S(2)}, u32[]{:S(2)}) collective-permute-start(bf16[128,3712]{1,0:T(8,128)(2,1)S(1)} %get-tuple-element.67), channel_id=1, source_target_pairs={{0,1},{1,0},{2,3},{3,2},{4,5},{5,4},{6,7},{7,6},{8,9},{9,8},{10,11... | collective-permute-start | bytes 2850824 | tf_op jit(solution)/shard_map/ppermute | solution.py:136
  390.1 67.1 %collective-permute-start.1 = (bf16[128,3712]{1,0:T(8,128)(2,1)S(1)}, bf16[128,3712]{1,0:T(8,128)(2,1)S(1)}, u32[]{:S(2)}, u32[]{:S(2)}) collective-permute-start(bf16[128,3712]{1,0:T(8,128)(2,1)S(1)} %get-tuple-element.66), channel_id=1, source_target_pairs={{0,1},{1,0},{2,3},{3,2},{4,5},{5,4},{6,7},{7,6},{8,9},{9,8},{10,11... | collective-permute-start | bytes 2850824 | tf_op jit(solution)/shard_map/ppermute | solution.py:136
  395.8 59.6 %collective-permute-start.14 = (bf16[128,4096]{1,0:T(8,128)(2,1)S(1)}, bf16[128,4096]{1,0:T(8,128)(2,1)S(1)}, u32[]{:S(2)}, u32[]{:S(2)}) collective-permute-start(bf16[128,4096]{1,0:T(8,128)(2,1)S(1)} %get-tuple-element.65), channel_id=1, source_target_pairs={{0,1},{1,0},{2,3},{3,2},{4,5},{5,4},{6,7},{7,6},{8,9},{9,8},{10,11... | collective-permute-start | bytes 3145736 | tf_op jit(solution)/shard_map/ppermute | solution.py:136
  397.3 113.6 %collective-permute-start.13 = (bf16[128,4096]{1,0:T(8,128)(2,1)S(1)}, bf16[128,4096]{1,0:T(8,128)(2,1)S(1)}, u32[]{:S(2)}, u32[]{:S(2)}) collective-permute-start(bf16[128,4096]{1,0:T(8,128)(2,1)S(1)} %get-tuple-element.64), channel_id=1, source_target_pairs={{0,1},{1,0},{2,3},{3,2},{4,5},{5,4},{6,7},{7,6},{8,9},{9,8},{10,11... | collective-permute-start | bytes 3145736 | tf_op jit(solution)/shard_map/ppermute | solution.py:136
  402.8 78.4 %collective-permute-start.20 = (bf16[128,4096]{1,0:T(8,128)(2,1)S(1)}, bf16[128,4096]{1,0:T(8,128)(2,1)S(1)}, u32[]{:S(2)}, u32[]{:S(2)}) collective-permute-start(bf16[128,4096]{1,0:T(8,128)(2,1)S(1)} %get-tuple-element.63), channel_id=1, source_target_pairs={{0,2},{1,3},{2,0},{3,1},{4,6},{5,7},{6,4},{7,5},{8,10},{9,11},{10,... | collective-permute-start | bytes 3145736 | tf_op jit(solution)/shard_map/ppermute | solution.py:136
  412.6 101.5 %collective-permute-start.19 = (bf16[128,4096]{1,0:T(8,128)(2,1)S(1)}, bf16[128,4096]{1,0:T(8,128)(2,1)S(1)}, u32[]{:S(2)}, u32[]{:S(2)}) collective-permute-start(bf16[128,4096]{1,0:T(8,128)(2,1)S(1)} %get-tuple-element.62), channel_id=1, source_target_pairs={{0,2},{1,3},{2,0},{3,1},{4,6},{5,7},{6,4},{7,5},{8,10},{9,11},{10,... | collective-permute-start | bytes 3145736 | tf_op jit(solution)/shard_map/ppermute | solution.py:136
  455.5 24.0 %collective-permute-start.3 = (bf16[128,3712]{1,0:T(8,128)(2,1)S(1)}, bf16[128,3712]{1,0:T(8,128)(2,1)S(1)}, u32[]{:S(2)}, u32[]{:S(2)}) collective-permute-start(bf16[128,3712]{1,0:T(8,128)(2,1)S(1)} %add_convert_fusion.19), channel_id=1, source_target_pairs={{0,2},{1,3},{2,0},{3,1},{4,6},{5,7},{6,4},{7,5},{8,10},{9,11},{10,... | collective-permute-start | bytes 2850824 | tf_op jit(solution)/shard_map/ppermute | solution.py:136
  457.2 53.7 %collective-permute-start.15 = (bf16[128,4096]{1,0:T(8,128)(2,1)S(1)}, bf16[128,4096]{1,0:T(8,128)(2,1)S(1)}, u32[]{:S(2)}, u32[]{:S(2)}) collective-permute-start(bf16[128,4096]{1,0:T(8,128)(2,1)S(1)} %add_convert_fusion.7), channel_id=1, source_target_pairs={{0,2},{1,3},{2,0},{3,1},{4,6},{5,7},{6,4},{7,5},{8,10},{9,11},{10,... | collective-permute-start | bytes 3145736 | tf_op jit(solution)/shard_map/ppermute | solution.py:136
  479.8 30.8 %collective-permute-start.4 = (bf16[64,3712]{1,0:T(8,128)(2,1)S(1)}, bf16[64,3712]{1,0:T(8,128)(2,1)S(1)}, u32[]{:S(2)}, u32[]{:S(2)}) collective-permute-start(bf16[64,3712]{1,0:T(8,128)(2,1)S(1)} %slice.352), channel_id=1, source_target_pairs={{0,16},{4,20},{8,24},{12,28},{16,0},{20,4},{24,8},{28,12},{1,17},{... | collective-permute-start | bytes 1425416 | tf_op jit(solution)/shard_map/ppermute | solution.py:136
  481.4 32.7 %collective-permute-start.21 = (bf16[128,4096]{1,0:T(8,128)(2,1)S(1)}, bf16[128,4096]{1,0:T(8,128)(2,1)S(1)}, u32[]{:S(2)}, u32[]{:S(2)}) collective-permute-start(bf16[128,4096]{1,0:T(8,128)(2,1)S(1)} %add_convert_fusion.4), channel_id=1, source_target_pairs={{0,1},{1,0},{2,3},{3,2},{4,5},{5,4},{6,7},{7,6},{8,9},{9,8},{10,11... | collective-permute-start | bytes 3145736 | tf_op jit(solution)/shard_map/ppermute | solution.py:136
  510.8 16.3 %collective-permute-start.5 = (bf16[32,3712]{1,0:T(8,128)(2,1)S(1)}, bf16[32,3712]{1,0:T(8,128)(2,1)S(1)}, u32[]{:S(2)}, u32[]{:S(2)}) collective-permute-start(bf16[32,3712]{1,0:T(8,128)(2,1)S(1)} %slice.354), channel_id=1, source_target_pairs={{0,8},{4,12},{8,0},{12,4},{16,24},{20,28},{24,16},{28,20},{1,9},{5... | collective-permute-start | bytes 712712 | tf_op jit(solution)/shard_map/ppermute | solution.py:136
  512.2 21.7 %collective-permute-start.16 = (bf16[64,4096]{1,0:T(8,128)(2,1)}, bf16[64,4096]{1,0:T(8,128)(2,1)S(1)}, u32[]{:S(2)}, u32[]{:S(2)}) collective-permute-start(bf16[64,4096]{1,0:T(8,128)(2,1)} %slice.381), channel_id=1, source_target_pairs={{0,16},{4,20},{8,24},{12,28},{16,0},{20,4},{24,8},{28,12},{1,17},{... | collective-permute-start | bytes 1572872 | tf_op jit(solution)/shard_map/ppermute | solution.py:136
  515.4 24.3 %collective-permute-start.22 = (bf16[64,4096]{1,0:T(8,128)(2,1)}, bf16[64,4096]{1,0:T(8,128)(2,1)}, u32[]{:S(2)}, u32[]{:S(2)}) collective-permute-start(bf16[64,4096]{1,0:T(8,128)(2,1)} %slice.392), channel_id=1, source_target_pairs={{0,16},{4,20},{8,24},{12,28},{16,0},{20,4},{24,8},{28,12},{1,17},{... | collective-permute-start | bytes 1572872 | tf_op jit(solution)/shard_map/ppermute | solution.py:136
  534.1 8.3 %collective-permute-start.17 = (bf16[32,4096]{1,0:T(8,128)(2,1)S(1)}, bf16[32,4096]{1,0:T(8,128)(2,1)S(1)}, u32[]{:S(2)}, u32[]{:S(2)}) collective-permute-start(bf16[32,4096]{1,0:T(8,128)(2,1)S(1)} %slice.383), channel_id=1, source_target_pairs={{0,8},{4,12},{8,0},{12,4},{16,24},{20,28},{24,16},{28,20},{1,9},{5... | collective-permute-start | bytes 786440 | tf_op jit(solution)/shard_map/ppermute | solution.py:136
  (46 other events, 441.7 us)
Sparse Core Ops, SparseCore 0:
  16.0 77.1 all-gather.2
  96.8 123.2 all-gather.4

commit v2 on v1

--- a/solution.py
+++ b/solution.py
@@ -6,6 +6,7 @@
 HEADS=16
 BF=jnp.bfloat16
 F32=jnp.float32
+COST=pl.CostEstimate(flops=10**9,bytes_accessed=10**6,transcendentals=0)
 
 def mm(a,b,ca,cb):
     return lax.dot_general(a,b,(((ca,),(cb,)),((),())),preferred_element_type=F32)
@@ -42,6 +43,7 @@
         in_specs=[col]*5+[pl.BlockSpec((t,1),lambda i:(0,0)),pl.BlockSpec((1,t),lambda i:(0,0))],
         out_specs=[col,pl.BlockSpec((2,t,t),lambda i:(i,0,0))],
         out_shape=[jax.ShapeDtypeStruct((t,d),BF),jax.ShapeDtypeStruct((HEADS,t,t),BF)],
+        cost_estimate=COST,
         compiler_params=pltpu.CompilerParams(vmem_limit_bytes=48*2**20),
     )(q,k,v,ek,eq,seg.reshape(t,1),seg.reshape(1,t))
 
@@ -81,18 +83,21 @@
     dek_ref[...]=(dek*scale).astype(BF)
     deq_ref[...]=(deq*scale).astype(BF)
 
-def attend_back(q,k,v,ek,eq,dc,p,scale):
+def attend_back(q,k,v,ek,eq,dc,p,scale,grads,at,count):
     t,d=q.shape
     w=2*d//HEADS
-    col=pl.BlockSpec((t,w),lambda i:(0,i))
+    col=pl.BlockSpec((t,w),lambda i:(0,i+at))
+    grads=[] if grads is None else list(grads)
     return pl.pallas_call(
-        lambda *r: attend_back_kernel(scale,*r),
-        grid=(HEADS//2,),
-        in_specs=[col]*6+[pl.BlockSpec((2,t,t),lambda i:(i,0,0))],
+        lambda *r: attend_back_kernel(scale,*r[:7],*r[len(r)-5:]),
+        grid=(count,),
+        in_specs=[col]*6+[pl.BlockSpec((2,t,t),lambda i:(i+at,0,0))]+[pl.BlockSpec(memory_space=pl.ANY)]*len(grads),
         out_specs=[col]*5,
         out_shape=[jax.ShapeDtypeStruct((t,d),BF)]*5,
+        input_output_aliases={7+i:i for i in range(len(grads))},
+        cost_estimate=COST,
         compiler_params=pltpu.CompilerParams(vmem_limit_bytes=48*2**20),
-    )(q,k,v,ek,eq,dc,p)
+    )(q,k,v,ek,eq,dc,p,*grads)
 
 
 NORM_EPS = 1e-7
@@ -135,27 +140,8 @@
         size = self.nf if axis == "fsdp" else self.ndp
         return lax.ppermute(a, axis, [(i, i ^ bit) for i in range(size)])
 
-    def finish(self, mine, flipped):
-        step = self.nz * self.rows
-        parts = [mine[i * step : (i + 1) * step] for i in range(self.nf)]
-        bits = [1 << b for b in range(self.nf.bit_length() - 1)]
-        for bit in bits[::-1] if flipped else bits:
-            live = [i for i in range(len(parts)) if parts[i] is not None]
-            for i in live:
-                if i & bit:
-                    got = self.swap(parts[i], "fsdp", bit)
-                    parts[i ^ bit] = (parts[i ^ bit].astype(F32) + got.astype(F32)).astype(BF)
-                    parts[i] = None
-        total = parts[0]
-        bit = self.nz // 2
-        while bit:
-            h = total.shape[0] // 2
-            got = self.swap(total[h:], "dp", 2 * bit)
-            total = total[:h].astype(F32) + got.astype(F32)
-            bit //= 2
-            if bit:
-                total = total.astype(BF)
-        return total
+    def job(self, mine, flipped):
+        return Job(self, mine, flipped)
 
     def core_sum(self, pairs):
         h = self.width // 2
@@ -164,6 +150,58 @@
         got = self.swap(away, "dp", 1)
         mine = cat([mm(a[:, :h], b, 0, cb) for a, b, cb in pairs])
         return (mine + got.astype(F32)).astype(BF)
+
+
+class Job:
+    def __init__(self, tree, mine, flipped):
+        self.tree = tree
+        step = tree.nz * tree.rows
+        self.parts = {i: mine[i * step : (i + 1) * step] for i in range(tree.nf)}
+        bits = [1 << b for b in range(tree.nf.bit_length() - 1)]
+        self.stages = [("fsdp", b) for b in (bits[::-1] if flipped else bits)]
+        bit = 1
+        while bit < tree.nz:
+            self.stages.append(("dp", 2 * bit))
+            bit *= 2
+
+    def open(self):
+        axis, bit = self.stages[0]
+        if axis == "dp" and set(self.parts) == {0}:
+            total = self.parts.pop(0)
+            self.parts = {2 * i: total[i * self.tree.rows : (i + 1) * self.tree.rows] for i in range(self.tree.nz)}
+            if self.tree.nz == 1:
+                self.parts = {0: total}
+        return [i for i in self.parts if i & bit]
+
+    def send(self):
+        axis, bit = self.stages[0]
+        away = self.open()
+        if axis == "dp":
+            block = jnp.concatenate([self.parts[i] for i in away], 0) if len(away) > 1 else self.parts[away[0]]
+            return [self.tree.swap(block, axis, bit)]
+        return [self.tree.swap(self.parts[i], axis, bit) for i in away]
+
+    def add(self, got):
+        axis, bit = self.stages.pop(0)
+        away = [i for i in self.parts if i & bit]
+        if axis == "dp":
+            got = [got[0][i * self.tree.rows : (i + 1) * self.tree.rows] for i in range(len(away))]
+        last = not self.stages
+        for i, g in zip(away, got):
+            total = self.parts[i ^ bit].astype(F32) + g.astype(F32)
+            self.parts[i ^ bit] = total if last else total.astype(BF)
+            del self.parts[i]
+
+    def hold(self, *others):
+        keys = list(self.parts)
+        out = lax.optimization_barrier((tuple(self.parts[i] for i in keys), others))
+        self.parts = dict(zip(keys, out[0]))
+        return out[1]
+
+    def run(self):
+        while self.stages:
+            self.add(self.send())
+        return self.parts[0]
 
 
 def per_device(
@@ -231,11 +269,15 @@
     d_bo = jnp.sum(d_attn.astype(F32), 0)
     d_context = mm(d_attn, wo_t, 1, 0).astype(BF)
     out_mine = tree.core_sum([(arrange(d_attn), context, 0)])
-    down_grad = tree.finish(down_mine, True)
-    up_grad = tree.finish(up_mine, False)
-    out_grad = tree.finish(out_mine, True)
-
-    dq, dk, dv, dek, deq = attend_back(q, k, v, ek, eq, d_context, probs, scale)
+    down, up_job, out_job = tree.job(down_mine, True), tree.job(up_mine, False), tree.job(out_mine, True)
+    (d_context,) = down.hold(d_context)
+    (d_context,) = up_job.hold(d_context)
+    grads = attend_back(q, k, v, ek, eq, d_context, probs, scale, None, 0, 8)
+    got_d, got_u = down.send(), up_job.send()
+    grads, got_d, got_u = lax.optimization_barrier((grads, got_d, got_u))
+    down.add(got_d)
+    up_job.add(got_u)
+    dq, dk, dv, dek, deq = grads
     d_pos_keys = mm(onehot, dek, 0, 0).astype(BF)
     d_pos_queries = mm(onehot, deq, 0, 0).astype(BF)
     colsum = lambda m: jnp.sum(m.astype(F32), 0)
@@ -256,7 +298,8 @@
         (place, d_table, 1),
         (place, lines, 1),
     ])
-    rest = tree.finish(rest_mine, False)
+    down_grad, up_grad, out_grad = down.run(), up_job.run(), out_job.run()
+    rest = tree.job(rest_mine, False).run()
     input_grad = (d_first + mm(dq, wq, 1, 1) + mm(dk, wk, 1, 1) + mm(dv, wv, 1, 1)).astype(BF)
     tail = rest[:, 3 * d + buckets :]
     vecs = [tail[:, i] for i in range(SPLIT)]

time: 559 us -> 518 us (0.927); the launches traced: 555 us -> 509 us
  waiting for transfers between devices: 281 us -> 220 us
    ppermute x24, waiting for transfers between devices: 142 us -> 72.4 us  [swap(): return lax.ppermute(a, axis, [(i, i ^ bit) for i in range(size)])]
    convert_element_type x12, other arithmetic: 3.63 us -> 10.9 us  [add(): self.parts[i ^ bit] = total if last else total.astype(BF)]
  transfers between devices with their start and end apart: 26 -> 26, of which waited for: 16 -> 14; matrix products, arithmetic and copies ran while one was open for 14% -> 21% of each run, Pallas kernels for 6% -> 13%
where the time goes in v2:
time: 518 us; the launch traced here: 509 us
  waiting for transfers between devices  220 us (42%)
  matrix products  130 us (25%)
  Pallas kernels  66.5 us (13%)
  other arithmetic  37.8 us (7%)
  starting transfers between devices  22 us (4%)
  local copies, waits for them, and re-layouts  17.1 us (3%)
  between operations  15.2 us (3%)
    dot_general x40, matrix products, mm(): lax.dot_general(a, b, (((ca,), (cb,)), ((), ())), preferred_element_type=...  130 us
    all_gather x1, waiting for transfers between devices, per_device(): w2 = lax.all_gather(second, ('dp', 'fsdp'), axis=0, tiled=True)  79.1 us
    ppermute x24, waiting for transfers between devices, swap(): return lax.ppermute(a, axis, [(i, i ^ bit) for i in range(size)])  72.4 us
    all_gather x1, waiting for transfers between devices, per_device(): w1 = lax.all_gather(first, ('dp', 'fsdp'), axis=0, tiled=True)  68.9 us
    pallas_call x1, Pallas kernels, attend(): pl.pallas_call(lambda *r: attend_kernel(scale, *r), grid=(HEADS // 2,), i...  33.4 us
    pallas_call x1, Pallas kernels, attend_back(): pl.pallas_call(lambda *r: attend_back_kernel(scale, *r[:7], *r[len(r) - 5...  33.1 us
    ppermute x24, starting transfers between devices, swap(): return lax.ppermute(a, axis, [(i, i ^ bit) for i in range(size)])  21.9 us
    convert_element_type x12, other arithmetic, add(): self.parts[i ^ bit] = total if last else total.astype(BF)  10.9 us
  transfers between devices with their start and end apart: 26, of which 14 were waited for; matrix products, arithmetic and copies ran while one was open for 21% of the time, Pallas kernels for 13%

profile of v2, /device:TPU:0, one launch (start us, length us, event | category | flops | bytes accessed | tf_op | source)
XLA Modules:
  0.0 508.6 jit_solution(8690325752706223006)
XLA Ops:
  20.2 4.1 fusion.21
  24.3 68.9 %all-gather.3.cloned.1.call-done = bf16[1024,3712]{1,0:T(8,128)(2,1)} async-done(((bf16[32,3712]{1,0:T(8,128)(2,1)}), bf16[1024,3712]{1,0:T(8,128)(2,1)}) %all-gather.3.cloned.1.call-update) | async-done | bytes 7602192 | tf_op jit(solution)/shard_map/all_gather | solution.py:228
  106.5 33.4 %shard_map.348 = (bf16[512,1024]{1,0:T(8,128)(2,1)S(1)}, bf16[16,512,512]{2,1,0:T(8,128)(2,1)}) custom-call(bf16[512,1024]{1,0:T(8,128)(2,1)S(1)} %fusion.62.r_0_, bf16[512,1024]{1,0:T(8,128)(2,1)S(1)} %fusion.63.r_1_, bf16[512,1024]{1,0:T(8,128)(2,1)S(1)} %fusion.64.r_2_, bf16[512,1024]{1,0:T(8,128)(2,1)S(1)} %add_convert_fusion.14.r_3_, ...), custom_call_target="tpu_custom_call" | custom-call | flops 1000000000 | bytes 1000000 | tf_op jit(solution)/shard_map/pallas_call | solution.py:40
  140.8 79.1 %all-gather.5.cloned.1.call-done = bf16[1024,9216]{1,0:T(8,128)(2,1)} async-done(((bf16[32,9216]{1,0:T(8,128)(2,1)}), bf16[1024,9216]{1,0:T(8,128)(2,1)}) %all-gather.5.cloned.1.call-update) | async-done | bytes 18874384 | tf_op jit(solution)/shard_map/all_gather | solution.py:229
  219.9 3.3 fusion.152
  223.6 9.8 %multiply_convert_fusion = (bf16[512,4096]{1,0:T(8,128)(2,1)S(1)}, f32[512,4096]{1,0:T(8,128)}) fusion(f32[4096]{0:T(1024)S(1)} %add.311, bf16[1024,9216]{1,0:T(8,128)(2,1)} %all-gather.5.cloned.1.call-done, f32[512,1024]{1,0:T(8,128)S(1)} %get-tuple-element.125, f32[1024]{0:T(1024)S(1)} %get-tuple-element.81, f32[1024]{0:T(1024)S(1)} %get-tuple-element.82, ...), kind=kOutput, calls=%fused_computation.9 | convolution fusion | flops 4310171648 | bytes 23097344 | tf_op jit(solution)/shard_map/dot_general | solution.py:12
  233.3 9.2 %fusion.153 = (f32[512]{0:T(512)S(1)}, f32[512,1024]{1,0:T(8,128)S(1)}) fusion(f32[1024]{0:T(1024)S(1)} %get-tuple-element.80, bf16[512,4096]{1,0:T(8,128)(2,1)S(1)} %get-tuple-element.126, bf16[1024,9216]{1,0:T(8,128)(2,1)} %all-gather.5.cloned.1.call-done, f32[1024]{0:T(1024)S(1)} %get-tuple-element.81, f32[1024]{0:T(1024)S(1)} %get-tuple-element.82, ...), kind=kOutput, calls=%fused_computation.274 | convolution fusion | flops 4298636800 | bytes 16795648 | tf_op jit(solution)/shard_map/dot_general | solution.py:12
  247.9 10.6 %fusion.154 = (bf16[4096]{0:T(1024)(128)(2,1)S(1)}, bf16[512,4096]{1,0:T(8,128)(2,1)S(1)}) fusion(f32[512,4096]{1,0:T(8,128)} %get-tuple-element.127, f32[4096]{0:T(1024)S(1)} %add.311, bf16[1024,9216]{1,0:T(8,128)(2,1)} %all-gather.5.cloned.1.call-done, f32[512,1024]{1,0:T(8,128)S(1)} %get-tuple-element.97), kind=kOutput, calls=%fused_computation.275 | convolution fusion | flops 4320653312 | bytes 23093248 | tf_op jit(solution)/shard_map/dot_general | solution.py:12
  258.6 9.4 %multiply_reduce_fusion = (bf16[1024]{0:T(1024)(128)(2,1)S(1)}, f32[512]{0:T(512)S(1)}, f32[512]{0:T(512)S(1)}, bf16[1024]{0:T(1024)(128)(2,1)S(1)}, f32[512,1024]{1,0:T(8,128)S(1)}) fusion(f32[512,1024]{1,0:T(8,128)S(1)} %get-tuple-element.125, f32[512]{0:T(512)S(1)} %add_rsqrt_fusion.1, f32[512]{0:T(512)S(1)} %broadcast_multiply_fusion.5, ...), kind=kOutput, calls=%fused_computation.69 | convolution fusion | flops 4300207104 | bytes 18890752 | tf_op jit(solution)/shard_map/dot_general | solution.py:12
  268.0 4.5 convolution_convert_fusion
  283.6 4.4 convolution_convert_fusion.1
  292.4 3.7 fusion.61
  299.7 4.6 fusion.51.r_5_
  306.4 4.6 add_convert_fusion
  315.0 4.6 add_convert_fusion.1
  325.8 4.6 convolution_convert_fusion.7
  331.4 33.1 %shard_map.349 = (bf16[512,1024]{1,0:T(8,128)(2,1)S(1)}, bf16[512,1024]{1,0:T(8,128)(2,1)S(1)}, bf16[512,1024]{1,0:T(8,128)(2,1)S(1)}, bf16[512,1024]{1,0:T(8,128)(2,1)S(1)}, bf16[512,1024]{1,0:T(8,128)(2,1)S(1)}) custom-call(bf16[512,1024]{1,0:T(8,128)(2,1)} %copy-done.1, bf16[512,1024]{1,0:T(8,128)(2,1)} %copy-done.2, bf16[512,1024]{1,0:T(8,128)(2,1)} %copy-done.3, ...), custom_call_target="tpu_custom_call" | custom-call | flops 1000000000 | bytes 1000000 | tf_op jit(solution)/shard_map/pallas_call | solution.py:91
  384.0 4.0 fusion.54
  400.9 4.3 convolution_dynamic-update-slice_fusion.1
  407.4 3.1 fusion.74
  428.4 21.1 %collective-permute-done.8 = bf16[128,3712]{1,0:T(8,128)(2,1)S(1)} collective-permute-done((bf16[128,3712]{1,0:T(8,128)(2,1)S(1)}, bf16[128,3712]{1,0:T(8,128)(2,1)S(1)}, u32[]{:S(2)}, u32[]{:S(2)}) %collective-permute-start.8) | collective-permute-done | bytes 950304 | tf_op jit(solution)/shard_map/ppermute | solution.py:141
  454.1 15.0 %collective-permute-done.7 = bf16[128,3712]{1,0:T(8,128)(2,1)S(1)} collective-permute-done((bf16[128,3712]{1,0:T(8,128)(2,1)S(1)}, bf16[128,3712]{1,0:T(8,128)(2,1)S(1)}, u32[]{:S(2)}, u32[]{:S(2)}) %collective-permute-start.7) | collective-permute-done | bytes 950304 | tf_op jit(solution)/shard_map/ppermute | solution.py:141
  473.5 12.1 %collective-permute-done.10 = bf16[64,3712]{1,0:T(8,128)(2,1)S(1)} collective-permute-done((bf16[64,3712]{1,0:T(8,128)(2,1)S(1)}, bf16[64,3712]{1,0:T(8,128)(2,1)S(1)}, u32[]{:S(2)}, u32[]{:S(2)}) %collective-permute-start.10) | collective-permute-done | bytes 475168 | tf_op jit(solution)/shard_map/ppermute | solution.py:141
  486.7 11.8 %collective-permute-done.11 = bf16[32,3712]{1,0:T(8,128)(2,1)S(1)} collective-permute-done((bf16[32,3712]{1,0:T(8,128)(2,1)S(1)}, bf16[32,3712]{1,0:T(8,128)(2,1)S(1)}, u32[]{:S(2)}, u32[]{:S(2)}) %collective-permute-start.11) | collective-permute-done | bytes 237600 | tf_op jit(solution)/shard_map/ppermute | solution.py:141
  (253 shorter events, 130.0 us)
Async XLA Ops:
  7.2 86.0 %all-gather.3.cloned.1.call-start = ((), (), s32[]{:S(2)}) async-start(), calls=%async_computation | async-start | bytes 7839744 | tf_op jit(solution)/shard_map/all_gather | solution.py:228
  15.8 204.1 %all-gather.5.cloned.1.call-start = ((), (), s32[]{:S(2)}) async-start(), calls=%async_computation.1 | async-start | bytes 19464192 | tf_op jit(solution)/shard_map/all_gather | solution.py:229
  272.5 33.9 %collective-permute-start.1 = (bf16[512,4096]{1,0:T(8,128)(2,1)}, bf16[512,4096]{1,0:T(8,128)(2,1)}, u32[]{:S(2)}, u32[]{:S(2)}) collective-permute-start(bf16[512,4096]{1,0:T(8,128)(2,1)} %convolution_convert_fusion), channel_id=1, source_target_pairs={{0,4},{4,0},{8,12},{12,8},{16,20},{20,16},{24,28},{28,24},{1,5},{5... | collective-permute-start | bytes 12582920 | tf_op jit(solution)/shard_map/ppermute | solution.py:141
  282.0 8.5 %collective-permute-start.14 = (bf16[128,1024]{1,0:T(8,128)(2,1)S(1)}, bf16[128,1024]{1,0:T(8,128)(2,1)S(1)}, u32[]{:S(2)}, u32[]{:S(2)}) collective-permute-start(bf16[128,1024]{1,0:T(8,128)(2,1)S(1)} %get-tuple-element.116), channel_id=1, source_target_pairs={{0,2},{1,3},{2,0},{3,1},{4,6},{5,7},{6,4},{7,5},{8,10},{9,11},{10,... | collective-permute-start | bytes 786440 | tf_op jit(solution)/shard_map/ppermute | solution.py:141
  288.0 25.3 %collective-permute-start = (bf16[512,4096]{1,0:T(8,128)(2,1)}, bf16[512,4096]{1,0:T(8,128)(2,1)}, u32[]{:S(2)}, u32[]{:S(2)}) collective-permute-start(bf16[512,4096]{1,0:T(8,128)(2,1)} %convolution_convert_fusion.1), channel_id=1, source_target_pairs={{0,4},{4,0},{8,12},{12,8},{16,20},{20,16},{24,28},{28,24},{1,5},{5... | collective-permute-start | bytes 12582920 | tf_op jit(solution)/shard_map/ppermute | solution.py:141
  288.0 8.7 %collective-permute-start.13 = (bf16[128,1024]{1,0:T(8,128)(2,1)S(1)}, bf16[128,1024]{1,0:T(8,128)(2,1)S(1)}, u32[]{:S(2)}, u32[]{:S(2)}) collective-permute-start(bf16[128,1024]{1,0:T(8,128)(2,1)S(1)} %get-tuple-element.115), channel_id=1, source_target_pairs={{0,2},{1,3},{2,0},{3,1},{4,6},{5,7},{6,4},{7,5},{8,10},{9,11},{10,... | collective-permute-start | bytes 786440 | tf_op jit(solution)/shard_map/ppermute | solution.py:141
  290.6 7.7 %collective-permute-start.15 = (bf16[128,1024]{1,0:T(8,128)(2,1)S(1)}, bf16[128,1024]{1,0:T(8,128)(2,1)S(1)}, u32[]{:S(2)}, u32[]{:S(2)}) collective-permute-start(bf16[128,1024]{1,0:T(8,128)(2,1)S(1)} %add_convert_fusion.26), channel_id=1, source_target_pairs={{0,1},{1,0},{2,3},{3,2},{4,5},{5,4},{6,7},{7,6},{8,9},{9,8},{10,11... | collective-permute-start | bytes 786440 | tf_op jit(solution)/shard_map/ppermute | solution.py:141
  304.6 26.1 %collective-permute-start.17 = (bf16[32,1024]{1,0:T(8,128)(2,1)S(1)}, bf16[32,1024]{1,0:T(8,128)(2,1)S(1)}, u32[]{:S(2)}, u32[]{:S(2)}) collective-permute-start(bf16[32,1024]{1,0:T(8,128)(2,1)S(1)} %add_convert_fusion.30), channel_id=1, source_target_pairs={{0,16},{4,20},{8,24},{12,28},{16,0},{20,4},{24,8},{28,12},{1,17},{... | collective-permute-start | bytes 196616 | tf_op jit(solution)/shard_map/ppermute | solution.py:141
  321.7 42.7 %collective-permute-start.4 = (bf16[128,4096]{1,0:T(8,128)(2,1)}, bf16[128,4096]{1,0:T(8,128)(2,1)}, u32[]{:S(2)}, u32[]{:S(2)}) collective-permute-start(bf16[128,4096]{1,0:T(8,128)(2,1)} %get-tuple-element.56), channel_id=1, source_target_pairs={{0,1},{1,0},{2,3},{3,2},{4,5},{5,4},{6,7},{7,6},{8,9},{9,8},{10,11... | collective-permute-start | bytes 3145736 | tf_op jit(solution)/shard_map/ppermute | solution.py:141
  323.2 44.3 %collective-permute-start.5 = (bf16[128,4096]{1,0:T(8,128)(2,1)}, bf16[128,4096]{1,0:T(8,128)(2,1)}, u32[]{:S(2)}, u32[]{:S(2)}) collective-permute-start(bf16[128,4096]{1,0:T(8,128)(2,1)} %get-tuple-element.57), channel_id=1, source_target_pairs={{0,1},{1,0},{2,3},{3,2},{4,5},{5,4},{6,7},{7,6},{8,9},{9,8},{10,11... | collective-permute-start | bytes 3145736 | tf_op jit(solution)/shard_map/ppermute | solution.py:141
  323.8 43.7 %collective-permute-start.2 = (bf16[128,4096]{1,0:T(8,128)(2,1)}, bf16[128,4096]{1,0:T(8,128)(2,1)}, u32[]{:S(2)}, u32[]{:S(2)}) collective-permute-start(bf16[128,4096]{1,0:T(8,128)(2,1)} %get-tuple-element.54), channel_id=1, source_target_pairs={{0,2},{1,3},{2,0},{3,1},{4,6},{5,7},{6,4},{7,5},{8,10},{9,11},{10,... | collective-permute-start | bytes 3145736 | tf_op jit(solution)/shard_map/ppermute | solution.py:141
  325.3 43.6 %collective-permute-start.3 = (bf16[128,4096]{1,0:T(8,128)(2,1)}, bf16[128,4096]{1,0:T(8,128)(2,1)}, u32[]{:S(2)}, u32[]{:S(2)}) collective-permute-start(bf16[128,4096]{1,0:T(8,128)(2,1)} %get-tuple-element.55), channel_id=1, source_target_pairs={{0,2},{1,3},{2,0},{3,1},{4,6},{5,7},{6,4},{7,5},{8,10},{9,11},{10,... | collective-permute-start | bytes 3145736 | tf_op jit(solution)/shard_map/ppermute | solution.py:141
  377.3 39.5 %collective-permute-start.21 = (bf16[128,4096]{1,0:T(8,128)(2,1)}, bf16[128,4096]{1,0:T(8,128)(2,1)}, u32[]{:S(2)}, u32[]{:S(2)}) collective-permute-start(bf16[128,4096]{1,0:T(8,128)(2,1)} %add_convert_fusion.4), channel_id=1, source_target_pairs={{0,1},{1,0},{2,3},{3,2},{4,5},{5,4},{6,7},{7,6},{8,9},{9,8},{10,11... | collective-permute-start | bytes 3145736 | tf_op jit(solution)/shard_map/ppermute | solution.py:141
  380.9 39.5 %collective-permute-start.18 = (bf16[128,4096]{1,0:T(8,128)(2,1)}, bf16[128,4096]{1,0:T(8,128)(2,1)}, u32[]{:S(2)}, u32[]{:S(2)}) collective-permute-start(bf16[128,4096]{1,0:T(8,128)(2,1)} %add_convert_fusion.7), channel_id=1, source_target_pairs={{0,2},{1,3},{2,0},{3,1},{4,6},{5,7},{6,4},{7,5},{8,10},{9,11},{10,... | collective-permute-start | bytes 3145736 | tf_op jit(solution)/shard_map/ppermute | solution.py:141
  400.9 21.5 %collective-permute-start.6 = (bf16[512,3712]{1,0:T(8,128)(2,1)}, bf16[512,3712]{1,0:T(8,128)(2,1)}, u32[]{:S(2)}, u32[]{:S(2)}) collective-permute-start(bf16[512,3712]{1,0:T(8,128)(2,1)} %fusion.81), channel_id=1, source_target_pairs={{0,4},{4,0},{8,12},{12,8},{16,20},{20,16},{24,28},{28,24},{1,5},{5... | collective-permute-start | bytes 11403272 | tf_op jit(solution)/shard_map/ppermute | solution.py:141
  418.9 32.0 %collective-permute-start.22 = (bf16[64,4096]{1,0:T(8,128)(2,1)S(1)}, bf16[64,4096]{1,0:T(8,128)(2,1)S(1)}, u32[]{:S(2)}, u32[]{:S(2)}) collective-permute-start(bf16[64,4096]{1,0:T(8,128)(2,1)S(1)} %pad_maximum_fusion.9), channel_id=1, source_target_pairs={{0,8},{4,12},{8,0},{12,4},{16,24},{20,28},{24,16},{28,20},{1,9},{5... | collective-permute-start | bytes 1572872 | tf_op jit(solution)/shard_map/ppermute | solution.py:141
  425.5 23.9 %collective-permute-start.8 = (bf16[128,3712]{1,0:T(8,128)(2,1)S(1)}, bf16[128,3712]{1,0:T(8,128)(2,1)S(1)}, u32[]{:S(2)}, u32[]{:S(2)}) collective-permute-start(bf16[128,3712]{1,0:T(8,128)(2,1)S(1)} %get-tuple-element.109), channel_id=1, source_target_pairs={{0,1},{1,0},{2,3},{3,2},{4,5},{5,4},{6,7},{7,6},{8,9},{9,8},{10,11... | collective-permute-start | bytes 2850824 | tf_op jit(solution)/shard_map/ppermute | solution.py:141
  426.8 25.7 %collective-permute-start.19 = (bf16[64,4096]{1,0:T(8,128)(2,1)S(1)}, bf16[64,4096]{1,0:T(8,128)(2,1)S(1)}, u32[]{:S(2)}, u32[]{:S(2)}) collective-permute-start(bf16[64,4096]{1,0:T(8,128)(2,1)S(1)} %pad_maximum_fusion.8), channel_id=1, source_target_pairs={{0,8},{4,12},{8,0},{12,4},{16,24},{20,28},{24,16},{28,20},{1,9},{5... | collective-permute-start | bytes 1572872 | tf_op jit(solution)/shard_map/ppermute | solution.py:141
  427.5 41.6 %collective-permute-start.7 = (bf16[128,3712]{1,0:T(8,128)(2,1)S(1)}, bf16[128,3712]{1,0:T(8,128)(2,1)S(1)}, u32[]{:S(2)}, u32[]{:S(2)}) collective-permute-start(bf16[128,3712]{1,0:T(8,128)(2,1)S(1)} %get-tuple-element.108), channel_id=1, source_target_pairs={{0,1},{1,0},{2,3},{3,2},{4,5},{5,4},{6,7},{7,6},{8,9},{9,8},{10,11... | collective-permute-start | bytes 2850824 | tf_op jit(solution)/shard_map/ppermute | solution.py:141
  449.7 21.7 %collective-permute-start.9 = (bf16[128,3712]{1,0:T(8,128)(2,1)S(1)}, bf16[128,3712]{1,0:T(8,128)(2,1)S(1)}, u32[]{:S(2)}, u32[]{:S(2)}) collective-permute-start(bf16[128,3712]{1,0:T(8,128)(2,1)S(1)} %add_convert_fusion.19), channel_id=1, source_target_pairs={{0,2},{1,3},{2,0},{3,1},{4,6},{5,7},{6,4},{7,5},{8,10},{9,11},{10,... | collective-permute-start | bytes 2850824 | tf_op jit(solution)/shard_map/ppermute | solution.py:141
  451.0 21.6 %collective-permute-start.23 = (bf16[32,4096]{1,0:T(8,128)(2,1)S(1)}, bf16[32,4096]{1,0:T(8,128)(2,1)S(1)}, u32[]{:S(2)}, u32[]{:S(2)}) collective-permute-start(bf16[32,4096]{1,0:T(8,128)(2,1)S(1)} %add_convert_fusion.21), channel_id=1, source_target_pairs={{0,16},{4,20},{8,24},{12,28},{16,0},{20,4},{24,8},{28,12},{1,17},{... | collective-permute-start | bytes 786440 | tf_op jit(solution)/shard_map/ppermute | solution.py:141
  452.5 33.2 %collective-permute-start.20 = (bf16[32,4096]{1,0:T(8,128)(2,1)S(1)}, bf16[32,4096]{1,0:T(8,128)(2,1)S(1)}, u32[]{:S(2)}, u32[]{:S(2)}) collective-permute-start(bf16[32,4096]{1,0:T(8,128)(2,1)S(1)} %add_convert_fusion.23), channel_id=1, source_target_pairs={{0,16},{4,20},{8,24},{12,28},{16,0},{20,4},{24,8},{28,12},{1,17},{... | collective-permute-start | bytes 786440 | tf_op jit(solution)/shard_map/ppermute | solution.py:141
  471.9 13.7 %collective-permute-start.10 = (bf16[64,3712]{1,0:T(8,128)(2,1)S(1)}, bf16[64,3712]{1,0:T(8,128)(2,1)S(1)}, u32[]{:S(2)}, u32[]{:S(2)}) collective-permute-start(bf16[64,3712]{1,0:T(8,128)(2,1)S(1)} %pad_maximum_fusion.10), channel_id=1, source_target_pairs={{0,8},{4,12},{8,0},{12,4},{16,24},{20,28},{24,16},{28,20},{1,9},{5... | collective-permute-start | bytes 1425416 | tf_op jit(solution)/shard_map/ppermute | solution.py:141
  485.7 12.7 %collective-permute-start.11 = (bf16[32,3712]{1,0:T(8,128)(2,1)S(1)}, bf16[32,3712]{1,0:T(8,128)(2,1)S(1)}, u32[]{:S(2)}, u32[]{:S(2)}) collective-permute-start(bf16[32,3712]{1,0:T(8,128)(2,1)S(1)} %add_convert_fusion.28), channel_id=1, source_target_pairs={{0,16},{4,20},{8,24},{12,28},{16,0},{20,4},{24,8},{28,12},{1,17},{... | collective-permute-start | bytes 712712 | tf_op jit(solution)/shard_map/ppermute | solution.py:141
  (43 other events, 423.5 us)
Sparse Core Ops, SparseCore 0:
  16.0 77.1 all-gather.2
  96.6 123.2 all-gather.4

commit v3 on v1

v3 whole, which is shorter than its diff:
```python
import math
import jax, jax.numpy as jnp
from jax import lax
from jax.sharding import PartitionSpec as P
import jax.experimental.pallas as pl, jax.experimental.pallas.tpu as pltpu
HEADS=16
BF=jnp.bfloat16
F32=jnp.float32
COST=pl.CostEstimate(flops=10**9,bytes_accessed=10**6,transcendentals=0)

def mm(a,b,ca,cb):
    return lax.dot_general(a,b,(((ca,),(cb,)),((),())),preferred_element_type=F32)

def attend_kernel(scale, q_ref,k_ref,v_ref,ek_ref,eq_ref,segc_ref,segr_ref,ctx_ref,p_ref):
    t=q_ref.shape[0]; half=t//2
    hd=q_ref.shape[1]//2
    same=segc_ref[...]==segr_ref[...]
    lane=lax.broadcasted_iota(jnp.int32,q_ref.shape,1)
    ctx=None
    for h in range(2):
        mine=(lane>=h*hd)&(lane<(h+1)*hd)
        pick=lambda r: jnp.where(mine,r[...],jnp.zeros((),BF))
        q=pick(q_ref); k=pick(k_ref)
        s=mm(q,k_ref[...],1,1)
        to=pltpu.roll(mm(q,ek_ref[...],1,1),half,1,stride=1,stride_axis=0)
        fr=pltpu.roll(mm(k,eq_ref[...],1,1),half,1,stride=1,stride_axis=0)
        s=jnp.where(same,s+to+fr.T,-1e30)
        top=jnp.max(s,axis=1,keepdims=True)
        e=jnp.exp((s-top)*scale)
        p=(e*(1.0/jnp.sum(e,axis=1,keepdims=True))).astype(BF)
        p_ref[h]=p
        part=mm(p,pick(v_ref),1,0)
        ctx=part if ctx is None else ctx+part
    ctx_ref[...]=ctx.astype(BF)

def attend(q,k,v,ek,eq,seg,scale,made,at,count):
    t,d=q.shape
    w=2*d//HEADS
    col=pl.BlockSpec((t,w),lambda i:(0,i+at))
    made=[] if made is None else list(made)
    return pl.pallas_call(
        lambda *r: attend_kernel(scale,*r[:7],*r[len(r)-2:]),
        grid=(count,),
        in_specs=[col]*5+[pl.BlockSpec((t,1),lambda i:(0,0)),pl.BlockSpec((1,t),lambda i:(0,0))]+[pl.BlockSpec(memory_space=pl.ANY)]*len(made),
        out_specs=[col,pl.BlockSpec((2,t,t),lambda i:(i+at,0,0))],
        out_shape=[jax.ShapeDtypeStruct((t,d),BF),jax.ShapeDtypeStruct((HEADS,t,t),BF)],
        input_output_aliases={7+i:i for i in range(len(made))},
        cost_estimate=COST,
        compiler_params=pltpu.CompilerParams(vmem_limit_bytes=48*2**20),
    )(q,k,v,ek,eq,seg.reshape(t,1),seg.reshape(1,t),*made)

def attend_back_kernel(scale,q_ref,k_ref,v_ref,ek_ref,eq_ref,dc_ref,p_ref,dq_ref,dk_ref,dv_ref,dek_ref,deq_ref):
    t=q_ref.shape[0]; half=t//2
    hd=q_ref.shape[1]//2
    r=lax.broadcasted_iota(jnp.int32,(half,half),0); c=lax.broadcasted_iota(jnp.int32,(half,half),1)
    flip=(r+c==half-1).astype(BF)
    lane=lax.broadcasted_iota(jnp.int32,q_ref.shape,1)
    def turn(x):
        return jnp.concatenate([mm(flip,x[:half],1,0),mm(flip,x[half:],1,0)],0)
    def turn_t(x):
        return jnp.concatenate([mm(flip,x[:,:half],1,1),mm(flip,x[:,half:],1,1)],0)
    def unroll(x):
        return jnp.concatenate([pltpu.roll(x[:half],1,1,stride=1,stride_axis=0),pltpu.roll(x[half:],half+1,1,stride=1,stride_axis=0)],0)
    q_turned=turn(q_ref[...]).astype(BF); k_turned=turn(k_ref[...]).astype(BF)
    dqt=dkt=dv=dek=deq=None
    plus=lambda a,b: b if a is None else a+b
    for h in range(2):
        mine=(lane>=h*hd)&(lane<(h+1)*hd)
        pick=lambda x: jnp.where(mine,x,jnp.zeros((),BF))
        p=p_ref[h]; dc=pick(dc_ref[...])
        dp=mm(dc,v_ref[...],1,1)
        pf=p.astype(F32)
        w=pf*dp
        ds=(w-pf*jnp.sum(w,axis=1,keepdims=True)).astype(BF)
        dv=plus(dv,mm(p,dc,0,0))
        a=turn(ds).astype(BF); au=unroll(a)
        b=turn_t(ds).astype(BF); bu=unroll(b)
        dqt=plus(dqt,mm(a,pick(k_ref[...]),1,0)+mm(au,pick(ek_ref[...]),1,0))
        dkt=plus(dkt,mm(b,pick(q_ref[...]),1,0)+mm(bu,pick(eq_ref[...]),1,0))
        dek=plus(dek,mm(au,pick(q_turned),0,0))
        deq=plus(deq,mm(bu,pick(k_turned),0,0))
    dq_ref[...]=turn((dqt*scale).astype(BF)).astype(BF)
    dk_ref[...]=turn((dkt*scale).astype(BF)).astype(BF)
    dv_ref[...]=dv.astype(BF)
    dek_ref[...]=(dek*scale).astype(BF)
    deq_ref[...]=(deq*scale).astype(BF)

def attend_back(q,k,v,ek,eq,dc,p,scale,grads,at,count):
    t,d=q.shape
    w=2*d//HEADS
    col=pl.BlockSpec((t,w),lambda i:(0,i+at))
    grads=[] if grads is None else list(grads)
    return pl.pallas_call(
        lambda *r: attend_back_kernel(scale,*r[:7],*r[len(r)-5:]),
        grid=(count,),
        in_specs=[col]*6+[pl.BlockSpec((2,t,t),lambda i:(i+at,0,0))]+[pl.BlockSpec(memory_space=pl.ANY)]*len(grads),
        out_specs=[col]*5,
        out_shape=[jax.ShapeDtypeStruct((t,d),BF)]*5,
        input_output_aliases={7+i:i for i in range(len(grads))},
        cost_estimate=COST,
        compiler_params=pltpu.CompilerParams(vmem_limit_bytes=48*2**20),
    )(q,k,v,ek,eq,dc,p,*grads)


NORM_EPS = 1e-7
SPLIT = 9
TILE = 512


def norm_parts(v):
    mean = jnp.mean(v, axis=-1, keepdims=True)
    c = v - mean
    r = lax.rsqrt(jnp.mean(c * c, axis=-1, keepdims=True) + NORM_EPS)
    return c * r, r


def norm_back(g, gain, n, r):
    u = g * gain
    d = r * (u - jnp.mean(u, -1, keepdims=True) - n * jnp.mean(u * n, -1, keepdims=True))
    return d, jnp.sum(g * n, 0, keepdims=True), jnp.sum(g, 0, keepdims=True)


def stack(refs):
    return jnp.concatenate([r[...] for r in refs], 0) if len(refs) > 1 else refs[0][...]


def whole(shape):
    return pl.BlockSpec(shape, lambda j: (0,) * len(shape))


def arrays(pieces):
    return [a for a, _ in pieces]


def piece_blocks(pieces, width, block):
    out = []
    for array, column in pieces:
        out.append(pl.BlockSpec((array.shape[0], width), lambda j, base=column // width: (0, base + block(j))))
    return out


def column_blocks(pieces, width, first, step=1):
    return piece_blocks(pieces, width, lambda j: first + step * j)


def feed_forward(vecs, bu, up, dn, first, count, start=None, end=None):
    opening = len(start) == 3 and isinstance(start[2], list)
    n = len(up)
    if opening:
        context, x, wo = start
        t, d = x.shape
        ins = [context, x] + [a for a, _ in wo]
        specs = [whole((t, d))] * 2 + column_blocks(wo, d, 0, 0)
    else:
        t, d = start[0].shape
        ins, specs = list(start), [whole((t, d))] * 3
    n_start = len(ins)
    ins += [vecs, bu] + [a for a, _ in up] + [a for a, _ in dn] + ([] if end is None else [end])
    specs += [whole(vecs.shape), pl.BlockSpec((1, TILE), lambda j: (0, j + first))]
    specs += column_blocks(up, TILE, 0) + column_blocks(dn, TILE, 0) + ([] if end is None else [whole((t, d))])
    shape = jax.ShapeDtypeStruct
    tile_out = pl.BlockSpec((t, TILE), lambda j: (0, j))
    outs = [(shape((t, count * TILE), BF), tile_out)] * 2
    full = lambda dt: (shape((t, d), dt), whole((t, d)))
    if opening:
        outs += [full(F32), (shape((t, 1), F32), whole((t, 1))), full(F32), full(BF)]
    if end is None:
        outs += [full(F32)]
    else:
        outs += [full(BF), full(F32), full(BF), (shape((8, d), F32), whole((8, d)))]

    def kernel(*refs):
        j = pl.program_id(0)
        begin, refs = refs[:n_start], refs[n_start:]
        vec_ref, bu_ref, refs = refs[0], refs[1], refs[2:]
        up_refs, dn_refs, refs = refs[:n], refs[n : 2 * n], refs[2 * n :]
        if end is not None:
            cot_ref, refs = refs[0], refs[1:]
        act_ref, slope_ref, refs = refs[0], refs[1], refs[2:]
        if opening:
            n1_ref, r1_ref, mixed_ref, low_ref = refs[:4]
            refs = refs[4:]
        else:
            mixed_ref, low_ref = begin[:2]
        acc = refs[-1]

        @pl.when(j == 0)
        def _():
            if opening:
                v = begin[1][...].astype(F32) + mm(begin[0][...], stack(begin[2:]), 1, 1) + vec_ref[0:1, :]
                n1, r1 = norm_parts(v)
                n1_ref[...] = n1
                r1_ref[...] = r1
                mixed = n1 * vec_ref[1:2, :] + vec_ref[2:3, :]
                mixed_ref[...] = mixed
                low_ref[...] = mixed.astype(BF)
                acc[...] = jnp.zeros(acc.shape, F32)
            else:
                acc[...] = begin[2][...]

        up_val = mm(low_ref[...], stack(up_refs), 1, 0) + bu_ref[...]
        cdf = 0.5 * (1.0 + lax.erf(up_val * math.sqrt(0.5)))
        act = (up_val * cdf).astype(BF)
        act_ref[...] = act
        slope_ref[...] = (cdf + up_val * (jnp.exp(-0.5 * up_val * up_val) * (1.0 / math.sqrt(2.0 * math.pi)))).astype(BF)
        acc[...] += mm(act, stack(dn_refs), 1, 1)

        @pl.when(j == count - 1)
        def _():
            if end is None:
                refs[0][...] = acc[...]
            else:
                out_ref, d_sum_ref, d_ffn_ref, sums_ref = refs[:4]
                n2, r2 = norm_parts(mixed_ref[...] + acc[...] + vec_ref[3:4, :])
                gain = vec_ref[4:5, :]
                out_ref[...] = (n2 * gain + vec_ref[5:6, :]).astype(BF)
                d_sum, d_gain, d_shift = norm_back(cot_ref[...].astype(F32), gain, n2, r2)
                d_sum_ref[...] = d_sum
                low = d_sum.astype(BF)
                d_ffn_ref[...] = low
                sums_ref[0:1, :] = jnp.sum(low.astype(F32), 0, keepdims=True)
                sums_ref[1:2, :] = d_gain
                sums_ref[2:3, :] = d_shift
                sums_ref[3:8, :] = jnp.zeros((5, d), F32)

    return pl.pallas_call(
        kernel, grid=(count,), in_specs=specs, out_specs=[o[1] for o in outs], out_shape=[o[0] for o in outs],
        scratch_shapes=[pltpu.VMEM((t, d), F32)], cost_estimate=COST,
        compiler_params=pltpu.CompilerParams(vmem_limit_bytes=56 * 2**20),
    )(*ins)


def split_out(tree, n):
    quarter = tree.width // 4
    spec = pl.BlockSpec((quarter, TILE), lambda j: (0, j))
    return [(jax.ShapeDtypeStruct((quarter, n), BF), spec)] * 2


def write_split(tree, flipped, away_ref, column, low_ref, high_ref, kept, value):
    step = tree.nz * tree.rows
    order = tree.f_order(flipped)
    half, quarter = tree.width // 2, tree.width // 4
    n = value.shape[1]
    for at, f in enumerate(order):
        row = at * step
        away_ref[row : row + step, pl.ds(column, n)] = value[half + f * step : half + (f + 1) * step].astype(BF)
        ref, row = (low_ref, row) if row < quarter else (high_ref, row - quarter)
        ref[row : row + step, pl.ds(kept, n)] = value[f * step : (f + 1) * step].astype(BF)


def feed_back(tree, d_ffn, mixed_low, act, slope, up, dn, total, count, tail=None):
    t, d = d_ffn.shape
    n = len(up)
    tile = pl.BlockSpec((t, TILE), lambda j: (0, j))
    ins = [d_ffn, mixed_low, act, slope, total] + [a for a, _ in up] + [a for a, _ in dn]
    specs = [whole((t, d))] * 2 + [tile] * 2 + [whole((t, d))] + column_blocks(up, TILE, 0) + column_blocks(dn, TILE, 0)
    shape = jax.ShapeDtypeStruct
    full = lambda dt: (shape((t, d), dt), whole((t, d)))
    n_up = count * TILE + (0 if tail is None else d)
    n_dn = count * TILE
    quarter = d // 4
    big = lambda r, c: (shape((r, c), BF), whole((r, c)))
    outs = [big(d // 2, n_up + n_dn), big(quarter, n_up), big(quarter, n_up), big(quarter, n_dn), big(quarter, n_dn)]
    outs += [(shape((1, count * TILE), F32), pl.BlockSpec((1, TILE), lambda j: (0, j)))]
    if tail is None:
        outs += [full(F32)]
    else:
        context, wo, n1, r1, gain = tail
        ins += [context, n1, r1, gain] + [a for a, _ in wo]
        specs += [whole((t, d)), whole((t, d)), whole((t, 1)), whole((1, d))] + column_blocks(wo, d, 0, 0)
        outs += [full(BF), full(BF), full(BF), (shape((8, d), F32), whole((8, d)))]

    def kernel(*refs):
        j = pl.program_id(0)
        d_ffn_ref, low_ref, act_ref, slope_ref, total_ref = refs[:5]
        refs = refs[5:]
        up_refs, dn_refs, refs = refs[:n], refs[n : 2 * n], refs[2 * n :]
        if tail is not None:
            ctx_ref, n1_ref, r1_ref, gain_ref = refs[:4]
            wo_refs, refs = refs[4 : 4 + n], refs[4 + n :]
        away_ref, up_lo, up_hi, dn_lo, dn_hi, d_bu_ref = refs[:6]
        refs = refs[6:]
        acc, d_ffn_t, low_t = refs[-3:]

        @pl.when(j == 0)
        def _():
            acc[...] = total_ref[...]
            d_ffn_t[...] = d_ffn_ref[...].T
            low_t[...] = low_ref[...].T

        d_up = (mm(d_ffn_ref[...], stack(dn_refs), 1, 0) * slope_ref[...].astype(F32)).astype(BF)
        d_bu_ref[...] = jnp.sum(d_up.astype(F32), 0, keepdims=True)
        at = pl.multiple_of(j * TILE, TILE)
        write_split(tree, True, away_ref, n_up + at, dn_lo, dn_hi, at, mm(d_ffn_t[...], act_ref[...], 1, 0))
        write_split(tree, False, away_ref, at, up_lo, up_hi, at, mm(low_t[...], d_up, 1, 0))
        acc[...] += mm(d_up, stack(up_refs), 1, 1)

        @pl.when(j == count - 1)
        def _():
            if tail is None:
                refs[0][...] = acc[...]
            else:
                d_attn_ref, rest_ref, d_ctx_ref, sums_ref = refs[:4]
                d_first, d_gain, d_shift = norm_back(acc[...], gain_ref[...], n1_ref[...], r1_ref[...])
                d_attn = d_first.astype(BF)
                d_attn_ref[...] = d_attn
                rest_ref[...] = (d_first - d_attn.astype(F32)).astype(BF)
                d_ctx_ref[...] = mm(d_attn, stack(wo_refs), 1, 0).astype(BF)
                d_ffn_t[...] = d_attn.T
                write_split(tree, False, away_ref, n_dn, up_lo, up_hi, n_dn, mm(d_ffn_t[...], ctx_ref[...], 1, 0))
                sums_ref[0:1, :] = jnp.sum(d_attn.astype(F32), 0, keepdims=True)
                sums_ref[1:2, :] = d_gain
                sums_ref[2:3, :] = d_shift
                sums_ref[3:8, :] = jnp.zeros((5, d), F32)

    return pl.pallas_call(
        kernel, grid=(count,), in_specs=specs, out_specs=[o[1] for o in outs], out_shape=[o[0] for o in outs],
        scratch_shapes=[pltpu.VMEM((t, d), F32), pltpu.VMEM((d, t), BF), pltpu.VMEM((d, t), BF)], cost_estimate=COST,
        compiler_params=pltpu.CompilerParams(vmem_limit_bytes=60 * 2**20),
    )(*ins)


def project(x_p, onehot, low, high, bias, tile):
    t, d = x_p.shape
    buckets = onehot.shape[1]
    n = len(low)
    per = d // tile
    clip = lambda j, a: jnp.clip(j - a * per, 0, per - 1)
    specs = [whole((t, d)), whole(onehot.shape), pl.BlockSpec((1, tile), lambda j: (0, j))]
    specs += piece_blocks(low, tile, lambda j: jnp.minimum(j, 2 * per - 1))
    specs += piece_blocks(high, tile, lambda j: clip(j, 2))
    specs += piece_blocks(high, buckets, lambda j: d // buckets)
    out = lambda a: pl.BlockSpec((t, tile), lambda j: (0, clip(j, a)))

    def kernel(x_ref, hot_ref, bias_ref, *refs):
        lows, highs, tables, refs = refs[:n], refs[n : 2 * n], refs[2 * n : 3 * n], refs[3 * n :]
        q_ref, k_ref, v_ref, ek_ref, eq_ref, table = refs
        j = pl.program_id(0)

        @pl.when(j == 0)
        def _():
            table[...] = mm(hot_ref[...], stack(tables), 1, 1).astype(BF)

        def both(out_ref, e_ref):
            w = stack(lows)
            out_ref[...] = (mm(x_ref[...], w, 1, 0) + bias_ref[...]).astype(BF)
            e_ref[...] = (mm(table[...], w, 1, 0) + bias_ref[...]).astype(BF)

        pl.when(j < per)(lambda: both(q_ref, eq_ref))
        pl.when((j >= per) & (j < 2 * per))(lambda: both(k_ref, ek_ref))

        @pl.when(j >= 2 * per)
        def _():
            v_ref[...] = (mm(x_ref[...], stack(highs), 1, 0) + bias_ref[...]).astype(BF)

    return pl.pallas_call(
        kernel, grid=(3 * per,), in_specs=specs, out_specs=[out(0), out(1), out(2), out(1), out(0)],
        out_shape=[jax.ShapeDtypeStruct((t, d), BF)] * 5, scratch_shapes=[pltpu.VMEM((t, d), BF)], cost_estimate=COST,
        compiler_params=pltpu.CompilerParams(vmem_limit_bytes=48 * 2**20),
    )(x_p, onehot, bias, *arrays(low), *arrays(high), *arrays(high))


def attention_grads(tree, x_p, onehot, low, high, dq, dk, dv, dek, deq, lines, ordered, place_t, tile):
    t, d = x_p.shape
    buckets = onehot.shape[1]
    n = len(low)
    per = d // tile
    clip = lambda j, a: jnp.clip(j - a * per, 0, per - 1)
    half = d // 2
    col = lambda a: pl.BlockSpec((t, tile), lambda j: (0, clip(j, a)))
    specs = [whole((t, d)), whole(onehot.shape), col(0), col(1), col(2), col(1), col(0)]
    specs += [whole(lines.shape), whole(ordered.shape), whole((d, d))]
    specs += piece_blocks(low, tile, lambda j: jnp.minimum(j, 2 * per - 1))
    specs += piece_blocks(high, buckets, lambda j: d // buckets)
    wide = d + buckets + 128
    shape = jax.ShapeDtypeStruct
    quarter = d // 4
    big = lambda r, c: (shape((r, c), BF), whole((r, c)))
    outs = [big(half, 2 * d + wide), big(quarter, 2 * d), big(quarter, 2 * d), big(quarter, wide), big(quarter, wide)]

    def kernel(*refs):
        x_ref, hot_ref, dq_ref, dk_ref, dv_ref, dek_ref, deq_ref, lines_ref, ordered_ref, place_ref = refs[:10]
        lows, tables, refs = refs[10 : 10 + n], refs[10 + n : 10 + 2 * n], refs[10 + 2 * n :]
        away_ref, qk_lo, qk_hi, wide_lo, wide_hi = refs[:5]
        x_t, table, d_table, sums = refs[5:]
        j = pl.program_id(0)

        @pl.when(j == 0)
        def _():
            x_t[...] = x_ref[...].T
            table[...] = stack(tables)
            d_table[...] = jnp.zeros(d_table.shape, F32)

        def wide_write(at, value):
            write_split(tree, True, away_ref, 2 * d + at, wide_lo, wide_hi, at, value)

        def both(g_ref, e_ref, row, at):
            pos = mm(hot_ref[...], e_ref[...], 0, 0).astype(BF)
            g = g_ref[...]
            value = mm(x_t[...], g, 1, 0) + mm(table[...], pos, 1, 0)
            write_split(tree, False, away_ref, row * d + at, qk_lo, qk_hi, row * d + at, value)
            sums[row : row + 1, at : at + tile] = jnp.sum(g.astype(F32), 0, keepdims=True) + jnp.sum(
                pos.astype(F32), 0, keepdims=True
            )
            d_table[...] += mm(stack(lows), pos, 1, 1)

        for c in range(per):
            pl.when(j == c)(lambda c=c: both(dq_ref, deq_ref, 0, c * tile))
            pl.when(j == per + c)(lambda c=c: both(dk_ref, dek_ref, 1, c * tile))

            @pl.when(j == 2 * per + c)
            def _(c=c):
                g = dv_ref[...]
                wide_write(c * tile, mm(x_t[...], g, 1, 0))
                sums[2:3, c * tile : (c + 1) * tile] = jnp.sum(g.astype(F32), 0, keepdims=True)

        @pl.when(j == 3 * per - 1)
        def _():
            wide_write(d, d_table[...])
            vectors = jnp.concatenate([sums[0:3, :], lines_ref[...]], 0)
            pad = lambda v, lead: jnp.concatenate(
                ([jnp.zeros((lead, d), F32)] if lead else []) + [v, jnp.zeros((128 - lead - v.shape[0], d), F32)], 0
            )
            natural = mm(place_ref[...], pad(vectors, 0).astype(BF), 1, 1)
            wide_write(d + buckets, natural + pad(ordered_ref[...], 16).T)

    return pl.pallas_call(
        kernel, grid=(3 * per,), in_specs=specs, out_specs=[o[1] for o in outs], out_shape=[o[0] for o in outs],
        scratch_shapes=[
            pltpu.VMEM((d, t), BF), pltpu.VMEM((d, buckets), BF), pltpu.VMEM((d, buckets), F32), pltpu.VMEM((8, d), F32),
        ],
        cost_estimate=COST, compiler_params=pltpu.CompilerParams(vmem_limit_bytes=56 * 2**20),
    )(x_p, onehot, dq, dk, dv, dek, deq, lines, ordered, place_t, *arrays(low), *arrays(high))


def input_grads(d_attn, d_rest, low, high, dq, dk, dv, out_p, place_t, tile):
    t, d = d_attn.shape
    n = len(low)
    per = d // tile
    clip = lambda j, a: jnp.clip(j - a * per, 0, per - 1)
    col = lambda a: pl.BlockSpec((t, tile), lambda j: (0, clip(j, a)))
    specs = [whole((t, d)), whole((t, d)), col(0), col(1), col(2), whole((t, d)), whole((d, d))]
    specs += piece_blocks(low, tile, lambda j: jnp.minimum(j, 2 * per - 1))
    specs += piece_blocks(high, tile, lambda j: clip(j, 2))

    def kernel(*refs):
        a_ref, r_ref, dq_ref, dk_ref, dv_ref, out_ref, place_ref = refs[:7]
        lows, highs, refs = refs[7 : 7 + n], refs[7 + n : 7 + 2 * n], refs[7 + 2 * n :]
        grad_ref, layer_ref, acc = refs
        j = pl.program_id(0)

        @pl.when(j == 0)
        def _():
            acc[...] = a_ref[...].astype(F32) + r_ref[...].astype(F32)
            layer_ref[...] = mm(out_ref[...], place_ref[...], 1, 0).astype(BF)

        def add(g_ref, ws):
            acc[...] += mm(g_ref[...], stack(ws), 1, 1)

        pl.when(j < per)(lambda: add(dq_ref, lows))
        pl.when((j >= per) & (j < 2 * per))(lambda: add(dk_ref, lows))
        pl.when(j >= 2 * per)(lambda: add(dv_ref, highs))

        @pl.when(j == 3 * per - 1)
        def _():
            grad_ref[...] = mm(acc[...].astype(BF), place_ref[...], 1, 0).astype(BF)

    return pl.pallas_call(
        kernel, grid=(3 * per,), in_specs=specs, out_specs=[whole((t, d))] * 2,
        out_shape=[jax.ShapeDtypeStruct((t, d), BF)] * 2, scratch_shapes=[pltpu.VMEM((t, d), F32)], cost_estimate=COST,
        compiler_params=pltpu.CompilerParams(vmem_limit_bytes=48 * 2**20),
    )(d_attn, d_rest, dq, dk, dv, out_p, place_t, *arrays(low), *arrays(high))


class Tree:
    def __init__(self, width):
        self.nf, self.ndp = lax.axis_size("fsdp"), lax.axis_size("dp")
        self.n = self.nf * self.ndp
        self.nz = self.ndp // 2
        self.rows = width // self.n
        self.width = width
        self.f_bits = [1 << b for b in range(self.nf.bit_length() - 1)]
        self.z_bits = [1 << b for b in range(self.nz.bit_length() - 1)]

    def place(self, transposed):
        me = lax.axis_index("dp") * self.nf + lax.axis_index("fsdp")
        d = jnp.arange(self.width, dtype=jnp.int32)
        rel = (d // self.rows) ^ me
        f = rel % self.nf
        core = (rel // self.nf) % 2
        z = sum(((rel // (2 * self.nf * b)) % 2) * (self.nz // (2 * b)) for b in self.z_bits)
        at = ((core * self.nf + f) * self.nz + z) * self.rows + d % self.rows
        j = lax.broadcasted_iota(jnp.int32, (self.width, self.width), 0 if transposed else 1)
        return ((at[None, :] if transposed else at[:, None]) == j).astype(BF)

    def swap(self, a, axis, bit):
        size = self.nf if axis == "fsdp" else self.ndp
        return lax.ppermute(a, axis, [(i, i ^ bit) for i in range(size)])

    def f_order(self, flipped):
        order = self.f_bits[::-1] if flipped else self.f_bits
        key = lambda f: [f & bit != 0 for bit in order]
        return sorted(range(self.nf), key=key)

    def gather(self, sides):
        cur = jnp.concatenate([a for a, _ in sides], 1)
        columns = [0]
        for a, _ in sides:
            columns.append(columns[-1] + a.shape[1])
        for bit in self.z_bits[::-1]:
            (got,) = yield [self.swap(cur, "dp", 2 * bit)]
            cur = jnp.concatenate([cur, got], 0)
        found = [{0: (cur, c)} for c in columns[:-1]]
        orders = [self.f_bits[::-1] if flipped else self.f_bits for _, flipped in sides]

        def keep(keys, array, whole_row):
            for s, i in keys:
                found[s][i] = (array, columns[s] if whole_row else 0)

        every = range(len(sides))
        sends = [([(s, bit) for s in every], True, self.swap(cur, "fsdp", bit)) for bit in self.f_bits]
        cores = [([(s, self.nf) for s in every], True, self.swap(cur, "dp", 1))]
        level = 1
        while sends or cores:
            got = yield [x for _, _, x in sends + cores]
            for (keys, whole_row, _), g in zip(sends + cores, got):
                keep(keys, g, whole_row)
            arrived, sends, cores = sends, [], []
            for keys, whole_row, _ in arrived:
                i = keys[0][1]
                cores.append(([(s, self.nf + i) for s, _ in keys], whole_row, self.swap(found[keys[0][0]][i][0], "dp", 1)))
                for s, _ in keys:
                    array, column = found[s][i]
                    last = max(at for at, bit in enumerate(orders[s]) if i & bit)
                    for bit in orders[s][last + 1 :]:
                        part = array[:, column : column + columns[s + 1] - columns[s]]
                        sends.append(([(s, i | bit)], False, self.swap(part, "fsdp", bit)))
            level += 1
        return [[f[i] for i in range(2 * self.nf)] for f in found]


class Job:
    def __init__(self, tree, away, *sides):
        self.tree = tree
        self.away = away
        self.sides = [list(sides[:2]), list(sides[2:])]
        self.stages = ["core"] + list(range(len(tree.f_bits))) + [("z", b) for b in tree.z_bits]
        self.total = None

    def send(self):
        stage = self.stages[0]
        if stage == "core":
            return [self.tree.swap(self.away, "dp", 1)]
        if isinstance(stage, int):
            bits = self.tree.f_bits
            return [self.tree.swap(side[1], "fsdp", b[stage]) for side, b in zip(self.sides, (bits, bits[::-1]))]
        return [self.tree.swap(self.total[1], "dp", 2 * stage[1])]

    def add(self, got):
        stage = self.stages.pop(0)
        more = bool(self.stages)
        sums = lambda a, g: (a.astype(F32) + g.astype(F32)).astype(BF)
        if stage == "core":
            column = 0
            for side in self.sides:
                r, n = side[0].shape
                side[0] = sums(side[0], got[0][:r, column : column + n])
                side[1] = sums(side[1], got[0][r:, column : column + n])
                column += n
        elif isinstance(stage, int):
            for side, g in zip(self.sides, got):
                r = side[0].shape[0] // 2
                side[0], side[1] = sums(side[0][:r], g[:r]), sums(side[0][r:], g[r:])
            if not isinstance(self.stages[0], int):
                self.total = [jnp.concatenate([side[i] for side in self.sides], 1) for i in range(2)]
        else:
            keep = self.total[0]
            if more:
                r = keep.shape[0] // 2
                self.total = [sums(keep[:r], got[0][:r]), sums(keep[r:], got[0][r:])]
            else:
                self.total = keep.astype(F32) + got[0].astype(F32)

    def run(self):
        while self.stages:
            self.add(self.send())
        return self.total


class Flow:
    def __init__(self, steps):
        self.steps = steps
        self.value = None
        self.sends = next(steps)

    def take(self, got):
        try:
            self.sends = self.steps.send(got)
        except StopIteration as end:
            self.sends, self.value = [], end.value


def drain(flow):
    while flow.value is None:
        window([flow])


def window(flows, jobs=(), others=()):
    flows = [f for f in flows if f.value is None]
    jobs = [j for j in jobs if j.stages]
    sent = [list(f.sends) for f in flows] + [j.send() for j in jobs]
    sent, others = lax.optimization_barrier((sent, tuple(others)))
    for f, got in zip(flows, sent):
        f.take(list(got))
    for j, got in zip(jobs, sent[len(flows):]):
        j.add(list(got))
    return others


def per_device(
    tokens, segment_ids, rel_bucket, query_weight, query_bias, key_weight, key_bias, value_weight, value_bias,
    out_weight, out_bias, attention_gain, attention_shift, up_weight, up_bias, down_weight, down_bias,
    output_gain, output_shift, position_table, cotangent,
):
    x = tokens[0]
    t, d = x.shape
    seg = segment_ids[0]
    tree = Tree(d)
    rows = tree.rows
    ff = up_weight.shape[1]
    spread = ff // d
    buckets = position_table.shape[0]
    scale = 1.0 / math.sqrt(3.0 * (d // HEADS))
    vectors = (query_bias, key_bias, value_bias, out_bias, attention_gain, attention_shift, down_bias, output_gain, output_shift)
    small = jnp.concatenate([v[:, None] for v in vectors] + [up_bias.reshape(spread, rows).T], axis=1).astype(BF)
    small = jnp.pad(small, ((0, 0), (0, 128 - small.shape[1])))
    rest_cols = jnp.concatenate([value_weight.astype(BF), position_table.T.astype(BF), small], axis=1)
    query_key = jnp.concatenate([query_weight.astype(BF), key_weight.astype(BF)], axis=1)
    down_t = down_weight.T.astype(BF)
    cut = ff // 2
    out_up = jnp.concatenate([out_weight.T.astype(BF), up_weight[:, :cut].astype(BF)], axis=1)
    one = Flow(tree.gather([(query_key, False), (rest_cols, True)]))
    two = Flow(tree.gather([(out_up, False), (down_t[:, :cut], True)]))
    three = Flow(tree.gather([(up_weight[:, cut:].astype(BF), False), (down_t[:, cut:], True)]))

    place = tree.place(False)
    place_t = tree.place(True)
    half = t // 2
    picked = lax.rev(rel_bucket[t - half : 2 * t - half], (0,))
    onehot = (picked[:, None] == lax.broadcasted_iota(jnp.int32, (t, buckets), 1)).astype(BF)
    place, place_t, onehot = window([one], (), (place, place_t, onehot))
    arrange = lambda m: mm(m, place, 1, 0).astype(BF)
    x_p = arrange(x)
    (x_p,) = window([one, two], (), (x_p,))
    cot_p = arrange(cotangent[0])
    (cot_p,) = window([one, two], (), (cot_p,))
    window([one, three])
    drain(one)
    low, high = one.value

    small = jnp.concatenate([a[:, c + d + buckets : c + d + buckets + 128] for a, c in high], 0)
    vec = mm(small, place, 0, 1)
    vecs = small.T[3:11].astype(F32)
    bias = vec[:3].reshape(1, 3 * d)
    bu = vec[SPLIT : SPLIT + spread].reshape(spread, tree.n, rows).transpose(1, 0, 2).reshape(1, ff)
    q, k, v, ek, eq = project(x_p, onehot, low, high, bias, TILE)
    q, k, v, ek, eq = window([two, three], (), (q, k, v, ek, eq))
    n_pairs = HEADS // 2
    made = attend(q, k, v, ek, eq, seg, scale, None, 0, n_pairs // 2)
    made = window([two, three], (), made)
    made = attend(q, k, v, ek, eq, seg, scale, made, n_pairs // 2, n_pairs // 2)
    context, probs = window([two, three], (), made)

    drain(two)
    wo = two.value[0]
    shifted = lambda pieces, by: [(a, c + by) for a, c in pieces]
    up_a, dn_a = shifted(wo, d), two.value[1]
    count = cut // TILE
    act_a, slope_a, n1, r1, mixed, mixed_low, so_far = feed_forward(vecs, bu, up_a, dn_a, 0, count, (context, x_p, wo))
    (so_far,) = window([three], (), (so_far,))
    drain(three)
    up_b, dn_b = three.value
    act_b, slope_b, out_p, d_sum, d_ffn, sums2 = feed_forward(
        vecs, bu, up_b, dn_b, count, count, (mixed, mixed_low, so_far), cot_p
    )
    back = feed_back(tree, d_ffn, mixed_low, act_a, slope_a, up_a, dn_a, d_sum, count)
    job_1 = Job(tree, *back[:5])
    d_bu_a, total = back[5:]
    back = feed_back(
        tree, d_ffn, mixed_low, act_b, slope_b, up_b, dn_b, total, count, (context, wo, n1, r1, vecs[1:2])
    )
    job_2 = Job(tree, *back[:5])
    d_bu_b, d_attn, d_rest, d_context, sums1 = back[5:]
    (d_context,) = window([], [job_1], (d_context,))

    args = (q, k, v, ek, eq, d_context, probs, scale)
    grads = attend_back(*args, None, 0, n_pairs // 2)
    grads = window([], [job_1, job_2], grads)
    grads = attend_back(*args, grads, n_pairs // 2, n_pairs // 2)
    dq, dk, dv, dek, deq = window([], [job_1, job_2], grads)
    d_bu = jnp.concatenate([d_bu_a, d_bu_b], 1)
    lines = d_bu.reshape(tree.n, spread, rows).transpose(1, 0, 2).reshape(spread, d)
    ordered = jnp.concatenate([sums1[:3], sums2[:3]], 0)
    ordered = jnp.concatenate([ordered, jnp.zeros((2, d), F32)], 0)
    split = attention_grads(tree, x_p, onehot, low, high, dq, dk, dv, dek, deq, lines, ordered, place_t, TILE)
    split = window([], [job_1, job_2], split)
    job_3 = Job(tree, *split)
    d_attn, d_rest = window([], [job_3], (d_attn, d_rest))
    grad_layer = input_grads(d_attn, d_rest, low, high, dq, dk, dv, out_p, place_t, TILE)
    input_grad, layer_out = window([], [job_1, job_2, job_3], grad_layer)
    one, two, three = [job.run() for job in (job_1, job_2, job_3)]
    up_a_grad, dn_a_grad = one[:, :cut], one[:, cut:]
    up_b_grad, out_grad, dn_b_grad = two[:, :cut], two[:, cut : cut + d], two[:, cut + d :]
    rest_a, rest_b = three[:, : 2 * d], three[:, 2 * d :]
    tail = rest_b[:, d + buckets :]
    d_bq, d_bk, d_bv = [tail[:, i] for i in range(3)]
    d_up_bias = tail[:, 3 : 3 + spread].T.reshape(-1)
    d_bo, d_gain1, d_shift1, d_bd, d_gain2, d_shift2 = [tail[:, 16 + i] for i in range(6)]
    return (
        layer_out[None], input_grad[None],
        rest_a[:, :d], d_bq, rest_a[:, d:], d_bk, rest_b[:, :d], d_bv,
        out_grad.T, d_bo, d_gain1, d_shift1, jnp.concatenate([up_a_grad, up_b_grad], 1), d_up_bias,
        jnp.concatenate([dn_a_grad.T, dn_b_grad.T], 0), d_bd, d_gain2, d_shift2,
        rest_b[:, d : d + buckets].T,
    )


def solution(mesh):
    both = ("dp", "fsdp")
    row, col, vec = P(both, None), P(None, both), P(both)
    seq = P(both, None, None)
    params = (row, vec, row, vec, row, vec, col, vec, vec, vec, row, vec, col, vec, vec, vec, col)
    return jax.shard_map(
        per_device, mesh=mesh, in_specs=(seq, row, P()) + params + (seq,), out_specs=(seq, seq) + params, check_vma=False
    )
```

time: 559 us -> 478 us (0.86)
  waiting for transfers between devices: 281 us -> 160 us
  matrix products: 126 us -> 5.28 us
  Pallas kernels: 66.3 us -> 187 us
  starting transfers between devices: 22 us -> 46.3 us
  other arithmetic: 33 us -> 48.6 us
  between operations: 15.3 us -> 2.3 us
  local copies, waits for them, and re-layouts: 11.9 us -> 22.6 us
    all_gather x2 -> x0, waiting for transfers between devices: 139 us -> none  [the longest x1 75.3 us: per_device(): w2 = lax.all_gather(second, ('dp', 'fsdp'), axis=0, tiled=True)]
    dot_general x40 -> x3, matrix products: 126 us -> 5.28 us  [mm(): lax.dot_general(a, b, (((ca,), (cb,)), ((), ())), preferred_element_type=...]
    pallas_call x2 -> x11, Pallas kernels: 66.3 us -> 187 us  [the longest x2 41.9 us: feed_back(): pl.pallas_call(kernel, grid=(count,), in_specs=specs, out_specs=[o[1] for...]
    ppermute x24 -> x54, starting transfers between devices: 21.9 us -> 46.3 us  [swap(): return lax.ppermute(a, axis, [(i, i ^ bit) for i in range(size)])]
    ppermute x24 -> x54, waiting for transfers between devices: 142 us -> 160 us  [swap(): return lax.ppermute(a, axis, [(i, i ^ bit) for i in range(size)])]
    convert_element_type x16 -> x24, other arithmetic: 11.8 us -> 27 us  [the longest x20 22 us: add(): sums = lambda a, g: (a.astype(F32) + g.astype(F32)).astype(BF)]
    concatenate x1 -> x15, other arithmetic: 0.85 us -> 6.81 us  [the longest x6 3.43 us: gather(): cur = jnp.concatenate([cur, got], 0)]
  transfers between devices with their start and end apart: 26 -> 54, of which waited for: 16 -> 22; matrix products, arithmetic and copies ran while one was open for 14% -> 9% of each run, Pallas kernels for 6% -> 33%
where the time goes in v3:
time: 478 us; the launch traced here: 471 us
  Pallas kernels  187 us (39%)
  waiting for transfers between devices  160 us (33%)
  other arithmetic  48.6 us (10%)
  starting transfers between devices  46.3 us (10%)
  local copies, waits for them, and re-layouts  22.6 us (5%)
  matrix products  5.28 us (1%)
    ppermute x54, waiting for transfers between devices, swap(): return lax.ppermute(a, axis, [(i, i ^ bit) for i in range(size)])  160 us
    ppermute x54, starting transfers between devices, swap(): return lax.ppermute(a, axis, [(i, i ^ bit) for i in range(size)])  46.3 us
    pallas_call x2, Pallas kernels, feed_back(): pl.pallas_call(kernel, grid=(count,), in_specs=specs, out_specs=[o[1] for...  41.9 us
    pallas_call x2, Pallas kernels, attend(): pl.pallas_call(lambda *r: attend_kernel(scale, *r[:7], *r[len(r) - 2:]),...  34.9 us
    pallas_call x2, Pallas kernels, attend_back(): pl.pallas_call(lambda *r: attend_back_kernel(scale, *r[:7], *r[len(r) - 5...  34.6 us
    pallas_call x2, Pallas kernels, feed_forward(): pl.pallas_call(kernel, grid=(count,), in_specs=specs, out_specs=[o[1] for...  30.3 us
    convert_element_type x20, other arithmetic, add(): sums = lambda a, g: (a.astype(F32) + g.astype(F32)).astype(BF)  22 us
    pallas_call x1, Pallas kernels, attention_grads(): pl.pallas_call(kernel, grid=(3 * per,), in_specs=specs, out_specs=[o[1] f...  18.8 us
  transfers between devices with their start and end apart: 54, of which 22 were waited for; matrix products, arithmetic and copies ran while one was open for 9% of the time, Pallas kernels for 33%

profile of v3, /device:TPU:0, one launch (start us, length us, event | category | flops | bytes accessed | tf_op | source)
XLA Modules:
  0.0 471.4 jit_solution(17003675776977014949)
XLA Ops:
  38.9 10.8 %collective-permute-done.2 = bf16[32,5120]{1,0:T(8,128)(2,1)S(1)} collective-permute-done((bf16[32,5120]{1,0:T(8,128)(2,1)S(1)}, bf16[32,5120]{1,0:T(8,128)(2,1)S(1)}, u32[]{:S(2)}, u32[]{:S(2)}) %collective-permute-start.2) | collective-permute-done | bytes 327712 | tf_op jit(solution)/shard_map/ppermute | solution.py:498
  62.3 16.5 %collective-permute-done.6 = bf16[64,5120]{1,0:T(8,128)(2,1)S(1)} collective-permute-done((bf16[64,5120]{1,0:T(8,128)(2,1)S(1)}, bf16[64,5120]{1,0:T(8,128)(2,1)S(1)}, u32[]{:S(2)}, u32[]{:S(2)}) %collective-permute-start.6) | collective-permute-done | bytes 655392 | tf_op jit(solution)/shard_map/ppermute | solution.py:498
  80.6 11.4 %collective-permute-done.11.refs_11_.refs_19_.refs_21_.refs_18_ = bf16[128,1664]{1,0:T(8,128)(2,1)S(1)} collective-permute-done((bf16[128,1664]{1,0:T(8,128)(2,1)S(1)}, bf16[128,1664]{1,0:T(8,128)(2,1)S(1)}, u32[]{:S(2)}, u32[]{:S(2)}) %collective-permute-start.11) | collective-permute-done | bytes 426016 | tf_op jit(solution)/shard_map/ppermute | solution.py:498
  99.7 12.4 %shard_map.348 = (bf16[512,1024]{1,0:T(8,128)(2,1)}, bf16[512,1024]{1,0:T(8,128)(2,1)}, bf16[512,1024]{1,0:T(8,128)(2,1)}, bf16[512,1024]{1,0:T(8,128)(2,1)}, bf16[512,1024]{1,0:T(8,128)(2,1)}) custom-call(bf16[512,1024]{1,0:T(8,128)(2,1)} %fusion.2.x_ref.refs_1_.refs_0_, bf16[512,512]{1,0:T(8,128)(2,1)S(1)} %fusion.6.hot_ref.refs_1_, ...), custom_call_target="tpu_custom_call" | custom-call | flops 1000000000 | bytes 1000000 | tf_op jit(solution)/shard_map/pallas_call | solution.py:356
  112.1 10.2 %collective-permute-done.8.refs_4_.refs_14_.refs_22_.refs_7_.refs_15_.refs_27_ = bf16[128,5120]{1,0:T(8,128)(2,1)} collective-permute-done((bf16[128,5120]{1,0:T(8,128)(2,1)S(1)}, bf16[128,5120]{1,0:T(8,128)(2,1)}, u32[]{:S(2)}, u32[]{:S(2)}) %collective-permute-start.8) | collective-permute-done | bytes 1310752 | tf_op jit(solution)/shard_map/ppermute | solution.py:498
  129.1 9.8 %collective-permute-done.19.refs_23_.refs_16_ = bf16[128,2048]{1,0:T(8,128)(2,1)S(1)} collective-permute-done((bf16[128,2048]{1,0:T(8,128)(2,1)S(1)}, bf16[128,2048]{1,0:T(8,128)(2,1)S(1)}, u32[]{:S(2)}, u32[]{:S(2)}) %collective-permute-start.19) | collective-permute-done | bytes 524320 | tf_op jit(solution)/shard_map/ppermute | solution.py:498
  147.9 17.5 %shard_map.349 = (bf16[512,1024]{1,0:T(8,128)(2,1)S(1)}, bf16[16,512,512]{2,1,0:T(8,128)(2,1)}) custom-call(bf16[512,1024]{1,0:T(8,128)(2,1)S(1)} %copy-done.10, bf16[512,1024]{1,0:T(8,128)(2,1)S(1)} %copy-done.11, bf16[512,1024]{1,0:T(8,128)(2,1)S(1)} %copy-done.12, bf16[512,1024]{1,0:T(8,128)(2,1)S(1)} %copy-done.13, ...), custom_call_target="tpu_custom_call" | custom-call | flops 1000000000 | bytes 1000000 | tf_op jit(solution)/shard_map/pallas_call | solution.py:41
  169.9 8.4 %collective-permute-done.28.refs_16_ = bf16[128,2048]{1,0:T(8,128)(2,1)} collective-permute-done((bf16[128,2048]{1,0:T(8,128)(2,1)S(1)}, bf16[128,2048]{1,0:T(8,128)(2,1)}, u32[]{:S(2)}, u32[]{:S(2)}) %collective-permute-start.28) | collective-permute-done | bytes 524320 | tf_op jit(solution)/shard_map/ppermute | solution.py:498
  178.3 17.4 %shard_map.350 = (bf16[512,1024]{1,0:T(8,128)(2,1)S(1)}, bf16[16,512,512]{2,1,0:T(8,128)(2,1)}) custom-call(bf16[512,1024]{1,0:T(8,128)(2,1)S(1)} %copy-done.10, bf16[512,1024]{1,0:T(8,128)(2,1)S(1)} %copy-done.11, bf16[512,1024]{1,0:T(8,128)(2,1)S(1)} %copy-done.12, bf16[512,1024]{1,0:T(8,128)(2,1)S(1)} %copy-done.13, ...), custom_call_target="tpu_custom_call", output_to_operand_aliasing={{0}: (7, {}), {1}: (8, {})} | custom-call | flops 1000000000 | bytes 1000000 | tf_op jit(solution)/shard_map/pallas_call | solution.py:41
  201.8 15.5 %shard_map.351 = (bf16[512,2048]{1,0:T(8,128)(2,1)}, bf16[512,2048]{1,0:T(8,128)(2,1)}, f32[512,1024]{1,0:T(8,128)}, f32[512,1]{1,0:T(8,128)}, f32[512,1024]{1,0...) custom-call(bf16[512,1024]{1,0:T(8,128)(2,1)} %copy-done.14, bf16[512,1024]{1,0:T(8,128)(2,1)} %fusion.2.x_ref.refs_1_.refs_0_, ...), custom_call_target="tpu_custom_call" | custom-call | flops 1000000000 | bytes 1000000 | tf_op jit(solution)/shard_map/pallas_call | solution.py:226
  218.4 14.8 %shard_map.352 = (bf16[512,2048]{1,0:T(8,128)(2,1)}, bf16[512,2048]{1,0:T(8,128)(2,1)}, bf16[512,1024]{1,0:T(8,128)(2,1)}, f32[512,1024]{1,0:T(8,128)}, bf16[512,1024]{1,0:T(8,128)(2,1)}, /*index=5*/f32[8,1024]{1,0:T(8,128)}) custom-call(f32[512,1024]{1,0:T(8,128)} %get-tuple-element.205.refs_0_, bf16[512,1024]{1,0:T(8,128)(2,1)} %get-tuple-element.206.refs_1_, ...), custom_call_target="tpu_custom_call" | custom-call | flops 1000000000 | bytes 1000000 | tf_op jit(solution)/shard_map/pallas_call | solution.py:226
  233.2 17.9 %shard_map.353 = (bf16[512,4096]{1,0:T(8,128)(2,1)}, bf16[256,2048]{1,0:T(8,128)(2,1)}, bf16[256,2048]{1,0:T(8,128)(2,1)}, bf16[256,2048]{1,0:T(8,128)(2,1)}, bf...) custom-call(bf16[512,1024]{1,0:T(8,128)(2,1)} %get-tuple-element.217.refs_0_, ...), custom_call_target="tpu_custom_call" | custom-call | flops 1000000000 | bytes 1000000 | tf_op jit(solution)/shard_map/pallas_call | solution.py:316
  252.7 23.9 %shard_map.354 = (bf16[512,5120]{1,0:T(8,128)(2,1)}, bf16[256,3072]{1,0:T(8,128)(2,1)}, bf16[256,3072]{1,0:T(8,128)(2,1)}, bf16[256,2048]{1,0:T(8,128)(2,1)}, bf...) custom-call(bf16[512,1024]{1,0:T(8,128)(2,1)} %get-tuple-element.217, ...), custom_call_target="tpu_custom_call" | custom-call | flops 1000000000 | bytes 1000000 | tf_op jit(solution)/shard_map/pallas_call | solution.py:316
  276.7 6.1 %add_convert_fusion.6 = (bf16[256,2048]{1,0:T(8,128)(2,1)S(1)}, bf16[256,2048]{1,0:T(8,128)(2,1)}, bf16[256,2048]{1,0:T(8,128)(2,1)}, bf16[256,2048]{1,0:T(8,128)(2,1)S(1)}) fusion(bf16[256,2048]{1,0:T(8,128)(2,1)S(1)} %copy-done.51, bf16[512,4096]{1,0:T(8,128)(2,1)} %collective-permute-done.33, bf16[256,2048]{1,0:T(8,128)(2,1)} %get-tuple-element.231, ...), kind=kLoop, calls=%fused_computation.10 | loop fusion | flops 8388608 | bytes 12582912 | tf_op jit(solution)/shard_map/convert_element_type | solution.py:562
  283.9 17.4 %shard_map.355 = (bf16[512,1024]{1,0:T(8,128)(2,1)S(1)}, bf16[512,1024]{1,0:T(8,128)(2,1)S(1)}, bf16[512,1024]{1,0:T(8,128)(2,1)S(1)}, bf16[512,1024]{1,0:T(8,128)(2,1)S(1)}, bf16[512,1024]{1,0:T(8,128)(2,1)S(1)}) custom-call(bf16[512,1024]{1,0:T(8,128)(2,1)} %get-tuple-element.184.r_0_, bf16[512,1024]{1,0:T(8,128)(2,1)} %get-tuple-element.185.r_1_, ...), custom_call_target="tpu_custom_call" | custom-call | flops 1000000000 | bytes 1000000 | tf_op jit(solution)/shard_map/pallas_call | solution.py:93
  301.3 7.4 %collective-permute-done.35 = bf16[256,2048]{1,0:T(8,128)(2,1)} collective-permute-done((bf16[256,2048]{1,0:T(8,128)(2,1)}, bf16[256,2048]{1,0:T(8,128)(2,1)}, u32[]{:S(2)}, u32[]{:S(2)}) %collective-permute-start.35) | collective-permute-done | bytes 1048608 | tf_op jit(solution)/shard_map/ppermute | solution.py:498
  321.6 17.2 %shard_map.356 = (bf16[512,1024]{1,0:T(8,128)(2,1)S(1)}, bf16[512,1024]{1,0:T(8,128)(2,1)S(1)}, bf16[512,1024]{1,0:T(8,128)(2,1)S(1)}, bf16[512,1024]{1,0:T(8,128)(2,1)S(1)}, bf16[512,1024]{1,0:T(8,128)(2,1)S(1)}) custom-call(bf16[512,1024]{1,0:T(8,128)(2,1)} %get-tuple-element.184.r_0, ...), custom_call_target="tpu_custom_call", output_to_operand_aliasing={{0}: (7, {}), {1}: (8, {}), {2}: (9, {}), {3}: (10, {}), {4... | custom-call | flops 1000000000 | bytes 1000000 | tf_op jit(solution)/shard_map/pallas_call | solution.py:93
  338.9 22.1 %collective-permute-done.38 = bf16[128,2048]{1,0:T(8,128)(2,1)S(1)} collective-permute-done((bf16[128,2048]{1,0:T(8,128)(2,1)S(1)}, bf16[128,2048]{1,0:T(8,128)(2,1)S(1)}, u32[]{:S(2)}, u32[]{:S(2)}) %collective-permute-start.38) | collective-permute-done | bytes 524320 | tf_op jit(solution)/shard_map/ppermute | solution.py:498
  371.5 18.8 %shard_map.357 = (bf16[512,3712]{1,0:T(8,128)(2,1)}, bf16[256,2048]{1,0:T(8,128)(2,1)}, bf16[256,2048]{1,0:T(8,128)(2,1)}, bf16[256,1664]{1,0:T(8,128)(2,1)}, bf16[256,1664]{1,0:T(8,128)(2,1)}) custom-call(bf16[512,1024]{1,0:T(8,128)(2,1)} %fusion.2.x_ref.refs_1_.refs_0_, bf16[512,512]{1,0:T(8,128)(2,1)} %copy-done.22, bf16[512,1024]{1,0:T(8,128)(2,1)} %copy-done.15, ...), custom_call_target="tpu_custom_call" | custom-call | flops 1000000000 | bytes 1000000 | tf_op jit(solution)/shard_map/pallas_call | solution.py:427
  402.6 13.8 %shard_map.358 = (bf16[512,1024]{1,0:T(8,128)(2,1)}, bf16[512,1024]{1,0:T(8,128)(2,1)}) custom-call(bf16[512,1024]{1,0:T(8,128)(2,1)} %get-tuple-element.286.refs_0_, bf16[512,1024]{1,0:T(8,128)(2,1)} %get-tuple-element.287.refs_1_, bf16[512,1024]{1,0:T(8,128)(2,1)} %copy-done.15, bf16[512,1024]{1,0:T(8,128)(2,1)} %copy-done.16, ...), custom_call_target="tpu_custom_call" | custom-call | flops 1000000000 | bytes 1000000 | tf_op jit(solution)/shard_map/pallas_call | solution.py:468
  418.9 5.9 %collective-permute-done.47 = bf16[256,2048]{1,0:T(8,128)(2,1)S(1)} collective-permute-done((bf16[256,2048]{1,0:T(8,128)(2,1)S(1)}, bf16[256,2048]{1,0:T(8,128)(2,1)S(1)}, u32[]{:S(2)}, u32[]{:S(2)}) %collective-permute-start.47) | collective-permute-done | bytes 1048608 | tf_op jit(solution)/shard_map/ppermute | solution.py:498
  429.4 12.2 %collective-permute-done.53 = bf16[32,5120]{1,0:T(8,128)(2,1)S(1)} collective-permute-done((bf16[32,5120]{1,0:T(8,128)(2,1)S(1)}, bf16[32,5120]{1,0:T(8,128)(2,1)S(1)}, u32[]{:S(2)}, u32[]{:S(2)}) %collective-permute-start.53) | collective-permute-done | bytes 327712 | tf_op jit(solution)/shard_map/ppermute | solution.py:498
  443.0 11.9 %collective-permute-done.51 = bf16[64,3712]{1,0:T(8,128)(2,1)S(1)} collective-permute-done((bf16[64,3712]{1,0:T(8,128)(2,1)S(1)}, bf16[64,3712]{1,0:T(8,128)(2,1)S(1)}, u32[]{:S(2)}, u32[]{:S(2)}) %collective-permute-start.51) | collective-permute-done | bytes 475168 | tf_op jit(solution)/shard_map/ppermute | solution.py:498
  456.5 11.3 %collective-permute-done.52 = bf16[32,3712]{1,0:T(8,128)(2,1)S(1)} collective-permute-done((bf16[32,3712]{1,0:T(8,128)(2,1)S(1)}, bf16[32,3712]{1,0:T(8,128)(2,1)S(1)}, u32[]{:S(2)}, u32[]{:S(2)}) %collective-permute-start.52) | collective-permute-done | bytes 237600 | tf_op jit(solution)/shard_map/ppermute | solution.py:498
  (351 shorter events, 138.5 us)
Async XLA Ops:
  51.8 26.9 %collective-permute-start.5 = (bf16[128,3712]{1,0:T(8,128)(2,1)S(1)}, bf16[128,3712]{1,0:T(8,128)(2,1)S(1)}, u32[]{:S(2)}, u32[]{:S(2)}) collective-permute-start(bf16[128,3712]{1,0:T(8,128)(2,1)S(1)} %pad_maximum_fusion.2.refs_0_.refs_8_.refs_16_.refs_10_.refs_18_.refs_7_.refs_15_), channel_id=1, source_target_pairs={{0,4},{4,0},{8,12},{12,8},{16,20},{20,16},{24,28},{28,24},{1,5},{5... | collective-permute-start | bytes 2850824 | tf_op jit(solution)/shard_map/ppermute | solution.py:498
  51.9 26.9 %collective-permute-start.4 = (bf16[128,3712]{1,0:T(8,128)(2,1)S(1)}, bf16[128,3712]{1,0:T(8,128)(2,1)S(1)}, u32[]{:S(2)}, u32[]{:S(2)}) collective-permute-start(bf16[128,3712]{1,0:T(8,128)(2,1)S(1)} %pad_maximum_fusion.2.refs_0_.refs_8_.refs_16_.refs_10_.refs_18_.refs_7_.refs_15_), channel_id=1, source_target_pairs={{0,2},{1,3},{2,0},{3,1},{4,6},{5,7},{6,4},{7,5},{8,10},{9,11},{10,... | collective-permute-start | bytes 2850824 | tf_op jit(solution)/shard_map/ppermute | solution.py:498
  53.3 25.5 %collective-permute-start.3 = (bf16[128,3712]{1,0:T(8,128)(2,1)S(1)}, bf16[128,3712]{1,0:T(8,128)(2,1)S(1)}, u32[]{:S(2)}, u32[]{:S(2)}) collective-permute-start(bf16[128,3712]{1,0:T(8,128)(2,1)S(1)} %pad_maximum_fusion.2.refs_0_.refs_8_.refs_16_.refs_10_.refs_18_.refs_7_.refs_15_), channel_id=1, source_target_pairs={{0,1},{1,0},{2,3},{3,2},{4,5},{5,4},{6,7},{7,6},{8,9},{9,8},{10,11... | collective-permute-start | bytes 2850824 | tf_op jit(solution)/shard_map/ppermute | solution.py:498
  80.5 31.7 %collective-permute-start.9 = (bf16[128,5120]{1,0:T(8,128)(2,1)S(1)}, bf16[128,5120]{1,0:T(8,128)(2,1)S(1)}, u32[]{:S(2)}, u32[]{:S(2)}) collective-permute-start(bf16[128,5120]{1,0:T(8,128)(2,1)S(1)} %pad_maximum_fusion.refs_2_.refs_12_.refs_20_.refs_5_.refs_13_.refs_25_), channel_id=1, source_target_pairs={{0,4},{4,0},{8,12},{12,8},{16,20},{20,16},{24,28},{28,24},{1,5},{5... | collective-permute-start | bytes 3932168 | tf_op jit(solution)/shard_map/ppermute | solution.py:498
  92.0 30.3 %collective-permute-start.8 = (bf16[128,5120]{1,0:T(8,128)(2,1)S(1)}, bf16[128,5120]{1,0:T(8,128)(2,1)}, u32[]{:S(2)}, u32[]{:S(2)}) collective-permute-start(bf16[128,5120]{1,0:T(8,128)(2,1)S(1)} %pad_maximum_fusion.refs_2_.refs_12_.refs_20_.refs_5_.refs_13_.refs_25_), channel_id=1, source_target_pairs={{0,2},{1,3},{2,0},{3,1},{4,6},{5,7},{6,4},{7,5},{8,10},{9,11},{10,... | collective-permute-start | bytes 3932168 | tf_op jit(solution)/shard_map/ppermute | solution.py:498
  93.5 30.2 %collective-permute-start.7 = (bf16[128,5120]{1,0:T(8,128)(2,1)S(1)}, bf16[128,5120]{1,0:T(8,128)(2,1)}, u32[]{:S(2)}, u32[]{:S(2)}) collective-permute-start(bf16[128,5120]{1,0:T(8,128)(2,1)S(1)} %pad_maximum_fusion.refs_2_.refs_12_.refs_20_.refs_5_.refs_13_.refs_25_), channel_id=1, source_target_pairs={{0,1},{1,0},{2,3},{3,2},{4,5},{5,4},{6,7},{7,6},{8,9},{9,8},{10,11... | collective-permute-start | bytes 3932168 | tf_op jit(solution)/shard_map/ppermute | solution.py:498
  95.9 27.9 %collective-permute-start.15 = (bf16[64,4096]{1,0:T(8,128)(2,1)S(1)}, bf16[64,4096]{1,0:T(8,128)(2,1)S(1)}, u32[]{:S(2)}, u32[]{:S(2)}) collective-permute-start(bf16[64,4096]{1,0:T(8,128)(2,1)S(1)} %pad_maximum_fusion.5), channel_id=1, source_target_pairs={{0,8},{4,12},{8,0},{12,4},{16,24},{20,28},{24,16},{28,20},{1,9},{5... | collective-permute-start | bytes 1572872 | tf_op jit(solution)/shard_map/ppermute | solution.py:498
  127.5 38.5 %collective-permute-start.20 = (bf16[128,5120]{1,0:T(8,128)(2,1)}, bf16[128,5120]{1,0:T(8,128)(2,1)}, u32[]{:S(2)}, u32[]{:S(2)}) collective-permute-start(bf16[128,5120]{1,0:T(8,128)(2,1)} %collective-permute-done.7.refs_3_.refs_13_.refs_21_.refs_6_.refs_14_.refs_26_), channel_id=1, source_target_pairs={{0,4},{4,0},{8,12},{12,8},{16,20},{20,16},{24,28},{28,24},{1,5},{5... | collective-permute-start | bytes 3932168 | tf_op jit(solution)/shard_map/ppermute | solution.py:498
  127.5 38.5 %collective-permute-start.21 = (bf16[128,5120]{1,0:T(8,128)(2,1)}, bf16[128,5120]{1,0:T(8,128)(2,1)}, u32[]{:S(2)}, u32[]{:S(2)}) collective-permute-start(bf16[128,5120]{1,0:T(8,128)(2,1)} %collective-permute-done.8.refs_4_.refs_14_.refs_22_.refs_7_.refs_15_.refs_27_), channel_id=1, source_target_pairs={{0,4},{4,0},{8,12},{12,8},{16,20},{20,16},{24,28},{28,24},{1,5},{5... | collective-permute-start | bytes 3932168 | tf_op jit(solution)/shard_map/ppermute | solution.py:498
  129.1 36.3 %collective-permute-start.24 = (bf16[128,4096]{1,0:T(8,128)(2,1)}, bf16[128,4096]{1,0:T(8,128)(2,1)}, u32[]{:S(2)}, u32[]{:S(2)}) collective-permute-start(bf16[128,4096]{1,0:T(8,128)(2,1)} %pad_maximum_fusion.1.refs_5_.refs_13_), channel_id=1, source_target_pairs={{0,4},{4,0},{8,12},{12,8},{16,20},{20,16},{24,28},{28,24},{1,5},{5... | collective-permute-start | bytes 3145736 | tf_op jit(solution)/shard_map/ppermute | solution.py:498
  138.9 26.7 %collective-permute-start.23 = (bf16[128,4096]{1,0:T(8,128)(2,1)}, bf16[128,4096]{1,0:T(8,128)(2,1)}, u32[]{:S(2)}, u32[]{:S(2)}) collective-permute-start(bf16[128,4096]{1,0:T(8,128)(2,1)} %pad_maximum_fusion.1.refs_5_.refs_13_), channel_id=1, source_target_pairs={{0,2},{1,3},{2,0},{3,1},{4,6},{5,7},{6,4},{7,5},{8,10},{9,11},{10,... | collective-permute-start | bytes 3145736 | tf_op jit(solution)/shard_map/ppermute | solution.py:498
  167.8 29.9 %collective-permute-start.29 = (bf16[128,4096]{1,0:T(8,128)(2,1)}, bf16[128,4096]{1,0:T(8,128)(2,1)}, u32[]{:S(2)}, u32[]{:S(2)}) collective-permute-start(bf16[128,4096]{1,0:T(8,128)(2,1)} %collective-permute-done.22.refs_6_.refs_14_), channel_id=1, source_target_pairs={{0,4},{4,0},{8,12},{12,8},{16,20},{20,16},{24,28},{28,24},{1,5},{5... | collective-permute-start | bytes 3145736 | tf_op jit(solution)/shard_map/ppermute | solution.py:498
  167.8 29.9 %collective-permute-start.30 = (bf16[128,4096]{1,0:T(8,128)(2,1)}, bf16[128,4096]{1,0:T(8,128)(2,1)}, u32[]{:S(2)}, u32[]{:S(2)}) collective-permute-start(bf16[128,4096]{1,0:T(8,128)(2,1)} %collective-permute-done.23.refs_7_.refs_15_), channel_id=1, source_target_pairs={{0,4},{4,0},{8,12},{12,8},{16,20},{20,16},{24,28},{28,24},{1,5},{5... | collective-permute-start | bytes 3145736 | tf_op jit(solution)/shard_map/ppermute | solution.py:498
  168.3 28.4 %collective-permute-start.25 = (bf16[128,3072]{1,0:T(8,128)(2,1)S(1)}, bf16[128,3072]{1,0:T(8,128)(2,1)S(1)}, u32[]{:S(2)}, u32[]{:S(2)}) collective-permute-start(bf16[128,3072]{1,0:T(8,128)(2,1)S(1)} %copy-done.35), channel_id=1, source_target_pairs={{0,4},{4,0},{8,12},{12,8},{16,20},{20,16},{24,28},{28,24},{1,5},{5... | collective-permute-start | bytes 2359304 | tf_op jit(solution)/shard_map/ppermute | solution.py:498
  169.4 27.3 %collective-permute-start.27 = (bf16[128,2048]{1,0:T(8,128)(2,1)S(1)}, bf16[128,2048]{1,0:T(8,128)(2,1)}, u32[]{:S(2)}, u32[]{:S(2)}) collective-permute-start(bf16[128,2048]{1,0:T(8,128)(2,1)S(1)} %slice.386), channel_id=1, source_target_pairs={{0,2},{1,3},{2,0},{3,1},{4,6},{5,7},{6,4},{7,5},{8,10},{9,11},{10,... | collective-permute-start | bytes 1572872 | tf_op jit(solution)/shard_map/ppermute | solution.py:498
  251.1 25.6 %collective-permute-start.33 = (bf16[512,4096]{1,0:T(8,128)(2,1)}, bf16[512,4096]{1,0:T(8,128)(2,1)}, u32[]{:S(2)}, u32[]{:S(2)}) collective-permute-start(bf16[512,4096]{1,0:T(8,128)(2,1)} %get-tuple-element.222), channel_id=1, source_target_pairs={{0,4},{4,0},{8,12},{12,8},{16,20},{20,16},{24,28},{28,24},{1,5},{5... | collective-permute-start | bytes 12582920 | tf_op jit(solution)/shard_map/ppermute | solution.py:498
  276.6 32.2 %collective-permute-start.36 = (bf16[512,5120]{1,0:T(8,128)(2,1)}, bf16[512,5120]{1,0:T(8,128)(2,1)S(1)}, u32[]{:S(2)}, u32[]{:S(2)}) collective-permute-start(bf16[512,5120]{1,0:T(8,128)(2,1)} %get-tuple-element.232), channel_id=1, source_target_pairs={{0,4},{4,0},{8,12},{12,8},{16,20},{20,16},{24,28},{28,24},{1,5},{5... | collective-permute-start | bytes 15728648 | tf_op jit(solution)/shard_map/ppermute | solution.py:498
  282.8 25.9 %collective-permute-start.35 = (bf16[256,2048]{1,0:T(8,128)(2,1)}, bf16[256,2048]{1,0:T(8,128)(2,1)}, u32[]{:S(2)}, u32[]{:S(2)}) collective-permute-start(bf16[256,2048]{1,0:T(8,128)(2,1)} %get-tuple-element.313), channel_id=1, source_target_pairs={{0,2},{1,3},{2,0},{3,1},{4,6},{5,7},{6,4},{7,5},{8,10},{9,11},{10,... | collective-permute-start | bytes 3145736 | tf_op jit(solution)/shard_map/ppermute | solution.py:498
  283.3 25.5 %collective-permute-start.34 = (bf16[256,2048]{1,0:T(8,128)(2,1)}, bf16[256,2048]{1,0:T(8,128)(2,1)S(1)}, u32[]{:S(2)}, u32[]{:S(2)}) collective-permute-start(bf16[256,2048]{1,0:T(8,128)(2,1)} %get-tuple-element.314), channel_id=1, source_target_pairs={{0,1},{1,0},{2,3},{3,2},{4,5},{5,4},{6,7},{7,6},{8,9},{9,8},{10,11... | collective-permute-start | bytes 3145736 | tf_op jit(solution)/shard_map/ppermute | solution.py:498
  313.7 47.3 %collective-permute-start.39 = (bf16[256,3072]{1,0:T(8,128)(2,1)}, bf16[256,3072]{1,0:T(8,128)(2,1)}, u32[]{:S(2)}, u32[]{:S(2)}) collective-permute-start(bf16[256,3072]{1,0:T(8,128)(2,1)} %get-tuple-element.311), channel_id=1, source_target_pairs={{0,1},{1,0},{2,3},{3,2},{4,5},{5,4},{6,7},{7,6},{8,9},{9,8},{10,11... | collective-permute-start | bytes 4718600 | tf_op jit(solution)/shard_map/ppermute | solution.py:498
  316.0 45.0 %collective-permute-start.40 = (bf16[256,2048]{1,0:T(8,128)(2,1)}, bf16[256,2048]{1,0:T(8,128)(2,1)S(1)}, u32[]{:S(2)}, u32[]{:S(2)}) collective-permute-start(bf16[256,2048]{1,0:T(8,128)(2,1)} %get-tuple-element.309), channel_id=1, source_target_pairs={{0,2},{1,3},{2,0},{3,1},{4,6},{5,7},{6,4},{7,5},{8,10},{9,11},{10,... | collective-permute-start | bytes 3145736 | tf_op jit(solution)/shard_map/ppermute | solution.py:498
  319.1 41.9 %collective-permute-start.38 = (bf16[128,2048]{1,0:T(8,128)(2,1)S(1)}, bf16[128,2048]{1,0:T(8,128)(2,1)S(1)}, u32[]{:S(2)}, u32[]{:S(2)}) collective-permute-start(bf16[128,2048]{1,0:T(8,128)(2,1)S(1)} %get-tuple-element.327), channel_id=1, source_target_pairs={{0,1},{1,0},{2,3},{3,2},{4,5},{5,4},{6,7},{7,6},{8,9},{9,8},{10,11... | collective-permute-start | bytes 1572872 | tf_op jit(solution)/shard_map/ppermute | solution.py:498
  321.1 39.9 %collective-permute-start.37 = (bf16[128,2048]{1,0:T(8,128)(2,1)S(1)}, bf16[128,2048]{1,0:T(8,128)(2,1)S(1)}, u32[]{:S(2)}, u32[]{:S(2)}) collective-permute-start(bf16[128,2048]{1,0:T(8,128)(2,1)S(1)} %get-tuple-element.328), channel_id=1, source_target_pairs={{0,2},{1,3},{2,0},{3,1},{4,6},{5,7},{6,4},{7,5},{8,10},{9,11},{10,... | collective-permute-start | bytes 1572872 | tf_op jit(solution)/shard_map/ppermute | solution.py:498
  362.4 28.0 %collective-permute-start.43 = (bf16[128,2048]{1,0:T(8,128)(2,1)}, bf16[128,2048]{1,0:T(8,128)(2,1)}, u32[]{:S(2)}, u32[]{:S(2)}) collective-permute-start(bf16[128,2048]{1,0:T(8,128)(2,1)} %get-tuple-element.325), channel_id=1, source_target_pairs={{0,1},{1,0},{2,3},{3,2},{4,5},{5,4},{6,7},{7,6},{8,9},{9,8},{10,11... | collective-permute-start | bytes 1572872 | tf_op jit(solution)/shard_map/ppermute | solution.py:498
  (99 other events, 1388.6 us)

commit v4 on v3

--- a/solution.py
+++ b/solution.py
@@ -46,7 +46,7 @@
         out_shape=[jax.ShapeDtypeStruct((t,d),BF),jax.ShapeDtypeStruct((HEADS,t,t),BF)],
         input_output_aliases={7+i:i for i in range(len(made))},
         cost_estimate=COST,
-        compiler_params=pltpu.CompilerParams(vmem_limit_bytes=48*2**20),
+        compiler_params=pltpu.CompilerParams(vmem_limit_bytes=60 * 2**20),
     )(q,k,v,ek,eq,seg.reshape(t,1),seg.reshape(1,t),*made)
 
 def attend_back_kernel(scale,q_ref,k_ref,v_ref,ek_ref,eq_ref,dc_ref,p_ref,dq_ref,dk_ref,dv_ref,dek_ref,deq_ref):
@@ -98,13 +98,14 @@
         out_shape=[jax.ShapeDtypeStruct((t,d),BF)]*5,
         input_output_aliases={7+i:i for i in range(len(grads))},
         cost_estimate=COST,
-        compiler_params=pltpu.CompilerParams(vmem_limit_bytes=48*2**20),
+        compiler_params=pltpu.CompilerParams(vmem_limit_bytes=60 * 2**20),
     )(q,k,v,ek,eq,dc,p,*grads)
 
 
 NORM_EPS = 1e-7
 SPLIT = 9
 TILE = 512
+WIDE = 512
 
 
 def norm_parts(v):
@@ -126,6 +127,21 @@
 
 def whole(shape):
     return pl.BlockSpec(shape, lambda j: (0,) * len(shape))
+
+
+def join(blocks):
+    rows, n = blocks[0].shape
+    if rows % 16:
+        return jnp.concatenate(blocks, 0)
+
+    def kernel(*refs):
+        for i, r in enumerate(refs[:-1]):
+            refs[-1][i * rows : (i + 1) * rows, :] = r[...]
+
+    return pl.pallas_call(
+        kernel, out_shape=jax.ShapeDtypeStruct((rows * len(blocks), n), BF), cost_estimate=COST,
+        compiler_params=pltpu.CompilerParams(vmem_limit_bytes=32 * 2**20),
+    )(*blocks)
 
 
 def arrays(pieces):
@@ -156,11 +172,11 @@
         ins, specs = list(start), [whole((t, d))] * 3
     n_start = len(ins)
     ins += [vecs, bu] + [a for a, _ in up] + [a for a, _ in dn] + ([] if end is None else [end])
-    specs += [whole(vecs.shape), pl.BlockSpec((1, TILE), lambda j: (0, j + first))]
-    specs += column_blocks(up, TILE, 0) + column_blocks(dn, TILE, 0) + ([] if end is None else [whole((t, d))])
+    specs += [whole(vecs.shape), pl.BlockSpec((1, WIDE), lambda j: (0, j + first))]
+    specs += column_blocks(up, WIDE, 0) + column_blocks(dn, WIDE, 0) + ([] if end is None else [whole((t, d))])
     shape = jax.ShapeDtypeStruct
-    tile_out = pl.BlockSpec((t, TILE), lambda j: (0, j))
-    outs = [(shape((t, count * TILE), BF), tile_out)] * 2
+    tile_out = pl.BlockSpec((t, WIDE), lambda j: (0, j))
+    outs = [(shape((t, count * WIDE), BF), tile_out)] * 2
     full = lambda dt: (shape((t, d), dt), whole((t, d)))
     if opening:
         outs += [full(F32), (shape((t, 1), F32), whole((t, 1))), full(F32), full(BF)]
@@ -230,12 +246,6 @@
     )(*ins)
 
 
-def split_out(tree, n):
-    quarter = tree.width // 4
-    spec = pl.BlockSpec((quarter, TILE), lambda j: (0, j))
-    return [(jax.ShapeDtypeStruct((quarter, n), BF), spec)] * 2
-
-
 def write_split(tree, flipped, away_ref, column, low_ref, high_ref, kept, value):
     step = tree.nz * tree.rows
     order = tree.f_order(flipped)
@@ -251,17 +261,17 @@
 def feed_back(tree, d_ffn, mixed_low, act, slope, up, dn, total, count, tail=None):
     t, d = d_ffn.shape
     n = len(up)
-    tile = pl.BlockSpec((t, TILE), lambda j: (0, j))
+    tile = pl.BlockSpec((t, WIDE), lambda j: (0, j))
     ins = [d_ffn, mixed_low, act, slope, total] + [a for a, _ in up] + [a for a, _ in dn]
-    specs = [whole((t, d))] * 2 + [tile] * 2 + [whole((t, d))] + column_blocks(up, TILE, 0) + column_blocks(dn, TILE, 0)
+    specs = [whole((t, d))] * 2 + [tile] * 2 + [whole((t, d))] + column_blocks(up, WIDE, 0) + column_blocks(dn, WIDE, 0)
     shape = jax.ShapeDtypeStruct
     full = lambda dt: (shape((t, d), dt), whole((t, d)))
-    n_up = count * TILE + (0 if tail is None else d)
-    n_dn = count * TILE
+    n_up = count * WIDE + (0 if tail is None else d)
+    n_dn = count * WIDE
     quarter = d // 4
     big = lambda r, c: (shape((r, c), BF), whole((r, c)))
     outs = [big(d // 2, n_up + n_dn), big(quarter, n_up), big(quarter, n_up), big(quarter, n_dn), big(quarter, n_dn)]
-    outs += [(shape((1, count * TILE), F32), pl.BlockSpec((1, TILE), lambda j: (0, j)))]
+    outs += [(shape((1, count * WIDE), F32), pl.BlockSpec((1, WIDE), lambda j: (0, j)))]
     if tail is None:
         outs += [full(F32)]
     else:
@@ -290,7 +300,7 @@
 
         d_up = (mm(d_ffn_ref[...], stack(dn_refs), 1, 0) * slope_ref[...].astype(F32)).astype(BF)
         d_bu_ref[...] = jnp.sum(d_up.astype(F32), 0, keepdims=True)
-        at = pl.multiple_of(j * TILE, TILE)
+        at = pl.multiple_of(j * WIDE, WIDE)
         write_split(tree, True, away_ref, n_up + at, dn_lo, dn_hi, at, mm(d_ffn_t[...], act_ref[...], 1, 0))
         write_split(tree, False, away_ref, at, up_lo, up_hi, at, mm(low_t[...], d_up, 1, 0))
         acc[...] += mm(d_up, stack(up_refs), 1, 1)
@@ -320,6 +330,49 @@
     )(*ins)
 
 
+def pack_first(query, key, value, table, vectors, up_bias):
+    rows, d = query.shape
+    buckets = table.shape[1]
+    spread = up_bias.shape[0]
+    wide = 3 * d + buckets + 128
+
+    def kernel(q_ref, k_ref, v_ref, t_ref, *refs):
+        vec_refs, ub_ref, out_ref, lines = refs[:-3], refs[-3], refs[-2], refs[-1]
+        out_ref[:, 0:d] = q_ref[...].astype(BF)
+        out_ref[:, d : 2 * d] = k_ref[...].astype(BF)
+        out_ref[:, 2 * d : 3 * d] = v_ref[...].astype(BF)
+        out_ref[:, 3 * d : 3 * d + buckets] = t_ref[...].astype(BF)
+        lines[...] = jnp.zeros(lines.shape, F32)
+        for i, r in enumerate(vec_refs):
+            lines[i : i + 1, 0:rows] = r[...]
+        lines[len(vec_refs) : len(vec_refs) + spread, 0:rows] = ub_ref[...]
+        out_ref[:, 3 * d + buckets : wide] = lines[...].T[:rows].astype(BF)
+
+    return pl.pallas_call(
+        kernel, out_shape=jax.ShapeDtypeStruct((rows, wide), BF), scratch_shapes=[pltpu.VMEM((128, 128), F32)],
+        cost_estimate=COST, compiler_params=pltpu.CompilerParams(vmem_limit_bytes=60 * 2**20),
+    )(query, key, value, table, *[v.reshape(1, rows) for v in vectors], up_bias)
+
+
+def pack_second(out_weight, up, down):
+    rows, ff = up.shape
+    d = out_weight.shape[1]
+    cut = ff // 2
+
+    def kernel(o_ref, u_ref, d_ref, a_ref, b_ref):
+        down_t = d_ref[...].astype(BF)
+        a_ref[:, 0:d] = o_ref[...].astype(BF)
+        a_ref[:, d : d + cut] = u_ref[:, 0:cut].astype(BF)
+        a_ref[:, d + cut : d + 2 * cut] = down_t[:, 0:cut]
+        b_ref[:, 0:cut] = u_ref[:, cut:ff].astype(BF)
+        b_ref[:, cut : 2 * cut] = down_t[:, cut:ff]
+
+    return pl.pallas_call(
+        kernel, out_shape=[jax.ShapeDtypeStruct((rows, d + 2 * cut), BF), jax.ShapeDtypeStruct((rows, 2 * cut), BF)],
+        cost_estimate=COST, compiler_params=pltpu.CompilerParams(vmem_limit_bytes=60 * 2**20),
+    )(out_weight, up, down)
+
+
 def project(x_p, onehot, low, high, bias, tile):
     t, d = x_p.shape
     buckets = onehot.shape[1]
@@ -356,81 +409,88 @@
     return pl.pallas_call(
         kernel, grid=(3 * per,), in_specs=specs, out_specs=[out(0), out(1), out(2), out(1), out(0)],
         out_shape=[jax.ShapeDtypeStruct((t, d), BF)] * 5, scratch_shapes=[pltpu.VMEM((t, d), BF)], cost_estimate=COST,
-        compiler_params=pltpu.CompilerParams(vmem_limit_bytes=48 * 2**20),
+        compiler_params=pltpu.CompilerParams(vmem_limit_bytes=60 * 2**20),
     )(x_p, onehot, bias, *arrays(low), *arrays(high), *arrays(high))
 
 
-def attention_grads(tree, x_p, onehot, low, high, dq, dk, dv, dek, deq, lines, ordered, place_t, tile):
+def attention_grads(tree, x_p, onehot, low, high, dq, dk, dv, dek, deq, tile, part, carried=None):
     t, d = x_p.shape
     buckets = onehot.shape[1]
     n = len(low)
     per = d // tile
-    clip = lambda j, a: jnp.clip(j - a * per, 0, per - 1)
-    half = d // 2
-    col = lambda a: pl.BlockSpec((t, tile), lambda j: (0, clip(j, a)))
-    specs = [whole((t, d)), whole(onehot.shape), col(0), col(1), col(2), col(1), col(0)]
-    specs += [whole(lines.shape), whole(ordered.shape), whole((d, d))]
-    specs += piece_blocks(low, tile, lambda j: jnp.minimum(j, 2 * per - 1))
+    last = carried is not None
+    half, quarter = d // 2, d // 4
+    col = pl.BlockSpec((t, tile), lambda j: (0, part))
+    specs = [whole((t, d)), whole(onehot.shape)] + [col] * 5
+    specs += piece_blocks(low, tile, lambda j: jnp.minimum(j, 1) * per + part)
     specs += piece_blocks(high, buckets, lambda j: d // buckets)
-    wide = d + buckets + 128
+    ins = [x_p, onehot, dq, dk, dv, dek, deq] + arrays(low) + arrays(high)
+    if last:
+        ins += list(carried)
+        specs += [whole(a.shape) for a in carried]
+    wide = tile + (buckets + 128 if last else 0)
     shape = jax.ShapeDtypeStruct
-    quarter = d // 4
     big = lambda r, c: (shape((r, c), BF), whole((r, c)))
-    outs = [big(half, 2 * d + wide), big(quarter, 2 * d), big(quarter, 2 * d), big(quarter, wide), big(quarter, wide)]
+    outs = [big(half, 2 * tile + wide), big(quarter, 2 * tile), big(quarter, 2 * tile), big(quarter, wide), big(quarter, wide)]
+    if not last:
+        outs += [(shape((d, buckets), F32), whole((d, buckets))), (shape((8, tile), F32), whole((8, tile)))]
 
     def kernel(*refs):
-        x_ref, hot_ref, dq_ref, dk_ref, dv_ref, dek_ref, deq_ref, lines_ref, ordered_ref, place_ref = refs[:10]
-        lows, tables, refs = refs[10 : 10 + n], refs[10 + n : 10 + 2 * n], refs[10 + 2 * n :]
+        x_ref, hot_ref, dq_ref, dk_ref, dv_ref, dek_ref, deq_ref = refs[:7]
+        lows, tables, refs = refs[7 : 7 + n], refs[7 + n : 7 + 2 * n], refs[7 + 2 * n :]
+        if last:
+            before_ref, sums_before_ref, lines_ref, ordered_ref, place_ref = refs[:5]
+            refs = refs[5:]
         away_ref, qk_lo, qk_hi, wide_lo, wide_hi = refs[:5]
-        x_t, table, d_table, sums = refs[5:]
+        if last:
+            x_t, table, d_table, sums = refs[5:]
+        else:
+            d_table, sums, x_t, table = refs[5:]
         j = pl.program_id(0)
 
         @pl.when(j == 0)
         def _():
             x_t[...] = x_ref[...].T
             table[...] = stack(tables)
-            d_table[...] = jnp.zeros(d_table.shape, F32)
+            d_table[...] = before_ref[...] if last else jnp.zeros(d_table.shape, F32)
+            sums[...] = jnp.zeros(sums.shape, F32)
 
         def wide_write(at, value):
-            write_split(tree, True, away_ref, 2 * d + at, wide_lo, wide_hi, at, value)
-
-        def both(g_ref, e_ref, row, at):
+            write_split(tree, True, away_ref, 2 * tile + at, wide_lo, wide_hi, at, value)
+
+        def both(g_ref, e_ref, row):
             pos = mm(hot_ref[...], e_ref[...], 0, 0).astype(BF)
             g = g_ref[...]
             value = mm(x_t[...], g, 1, 0) + mm(table[...], pos, 1, 0)
-            write_split(tree, False, away_ref, row * d + at, qk_lo, qk_hi, row * d + at, value)
-            sums[row : row + 1, at : at + tile] = jnp.sum(g.astype(F32), 0, keepdims=True) + jnp.sum(
-                pos.astype(F32), 0, keepdims=True
-            )
+            write_split(tree, False, away_ref, row * tile, qk_lo, qk_hi, row * tile, value)
+            sums[row : row + 1, :] = jnp.sum(g.astype(F32), 0, keepdims=True) + jnp.sum(pos.astype(F32), 0, keepdims=True)
             d_table[...] += mm(stack(lows), pos, 1, 1)
 
-        for c in range(per):
-            pl.when(j == c)(lambda c=c: both(dq_ref, deq_ref, 0, c * tile))
-            pl.when(j == per + c)(lambda c=c: both(dk_ref, dek_ref, 1, c * tile))
-
-            @pl.when(j == 2 * per + c)
-            def _(c=c):
-                g = dv_ref[...]
-                wide_write(c * tile, mm(x_t[...], g, 1, 0))
-                sums[2:3, c * tile : (c + 1) * tile] = jnp.sum(g.astype(F32), 0, keepdims=True)
-
-        @pl.when(j == 3 * per - 1)
-        def _():
-            wide_write(d, d_table[...])
-            vectors = jnp.concatenate([sums[0:3, :], lines_ref[...]], 0)
-            pad = lambda v, lead: jnp.concatenate(
-                ([jnp.zeros((lead, d), F32)] if lead else []) + [v, jnp.zeros((128 - lead - v.shape[0], d), F32)], 0
-            )
-            natural = mm(place_ref[...], pad(vectors, 0).astype(BF), 1, 1)
-            wide_write(d + buckets, natural + pad(ordered_ref[...], 16).T)
-
-    return pl.pallas_call(
-        kernel, grid=(3 * per,), in_specs=specs, out_specs=[o[1] for o in outs], out_shape=[o[0] for o in outs],
-        scratch_shapes=[
-            pltpu.VMEM((d, t), BF), pltpu.VMEM((d, buckets), BF), pltpu.VMEM((d, buckets), F32), pltpu.VMEM((8, d), F32),
-        ],
-        cost_estimate=COST, compiler_params=pltpu.CompilerParams(vmem_limit_bytes=56 * 2**20),
-    )(x_p, onehot, dq, dk, dv, dek, deq, lines, ordered, place_t, *arrays(low), *arrays(high))
+        pl.when(j == 0)(lambda: both(dq_ref, deq_ref, 0))
+        pl.when(j == 1)(lambda: both(dk_ref, dek_ref, 1))
+
+        @pl.when(j == 2)
+        def _():
+            g = dv_ref[...]
+            wide_write(0, mm(x_t[...], g, 1, 0))
+            sums[2:3, :] = jnp.sum(g.astype(F32), 0, keepdims=True)
+            if last:
+                wide_write(tile, d_table[...])
+                known = [sums_before_ref[0:3, i * tile : (i + 1) * tile] for i in range(per - 1)]
+                vectors = jnp.concatenate([jnp.concatenate(known + [sums[0:3, :]], 1), lines_ref[...]], 0)
+                pad = lambda v, lead: jnp.concatenate(
+                    ([jnp.zeros((lead, d), F32)] if lead else []) + [v, jnp.zeros((128 - lead - v.shape[0], d), F32)], 0
+                )
+                natural = mm(place_ref[...], pad(vectors, 0).astype(BF), 1, 1)
+                wide_write(tile + buckets, natural + pad(ordered_ref[...], 16).T)
+
+    scratch = [pltpu.VMEM((d, t), BF), pltpu.VMEM((d, buckets), BF)]
+    if last:
+        scratch += [pltpu.VMEM((d, buckets), F32), pltpu.VMEM((8, tile), F32)]
+    return pl.pallas_call(
+        kernel, grid=(3,), in_specs=specs, out_specs=[o[1] for o in outs], out_shape=[o[0] for o in outs],
+        scratch_shapes=scratch, cost_estimate=COST, compiler_params=pltpu.CompilerParams(vmem_limit_bytes=56 * 2**20),
+    )(*ins)
 
 
 def input_grads(d_attn, d_rest, low, high, dq, dk, dv, out_p, place_t, tile):
@@ -502,14 +562,19 @@
         key = lambda f: [f & bit != 0 for bit in order]
         return sorted(range(self.nf), key=key)
 
-    def gather(self, sides):
-        cur = jnp.concatenate([a for a, _ in sides], 1)
+    def gather(self, cur, sides, direct=False):
         columns = [0]
-        for a, _ in sides:
-            columns.append(columns[-1] + a.shape[1])
-        for bit in self.z_bits[::-1]:
-            (got,) = yield [self.swap(cur, "dp", 2 * bit)]
-            cur = jnp.concatenate([cur, got], 0)
+        for width, _ in sides:
+            columns.append(columns[-1] + width)
+        if direct and self.nz <= 4:
+            got = yield [(cur, "dp", 2 * z) for z in range(1, self.nz)]
+            got = [cur] + list(got)
+            near_first = sorted(range(self.nz), key=lambda z: [z & bit != 0 for bit in self.z_bits])
+            cur = join([got[z] for z in near_first])
+        else:
+            for bit in self.z_bits[::-1]:
+                (got,) = yield [(cur, "dp", 2 * bit)]
+                cur = join([cur, got])
         found = [{0: (cur, c)} for c in columns[:-1]]
         orders = [self.f_bits[::-1] if flipped else self.f_bits for _, flipped in sides]
 
@@ -518,9 +583,8 @@
                 found[s][i] = (array, columns[s] if whole_row else 0)
 
         every = range(len(sides))
-        sends = [([(s, bit) for s in every], True, self.swap(cur, "fsdp", bit)) for bit in self.f_bits]
-        cores = [([(s, self.nf) for s in every], True, self.swap(cur, "dp", 1))]
-        level = 1
+        sends = [([(s, bit) for s in every], True, (cur, "fsdp", bit)) for bit in self.f_bits]
+        cores = [([(s, self.nf) for s in every], True, (cur, "dp", 1))]
         while sends or cores:
             got = yield [x for _, _, x in sends + cores]
             for (keys, whole_row, _), g in zip(sends + cores, got):
@@ -528,14 +592,13 @@
             arrived, sends, cores = sends, [], []
             for keys, whole_row, _ in arrived:
                 i = keys[0][1]
-                cores.append(([(s, self.nf + i) for s, _ in keys], whole_row, self.swap(found[keys[0][0]][i][0], "dp", 1)))
+                cores.append(([(s, self.nf + i) for s, _ in keys], whole_row, (found[keys[0][0]][i][0], "dp", 1)))
                 for s, _ in keys:
                     array, column = found[s][i]
                     last = max(at for at, bit in enumerate(orders[s]) if i & bit)
                     for bit in orders[s][last + 1 :]:
                         part = array[:, column : column + columns[s + 1] - columns[s]]
-                        sends.append(([(s, i | bit)], False, self.swap(part, "fsdp", bit)))
-            level += 1
+                        sends.append(([(s, i | bit)], False, (part, "fsdp", bit)))
         return [[f[i] for i in range(2 * self.nf)] for f in found]
 
 
@@ -543,18 +606,20 @@
     def __init__(self, tree, away, *sides):
         self.tree = tree
         self.away = away
-        self.sides = [list(sides[:2]), list(sides[2:])]
-        self.stages = ["core"] + list(range(len(tree.f_bits))) + [("z", b) for b in tree.z_bits]
+        self.sides = [list(side) for side in sides]
+        self.stages = ([] if away is None else ["core"]) + list(range(len(tree.f_bits))) + [("z", b) for b in tree.z_bits]
         self.total = None
 
-    def send(self):
+    def wanted(self):
+        if not self.stages:
+            return []
         stage = self.stages[0]
         if stage == "core":
-            return [self.tree.swap(self.away, "dp", 1)]
+            return [(self.away, "dp", 1)]
         if isinstance(stage, int):
             bits = self.tree.f_bits
-            return [self.tree.swap(side[1], "fsdp", b[stage]) for side, b in zip(self.sides, (bits, bits[::-1]))]
-        return [self.tree.swap(self.total[1], "dp", 2 * stage[1])]
+            return [(side[1], "fsdp", (bits[::-1] if side[2] else bits)[stage]) for side in self.sides]
+        return [(self.total[1], "dp", 2 * stage[1])]
 
     def add(self, got):
         stage = self.stages.pop(0)
@@ -572,7 +637,8 @@
                 r = side[0].shape[0] // 2
                 side[0], side[1] = sums(side[0][:r], g[:r]), sums(side[0][r:], g[r:])
             if not isinstance(self.stages[0], int):
-                self.total = [jnp.concatenate([side[i] for side in self.sides], 1) for i in range(2)]
+                cat = lambda xs: xs[0] if len(xs) == 1 else jnp.concatenate(xs, 1)
+                self.total = [cat([side[i] for side in self.sides]) for i in range(2)]
         else:
             keep = self.total[0]
             if more:
@@ -581,10 +647,15 @@
             else:
                 self.total = keep.astype(F32) + got[0].astype(F32)
 
-    def run(self):
-        while self.stages:
-            self.add(self.send())
-        return self.total
+    def hold(self, arrays):
+        stage = self.stages[0]
+        if stage == "core":
+            (self.away,) = arrays
+        elif isinstance(stage, int):
+            for side, a in zip(self.sides, arrays):
+                side[1] = a
+        else:
+            self.total[1] = arrays[0]
 
 
 class Flow:
@@ -593,27 +664,46 @@
         self.value = None
         self.sends = next(steps)
 
-    def take(self, got):
+    def wanted(self):
+        return list(self.sends)
+
+    def add(self, got):
         try:
             self.sends = self.steps.send(got)
         except StopIteration as end:
             self.sends, self.value = [], end.value
 
-
-def drain(flow):
+    def hold(self, arrays):
+        self.sends = [(a,) + rest[1:] for a, rest in zip(arrays, self.sends)]
+
+
+class Pair:
+    def __init__(self, *arrays):
+        self.arrays = arrays
+        self.value = None
+
+    def wanted(self):
+        return [] if self.value is not None else [(a, "dp", 1) for a in self.arrays]
+
+    def add(self, got):
+        self.value = got
+
+
+def drain(tree, flow):
     while flow.value is None:
-        window([flow])
-
-
-def window(flows, jobs=(), others=()):
-    flows = [f for f in flows if f.value is None]
-    jobs = [j for j in jobs if j.stages]
-    sent = [list(f.sends) for f in flows] + [j.send() for j in jobs]
-    sent, others = lax.optimization_barrier((sent, tuple(others)))
-    for f, got in zip(flows, sent):
-        f.take(list(got))
-    for j, got in zip(jobs, sent[len(flows):]):
-        j.add(list(got))
+        window(tree, [flow])
+
+
+def window(tree, works, others=(), later=()):
+    works = [w for w in works if w.wanted()]
+    later = [w for w in later if w.wanted()]
+    sent = [[tree.swap(*x) for x in w.wanted()] for w in works]
+    kept = [[x[0] for x in w.wanted()] for w in later]
+    sent, kept, others = lax.optimization_barrier((sent, kept, tuple(others)))
+    for w, arrays_in in zip(later, kept):
+        w.hold(list(arrays_in))
+    for w, got in zip(works, sent):
+        w.add(list(got))
     return others
 
 
@@ -632,30 +722,24 @@
     buckets = position_table.shape[0]
     scale = 1.0 / math.sqrt(3.0 * (d // HEADS))
     vectors = (query_bias, key_bias, value_bias, out_bias, attention_gain, attention_shift, down_bias, output_gain, output_shift)
-    small = jnp.concatenate([v[:, None] for v in vectors] + [up_bias.reshape(spread, rows).T], axis=1).astype(BF)
-    small = jnp.pad(small, ((0, 0), (0, 128 - small.shape[1])))
-    rest_cols = jnp.concatenate([value_weight.astype(BF), position_table.T.astype(BF), small], axis=1)
-    query_key = jnp.concatenate([query_weight.astype(BF), key_weight.astype(BF)], axis=1)
-    down_t = down_weight.T.astype(BF)
     cut = ff // 2
-    out_up = jnp.concatenate([out_weight.T.astype(BF), up_weight[:, :cut].astype(BF)], axis=1)
-    one = Flow(tree.gather([(query_key, False), (rest_cols, True)]))
-    two = Flow(tree.gather([(out_up, False), (down_t[:, :cut], True)]))
-    three = Flow(tree.gather([(up_weight[:, cut:].astype(BF), False), (down_t[:, cut:], True)]))
-
+    lead = pack_first(query_weight, key_weight, value_weight, position_table.T, vectors, up_bias.reshape(spread, rows))
+    one = Flow(tree.gather(lead, [(2 * d, False), (d + buckets + 128, True)], True))
     place = tree.place(False)
     place_t = tree.place(True)
     half = t // 2
     picked = lax.rev(rel_bucket[t - half : 2 * t - half], (0,))
     onehot = (picked[:, None] == lax.broadcasted_iota(jnp.int32, (t, buckets), 1)).astype(BF)
-    place, place_t, onehot = window([one], (), (place, place_t, onehot))
+    early, late = pack_second(out_weight.T, up_weight, down_weight.T)
+    early, late, place, place_t, onehot = window(tree, [one], (early, late, place, place_t, onehot))
+    two = Flow(tree.gather(early, [(d + cut, False), (cut, True)]))
     arrange = lambda m: mm(m, place, 1, 0).astype(BF)
     x_p = arrange(x)
-    (x_p,) = window([one, two], (), (x_p,))
+    late, x_p = window(tree, [one, two], (late, x_p))
     cot_p = arrange(cotangent[0])
-    (cot_p,) = window([one, two], (), (cot_p,))
-    window([one, three])
-    drain(one)
+    late, cot_p = window(tree, [one, two], (late, cot_p))
+    three = Flow(tree.gather(late, [(cut, False), (cut, True)]))
+    drain(tree, one)
     low, high = one.value
 
     small = jnp.concatenate([a[:, c + d + buckets : c + d + buckets + 128] for a, c in high], 0)
@@ -664,64 +748,80 @@
     bias = vec[:3].reshape(1, 3 * d)
     bu = vec[SPLIT : SPLIT + spread].reshape(spread, tree.n, rows).transpose(1, 0, 2).reshape(1, ff)
     q, k, v, ek, eq = project(x_p, onehot, low, high, bias, TILE)
-    q, k, v, ek, eq = window([two, three], (), (q, k, v, ek, eq))
     n_pairs = HEADS // 2
-    made = attend(q, k, v, ek, eq, seg, scale, None, 0, n_pairs // 2)
-    made = window([two, three], (), made)
-    made = attend(q, k, v, ek, eq, seg, scale, made, n_pairs // 2, n_pairs // 2)
-    context, probs = window([two, three], (), made)
-
-    drain(two)
+    plan = (
+        (0, n_pairs // 4, [two, three], []),
+        (n_pairs // 4, n_pairs * 5 // 8, [two, three], []),
+        (n_pairs * 5 // 8, n_pairs, [two, three], []),
+    )
+    made = None
+    for begin, after, works, later in plan:
+        made = attend(q, k, v, ek, eq, seg, scale, made, begin, after - begin)
+        made = window(tree, works, made, later)
+    context, probs = made
+
+    drain(tree, two)
     wo = two.value[0]
     shifted = lambda pieces, by: [(a, c + by) for a, c in pieces]
-    up_a, dn_a = shifted(wo, d), two.value[1]
-    count = cut // TILE
-    act_a, slope_a, n1, r1, mixed, mixed_low, so_far = feed_forward(vecs, bu, up_a, dn_a, 0, count, (context, x_p, wo))
-    (so_far,) = window([three], (), (so_far,))
-    drain(three)
-    up_b, dn_b = three.value
+    up_a, dn_early = shifted(wo, d), two.value[1]
+    count = cut // WIDE
+    act_a, slope_a, n1, r1, mixed, mixed_low, so_far = feed_forward(vecs, bu, up_a, dn_early, 0, count, (context, x_p, wo))
+    (so_far,) = window(tree, [three], (so_far,))
+    drain(tree, three)
+    up_b, dn_late = three.value
     act_b, slope_b, out_p, d_sum, d_ffn, sums2 = feed_forward(
-        vecs, bu, up_b, dn_b, count, count, (mixed, mixed_low, so_far), cot_p
+        vecs, bu, up_b, dn_late, count, count, (mixed, mixed_low, so_far), cot_p
     )
-    back = feed_back(tree, d_ffn, mixed_low, act_a, slope_a, up_a, dn_a, d_sum, count)
-    job_1 = Job(tree, *back[:5])
+    back = feed_back(tree, d_ffn, mixed_low, act_a, slope_a, up_a, dn_early, d_sum, count)
+    job_1 = Job(tree, back[0], (*back[1:3], False), (*back[3:5], True))
     d_bu_a, total = back[5:]
     back = feed_back(
-        tree, d_ffn, mixed_low, act_b, slope_b, up_b, dn_b, total, count, (context, wo, n1, r1, vecs[1:2])
+        tree, d_ffn, mixed_low, act_b, slope_b, up_b, dn_late, total, count, (context, wo, n1, r1, vecs[1:2])
     )
-    job_2 = Job(tree, *back[:5])
+    job_2 = Job(tree, back[0], (*back[1:3], False), (*back[3:5], True))
     d_bu_b, d_attn, d_rest, d_context, sums1 = back[5:]
-    (d_context,) = window([], [job_1], (d_context,))
+    (d_context,) = window(tree, [job_1], (d_context,))
 
     args = (q, k, v, ek, eq, d_context, probs, scale)
     grads = attend_back(*args, None, 0, n_pairs // 2)
-    grads = window([], [job_1, job_2], grads)
+    grads = window(tree, [job_1, job_2], grads)
+    split = attention_grads(tree, x_p, onehot, low, high, *grads, d // 2, 0)
+    (*grads, d_table, sums) = window(tree, [job_1], (*grads, *split[5:]))
+    job_3 = Job(tree, split[0], (*split[1:3], False), (*split[3:5], True))
     grads = attend_back(*args, grads, n_pairs // 2, n_pairs // 2)
-    dq, dk, dv, dek, deq = window([], [job_1, job_2], grads)
+    grads = window(tree, [job_2, job_3, job_1], grads)
     d_bu = jnp.concatenate([d_bu_a, d_bu_b], 1)
     lines = d_bu.reshape(tree.n, spread, rows).transpose(1, 0, 2).reshape(spread, d)
     ordered = jnp.concatenate([sums1[:3], sums2[:3]], 0)
     ordered = jnp.concatenate([ordered, jnp.zeros((2, d), F32)], 0)
-    split = attention_grads(tree, x_p, onehot, low, high, dq, dk, dv, dek, deq, lines, ordered, place_t, TILE)
-    split = window([], [job_1, job_2], split)
-    job_3 = Job(tree, *split)
-    d_attn, d_rest = window([], [job_3], (d_attn, d_rest))
+    carried = (d_table, sums, lines, ordered, place_t)
+    split = attention_grads(tree, x_p, onehot, low, high, *grads, d // 2, 1, carried)
+    split = window(tree, [job_3, job_1], split)
+    job_4 = Job(tree, split[0], (*split[1:3], False), (*split[3:5], True))
+    dq, dk, dv, _, _ = grads
+    d_attn, d_rest = window(tree, [job_4, job_2], (d_attn, d_rest))
     grad_layer = input_grads(d_attn, d_rest, low, high, dq, dk, dv, out_p, place_t, TILE)
-    input_grad, layer_out = window([], [job_1, job_2, job_3], grad_layer)
-    one, two, three = [job.run() for job in (job_1, job_2, job_3)]
+    input_grad, layer_out = window(tree, [job_4, job_3], grad_layer)
+    works = [job_4, job_3, job_2, job_1]
+    while any(w.stages for w in works):
+        window(tree, works)
+    four, three, two, one = [w.total for w in works]
+    h = d // 2
     up_a_grad, dn_a_grad = one[:, :cut], one[:, cut:]
     up_b_grad, out_grad, dn_b_grad = two[:, :cut], two[:, cut : cut + d], two[:, cut + d :]
-    rest_a, rest_b = three[:, : 2 * d], three[:, 2 * d :]
-    tail = rest_b[:, d + buckets :]
+    query_grad, key_grad, value_grad = [
+        jnp.concatenate([three[:, i * h : (i + 1) * h], four[:, i * h : (i + 1) * h]], 1) for i in range(3)
+    ]
+    table_grad, tail = four[:, 3 * h : 3 * h + buckets], four[:, 3 * h + buckets :]
     d_bq, d_bk, d_bv = [tail[:, i] for i in range(3)]
     d_up_bias = tail[:, 3 : 3 + spread].T.reshape(-1)
     d_bo, d_gain1, d_shift1, d_bd, d_gain2, d_shift2 = [tail[:, 16 + i] for i in range(6)]
     return (
         layer_out[None], input_grad[None],
-        rest_a[:, :d], d_bq, rest_a[:, d:], d_bk, rest_b[:, :d], d_bv,
+        query_grad, d_bq, key_grad, d_bk, value_grad, d_bv,
         out_grad.T, d_bo, d_gain1, d_shift1, jnp.concatenate([up_a_grad, up_b_grad], 1), d_up_bias,
         jnp.concatenate([dn_a_grad.T, dn_b_grad.T], 0), d_bd, d_gain2, d_shift2,
-        rest_b[:, d : d + buckets].T,
+        table_grad.T,
     )
 
 

time: 478 us -> 436 us (0.912)
  waiting for transfers between devices: 160 us -> 110 us
  Pallas kernels: 187 us -> 200 us
  other arithmetic: 48.6 us -> 39.4 us
  starting transfers between devices: 46.3 us -> 51.8 us
    ppermute x54 -> x62, waiting for transfers between devices: 160 us -> 110 us  [swap(): return lax.ppermute(a, axis, [(i, i ^ bit) for i in range(size)])]
    pallas_call x1 -> x9, Pallas kernels: 18.8 us -> 29.1 us  [the longest x2 22.9 us: attention_grads(): pl.pallas_call(kernel, grid=(3,), in_specs=specs, out_specs=[o[1] for o i...]
    convert_element_type x20 -> x26, other arithmetic: 22 us -> 28.1 us  [add(): sums = lambda a, g: (a.astype(F32) + g.astype(F32)).astype(BF)]
    unnamed x4 -> x0, other arithmetic: 6.1 us -> none
    broadcast_in_dim x9 -> x0, other arithmetic: 6 us -> none  [per_device(): v[:, None]]
    ppermute x54 -> x62, starting transfers between devices: 46.3 us -> 51.8 us  [swap(): return lax.ppermute(a, axis, [(i, i ^ bit) for i in range(size)])]
    pallas_call x2 -> x3, Pallas kernels: 34.9 us -> 36.8 us  [attend(): pl.pallas_call(lambda *r: attend_kernel(scale, *r[:7], *r[len(r) - 2:]),...]
  transfers between devices with their start and end apart: 54 -> 62, of which waited for: 22 -> 28; matrix products, arithmetic and copies ran while one was open for 9% -> 13% of each run, Pallas kernels for 33% -> 38%
where the time goes in v4:
time: 436 us; the launch traced here: 430 us
  Pallas kernels  200 us (46%)
  waiting for transfers between devices  110 us (25%)
  starting transfers between devices  51.8 us (12%)
  other arithmetic  39.4 us (9%)
  local copies, waits for them, and re-layouts  19.9 us (5%)
  matrix products  7.02 us (2%)
    ppermute x62, waiting for transfers between devices, swap(): return lax.ppermute(a, axis, [(i, i ^ bit) for i in range(size)])  110 us
    ppermute x62, starting transfers between devices, swap(): return lax.ppermute(a, axis, [(i, i ^ bit) for i in range(size)])  51.8 us
    pallas_call x2, Pallas kernels, feed_back(): pl.pallas_call(kernel, grid=(count,), in_specs=specs, out_specs=[o[1] for...  41.8 us
    pallas_call x3, Pallas kernels, attend(): pl.pallas_call(lambda *r: attend_kernel(scale, *r[:7], *r[len(r) - 2:]),...  36.8 us
    pallas_call x2, Pallas kernels, attend_back(): pl.pallas_call(lambda *r: attend_back_kernel(scale, *r[:7], *r[len(r) - 5...  35.2 us
    pallas_call x2, Pallas kernels, feed_forward(): pl.pallas_call(kernel, grid=(count,), in_specs=specs, out_specs=[o[1] for...  30.1 us
    convert_element_type x26, other arithmetic, add(): sums = lambda a, g: (a.astype(F32) + g.astype(F32)).astype(BF)  28.1 us
    pallas_call x2, Pallas kernels, attention_grads(): pl.pallas_call(kernel, grid=(3,), in_specs=specs, out_specs=[o[1] for o i...  22.9 us
  transfers between devices with their start and end apart: 62, of which 28 were waited for; matrix products, arithmetic and copies ran while one was open for 13% of the time, Pallas kernels for 38%

profile of v4, /device:TPU:0, one launch (start us, length us, event | category | flops | bytes accessed | tf_op | source)
XLA Modules:
  0.0 430.0 jit_solution(11708005957766479528)
XLA Ops:
  4.0 5.0 %collective-permute-start.2 = (bf16[32,3712]{1,0:T(8,128)(2,1)}, bf16[32,3712]{1,0:T(8,128)(2,1)S(1)}, u32[]{:S(2)}, u32[]{:S(2)}) collective-permute-start(bf16[32,3712]{1,0:T(8,128)(2,1)} %shard_map.348.refs_0_), channel_id=1, source_target_pairs={{0,24},{4,28},{8,16},{12,20},{16,8},{20,12},{24,0},{28,4},{1,25},{... | collective-permute-start | bytes 712712 | tf_op jit(solution)/shard_map/ppermute | solution.py:558
  16.0 13.5 %collective-permute-done.1.refs_1_ = bf16[32,3712]{1,0:T(8,128)(2,1)S(1)} collective-permute-done((bf16[32,3712]{1,0:T(8,128)(2,1)}, bf16[32,3712]{1,0:T(8,128)(2,1)S(1)}, u32[]{:S(2)}, u32[]{:S(2)}) %collective-permute-start.1) | collective-permute-done | bytes 237600 | tf_op jit(solution)/shard_map/ppermute | solution.py:558
  38.3 13.3 %collective-permute-done.6.refs_1_ = bf16[32,5120]{1,0:T(8,128)(2,1)S(1)} collective-permute-done((bf16[32,5120]{1,0:T(8,128)(2,1)S(1)}, bf16[32,5120]{1,0:T(8,128)(2,1)S(1)}, u32[]{:S(2)}, u32[]{:S(2)}) %collective-permute-start.6) | collective-permute-done | bytes 327712 | tf_op jit(solution)/shard_map/ppermute | solution.py:558
  61.3 9.9 %collective-permute-done.8.refs_11_.refs_19_.refs_18_ = bf16[128,1664]{1,0:T(8,128)(2,1)S(1)} collective-permute-done((bf16[128,1664]{1,0:T(8,128)(2,1)S(1)}, bf16[128,1664]{1,0:T(8,128)(2,1)S(1)}, u32[]{:S(2)}, u32[]{:S(2)}) %collective-permute-start.8) | collective-permute-done | bytes 426016 | tf_op jit(solution)/shard_map/ppermute | solution.py:558
  83.3 13.0 %shard_map.353 = (bf16[512,1024]{1,0:T(8,128)(2,1)}, bf16[512,1024]{1,0:T(8,128)(2,1)}, bf16[512,1024]{1,0:T(8,128)(2,1)}, bf16[512,1024]{1,0:T(8,128)(2,1)}, bf16[512,1024]{1,0:T(8,128)(2,1)}) custom-call(bf16[512,1024]{1,0:T(8,128)(2,1)} %fusion.2.x_ref.refs_1_.refs_0_, bf16[512,512]{1,0:T(8,128)(2,1)} %fusion.6.hot_ref.refs_1_, f32[1,3072]{1,0:T(1,128)} %bitcast.53, ...), custom_call_target="tpu_custom_call" | custom-call | flops 1000000000 | bytes 1000000 | tf_op jit(solution)/shard_map/pallas_call | solution.py:409
  96.4 9.6 %shard_map.354 = (bf16[512,1024]{1,0:T(8,128)(2,1)}, bf16[16,512,512]{2,1,0:T(8,128)(2,1)}) custom-call(bf16[512,1024]{1,0:T(8,128)(2,1)} %get-tuple-element.213.r_0_, bf16[512,1024]{1,0:T(8,128)(2,1)} %get-tuple-element.214.r_1_, bf16[512,1024]{1,0:T(8,128)(2,1)} %get-tuple-element.215.r_2_, bf16[512,1024]{1,0:T(8,128)(2,1)} %get-tuple-element.216.r_3_, ...), custom_call_target="tpu_custom_call" | custom-call | flops 1000000000 | bytes 1000000 | tf_op jit(solution)/shard_map/pallas_call | solution.py:41
  115.0 13.3 %shard_map.356 = (bf16[512,1024]{1,0:T(8,128)(2,1)}, bf16[16,512,512]{2,1,0:T(8,128)(2,1)}) custom-call(bf16[512,1024]{1,0:T(8,128)(2,1)} %get-tuple-element.213.r_0_, bf16[512,1024]{1,0:T(8,128)(2,1)} %get-tuple-element.214.r_1_, bf16[512,1024]{1,0:T(8,128)(2,1)} %get-tuple-element.215.r_2_, ...), custom_call_target="tpu_custom_call", output_to_operand_aliasing={{0}: (7, {}), {1}: (8, {})} | custom-call | flops 1000000000 | bytes 1000000 | tf_op jit(solution)/shard_map/pallas_call | solution.py:41
  132.1 13.9 %shard_map.358 = (bf16[512,1024]{1,0:T(8,128)(2,1)}, bf16[16,512,512]{2,1,0:T(8,128)(2,1)}) custom-call(bf16[512,1024]{1,0:T(8,128)(2,1)} %get-tuple-element.213.r_0_, bf16[512,1024]{1,0:T(8,128)(2,1)} %get-tuple-element.214.r_1_, bf16[512,1024]{1,0:T(8,128)(2,1)} %get-tuple-element.215.r_2_, ...), custom_call_target="tpu_custom_call", output_to_operand_aliasing={{0}: (7, {}), {1}: (8, {})} | custom-call | flops 1000000000 | bytes 1000000 | tf_op jit(solution)/shard_map/pallas_call | solution.py:41
  146.0 9.2 %collective-permute-done.26.refs_7_.refs_15_ = bf16[128,4096]{1,0:T(8,128)(2,1)} collective-permute-done((bf16[128,4096]{1,0:T(8,128)(2,1)S(1)}, bf16[128,4096]{1,0:T(8,128)(2,1)}, u32[]{:S(2)}, u32[]{:S(2)}) %collective-permute-start.26) | collective-permute-done | bytes 1048608 | tf_op jit(solution)/shard_map/ppermute | solution.py:558
  166.2 15.2 %shard_map.359 = (bf16[512,2048]{1,0:T(8,128)(2,1)}, bf16[512,2048]{1,0:T(8,128)(2,1)}, f32[512,1024]{1,0:T(8,128)}, f32[512,1]{1,0:T(8,128)}, f32[512,1024]{1,0...) custom-call(bf16[512,1024]{1,0:T(8,128)(2,1)} %get-tuple-element.234.refs_0_.refs_21_, ...), custom_call_target="tpu_custom_call" | custom-call | flops 1000000000 | bytes 1000000 | tf_op jit(solution)/shard_map/pallas_call | solution.py:242
  185.0 14.9 %shard_map.360 = (bf16[512,2048]{1,0:T(8,128)(2,1)}, bf16[512,2048]{1,0:T(8,128)(2,1)}, bf16[512,1024]{1,0:T(8,128)(2,1)}, f32[512,1024]{1,0:T(8,128)}, bf16[512,1024]{1,0:T(8,128)(2,1)}, /*index=5*/f32[8,1024]{1,0:T(8,128)}) custom-call(f32[512,1024]{1,0:T(8,128)} %get-tuple-element.240.refs_0_, bf16[512,1024]{1,0:T(8,128)(2,1)} %get-tuple-element.241.refs_1_, ...), custom_call_target="tpu_custom_call" | custom-call | flops 1000000000 | bytes 1000000 | tf_op jit(solution)/shard_map/pallas_call | solution.py:242
  199.9 18.1 %shard_map.361 = (bf16[512,4096]{1,0:T(8,128)(2,1)}, bf16[256,2048]{1,0:T(8,128)(2,1)}, bf16[256,2048]{1,0:T(8,128)(2,1)}, bf16[256,2048]{1,0:T(8,128)(2,1)}, bf...) custom-call(bf16[512,1024]{1,0:T(8,128)(2,1)} %get-tuple-element.254.refs_0_, ...), custom_call_target="tpu_custom_call" | custom-call | flops 1000000000 | bytes 1000000 | tf_op jit(solution)/shard_map/pallas_call | solution.py:326
  219.2 23.7 %shard_map.362 = (bf16[512,5120]{1,0:T(8,128)(2,1)}, bf16[256,3072]{1,0:T(8,128)(2,1)}, bf16[256,3072]{1,0:T(8,128)(2,1)}, bf16[256,2048]{1,0:T(8,128)(2,1)}, bf...) custom-call(bf16[512,1024]{1,0:T(8,128)(2,1)} %get-tuple-element.254, ...), custom_call_target="tpu_custom_call" | custom-call | flops 1000000000 | bytes 1000000 | tf_op jit(solution)/shard_map/pallas_call | solution.py:326
  243.4 6.8 %add_convert_fusion.4 = (bf16[256,2048]{1,0:T(8,128)(2,1)S(1)}, bf16[256,2048]{1,0:T(8,128)(2,1)S(1)}, bf16[256,2048]{1,0:T(8,128)(2,1)}, bf16[256,2048]{1,0:T(8,128)(2,1)}) fusion(bf16[256,2048]{1,0:T(8,128)(2,1)S(1)} %copy-done.32, bf16[512,4096]{1,0:T(8,128)(2,1)} %collective-permute-done.34, bf16[256,2048]{1,0:T(8,128)(2,1)} %get-tuple-element.288, ...), kind=kLoop, calls=%fused_computation.8 | loop fusion | flops 8388608 | bytes 12582912 | tf_op jit(solution)/shard_map/convert_element_type | solution.py:627
  251.3 17.5 %shard_map.363 = (bf16[512,1024]{1,0:T(8,128)(2,1)}, bf16[512,1024]{1,0:T(8,128)(2,1)}, bf16[512,1024]{1,0:T(8,128)(2,1)}, bf16[512,1024]{1,0:T(8,128)(2,1)}, bf16[512,1024]{1,0:T(8,128)(2,1)}) custom-call(bf16[512,1024]{1,0:T(8,128)(2,1)} %get-tuple-element.213.r_0_, bf16[512,1024]{1,0:T(8,128)(2,1)} %get-tuple-element.214.r_1_, ...), custom_call_target="tpu_custom_call" | custom-call | flops 1000000000 | bytes 1000000 | tf_op jit(solution)/shard_map/pallas_call | solution.py:93
  268.8 6.9 %collective-permute-done.36 = bf16[256,2048]{1,0:T(8,128)(2,1)} collective-permute-done((bf16[256,2048]{1,0:T(8,128)(2,1)}, bf16[256,2048]{1,0:T(8,128)(2,1)}, u32[]{:S(2)}, u32[]{:S(2)}) %collective-permute-start.36) | collective-permute-done | bytes 1048608 | tf_op jit(solution)/shard_map/ppermute | solution.py:558
  286.5 10.5 %shard_map.364 = (bf16[512,1536]{1,0:T(8,128)(2,1)}, bf16[256,1024]{1,0:T(8,128)(2,1)}, bf16[256,1024]{1,0:T(8,128)(2,1)}, bf16[256,512]{1,0:T(8,128)(2,1)}, bf1...) custom-call(bf16[512,1024]{1,0:T(8,128)(2,1)} %fusion.2.x_ref.refs_1_.refs_0_, ...), custom_call_target="tpu_custom_call" | custom-call | flops 1000000000 | bytes 1000000 | tf_op jit(solution)/shard_map/pallas_call | solution.py:490
  305.2 17.7 %shard_map.365 = (bf16[512,1024]{1,0:T(8,128)(2,1)}, bf16[512,1024]{1,0:T(8,128)(2,1)}, bf16[512,1024]{1,0:T(8,128)(2,1)}, bf16[512,1024]{1,0:T(8,128)(2,1)}, bf16[512,1024]{1,0:T(8,128)(2,1)}) custom-call(bf16[512,1024]{1,0:T(8,128)(2,1)} %get-tuple-element.213.r_0_, ...), custom_call_target="tpu_custom_call", output_to_operand_aliasing={{0}: (7, {}), {1}: (8, {}), {2}: (9, {}), {3}: (10, {}), {4... | custom-call | flops 1000000000 | bytes 1000000 | tf_op jit(solution)/shard_map/pallas_call | solution.py:93
  335.2 12.4 %shard_map.366 = (bf16[512,2176]{1,0:T(8,128)(2,1)}, bf16[256,1024]{1,0:T(8,128)(2,1)}, bf16[256,1024]{1,0:T(8,128)(2,1)}, bf16[256,1152]{1,0:T(8,128)(2,1)}, bf16[256,1152]{1,0:T(8,128)(2,1)}) custom-call(bf16[512,1024]{1,0:T(8,128)(2,1)} %fusion.2.x_ref.refs_1_.refs_0_, bf16[512,512]{1,0:T(8,128)(2,1)} %fusion.6.hot_ref.refs_1_, ...), custom_call_target="tpu_custom_call" | custom-call | flops 1000000000 | bytes 1000000 | tf_op jit(solution)/shard_map/pallas_call | solution.py:490
  355.9 10.8 %collective-permute-done.49 = bf16[128,2048]{1,0:T(8,128)(2,1)S(1)} collective-permute-done((bf16[128,2048]{1,0:T(8,128)(2,1)S(1)}, bf16[128,2048]{1,0:T(8,128)(2,1)S(1)}, u32[]{:S(2)}, u32[]{:S(2)}) %collective-permute-start.49) | collective-permute-done | bytes 524320 | tf_op jit(solution)/shard_map/ppermute | solution.py:558
  374.5 13.7 %shard_map.367 = (bf16[512,1024]{1,0:T(8,128)(2,1)}, bf16[512,1024]{1,0:T(8,128)(2,1)}) custom-call(bf16[512,1024]{1,0:T(8,128)(2,1)} %get-tuple-element.338.refs_0_, bf16[512,1024]{1,0:T(8,128)(2,1)} %get-tuple-element.339.refs_1_, bf16[512,1024]{1,0:T(8,128)(2,1)} %get-tuple-element.307.refs_2_, bf16[512,1024]{1,0:T(8,128)(2,1)} %get-tuple-element.308.refs_3_, ...), custom_call_target="tpu_custom_call" | custom-call | flops 1000000000 | bytes 1000000 | tf_op jit(solution)/shard_map/pallas_call | solution.py:528
  402.6 4.9 %collective-permute-done.59 = bf16[32,1536]{1,0:T(8,128)(2,1)S(1)} collective-permute-done((bf16[32,1536]{1,0:T(8,128)(2,1)S(1)}, bf16[32,1536]{1,0:T(8,128)(2,1)S(1)}, u32[]{:S(2)}, u32[]{:S(2)}) %collective-permute-start.59) | collective-permute-done | bytes 98336 | tf_op jit(solution)/shard_map/ppermute | solution.py:558
  411.7 5.8 %collective-permute-done.60 = bf16[32,5120]{1,0:T(8,128)(2,1)S(1)} collective-permute-done((bf16[32,5120]{1,0:T(8,128)(2,1)S(1)}, bf16[32,5120]{1,0:T(8,128)(2,1)S(1)}, u32[]{:S(2)}, u32[]{:S(2)}) %collective-permute-start.60) | collective-permute-done | bytes 327712 | tf_op jit(solution)/shard_map/ppermute | solution.py:558
  420.2 5.4 %collective-permute-done.61 = bf16[32,2176]{1,0:T(8,128)(2,1)S(1)} collective-permute-done((bf16[32,2176]{1,0:T(8,128)(2,1)S(1)}, bf16[32,2176]{1,0:T(8,128)(2,1)S(1)}, u32[]{:S(2)}, u32[]{:S(2)}) %collective-permute-start.61) | collective-permute-done | bytes 139296 | tf_op jit(solution)/shard_map/ppermute | solution.py:558
  (311 shorter events, 143.1 us)
Async XLA Ops:
  30.5 23.7 %collective-permute-start.4 = (bf16[128,3712]{1,0:T(8,128)(2,1)}, bf16[128,3712]{1,0:T(8,128)(2,1)S(1)}, u32[]{:S(2)}, u32[]{:S(2)}) collective-permute-start(bf16[128,3712]{1,0:T(8,128)(2,1)} %shard_map.350.refs_0_.refs_8_.refs_16_.refs_7_.refs_15_), channel_id=1, source_target_pairs={{0,2},{1,3},{2,0},{3,1},{4,6},{5,7},{6,4},{7,5},{8,10},{9,11},{10,... | collective-permute-start | bytes 2850824 | tf_op jit(solution)/shard_map/ppermute | solution.py:558
  32.0 23.4 %collective-permute-start.3 = (bf16[128,3712]{1,0:T(8,128)(2,1)}, bf16[128,3712]{1,0:T(8,128)(2,1)S(1)}, u32[]{:S(2)}, u32[]{:S(2)}) collective-permute-start(bf16[128,3712]{1,0:T(8,128)(2,1)} %shard_map.350.refs_0_.refs_8_.refs_16_.refs_7_.refs_15_), channel_id=1, source_target_pairs={{0,1},{1,0},{2,3},{3,2},{4,5},{5,4},{6,7},{7,6},{8,9},{9,8},{10,11... | collective-permute-start | bytes 2850824 | tf_op jit(solution)/shard_map/ppermute | solution.py:558
  75.4 30.6 %collective-permute-start.14 = (bf16[128,5120]{1,0:T(8,128)(2,1)S(1)}, bf16[128,5120]{1,0:T(8,128)(2,1)}, u32[]{:S(2)}, u32[]{:S(2)}) collective-permute-start(bf16[128,5120]{1,0:T(8,128)(2,1)S(1)} %shard_map.352.refs_2_.refs_12_.refs_20_.refs_5_.refs_13_.refs_25_), channel_id=1, source_target_pairs={{0,4},{4,0},{8,12},{12,8},{16,20},{20,16},{24,28},{28,24},{1,5},{5... | collective-permute-start | bytes 3932168 | tf_op jit(solution)/shard_map/ppermute | solution.py:558
  75.4 31.3 %collective-permute-start.13 = (bf16[128,5120]{1,0:T(8,128)(2,1)S(1)}, bf16[128,5120]{1,0:T(8,128)(2,1)}, u32[]{:S(2)}, u32[]{:S(2)}) collective-permute-start(bf16[128,5120]{1,0:T(8,128)(2,1)S(1)} %shard_map.352.refs_2_.refs_12_.refs_20_.refs_5_.refs_13_.refs_25_), channel_id=1, source_target_pairs={{0,2},{1,3},{2,0},{3,1},{4,6},{5,7},{6,4},{7,5},{8,10},{9,11},{10,... | collective-permute-start | bytes 3932168 | tf_op jit(solution)/shard_map/ppermute | solution.py:558
  77.0 31.0 %collective-permute-start.12 = (bf16[128,5120]{1,0:T(8,128)(2,1)S(1)}, bf16[128,5120]{1,0:T(8,128)(2,1)}, u32[]{:S(2)}, u32[]{:S(2)}) collective-permute-start(bf16[128,5120]{1,0:T(8,128)(2,1)S(1)} %shard_map.352.refs_2_.refs_12_.refs_20_.refs_5_.refs_13_.refs_25_), channel_id=1, source_target_pairs={{0,1},{1,0},{2,3},{3,2},{4,5},{5,4},{6,7},{7,6},{8,9},{9,8},{10,11... | collective-permute-start | bytes 3932168 | tf_op jit(solution)/shard_map/ppermute | solution.py:558
  80.3 25.7 %collective-permute-start.15 = (bf16[32,4096]{1,0:T(8,128)(2,1)}, bf16[32,4096]{1,0:T(8,128)(2,1)S(1)}, u32[]{:S(2)}, u32[]{:S(2)}) collective-permute-start(bf16[32,4096]{1,0:T(8,128)(2,1)} %get-tuple-element.205.refs_0_), channel_id=1, source_target_pairs={{0,16},{4,20},{8,24},{12,28},{16,0},{20,4},{24,8},{28,12},{1,17},{... | collective-permute-start | bytes 786440 | tf_op jit(solution)/shard_map/ppermute | solution.py:558
  129.5 25.7 %collective-permute-start.26 = (bf16[128,4096]{1,0:T(8,128)(2,1)S(1)}, bf16[128,4096]{1,0:T(8,128)(2,1)}, u32[]{:S(2)}, u32[]{:S(2)}) collective-permute-start(bf16[128,4096]{1,0:T(8,128)(2,1)S(1)} %shard_map.357.refs_5_.refs_13_), channel_id=1, source_target_pairs={{0,2},{1,3},{2,0},{3,1},{4,6},{5,7},{6,4},{7,5},{8,10},{9,11},{10,... | collective-permute-start | bytes 3145736 | tf_op jit(solution)/shard_map/ppermute | solution.py:558
  130.1 25.3 %collective-permute-start.25 = (bf16[128,4096]{1,0:T(8,128)(2,1)S(1)}, bf16[128,4096]{1,0:T(8,128)(2,1)}, u32[]{:S(2)}, u32[]{:S(2)}) collective-permute-start(bf16[128,4096]{1,0:T(8,128)(2,1)S(1)} %shard_map.357.refs_5_.refs_13_), channel_id=1, source_target_pairs={{0,1},{1,0},{2,3},{3,2},{4,5},{5,4},{6,7},{7,6},{8,9},{9,8},{10,11... | collective-permute-start | bytes 3145736 | tf_op jit(solution)/shard_map/ppermute | solution.py:558
  155.5 26.0 %collective-permute-start.30 = (bf16[128,4096]{1,0:T(8,128)(2,1)}, bf16[128,4096]{1,0:T(8,128)(2,1)S(1)}, u32[]{:S(2)}, u32[]{:S(2)}) collective-permute-start(bf16[128,4096]{1,0:T(8,128)(2,1)} %collective-permute-done.25.refs_6_.refs_14_), channel_id=1, source_target_pairs={{0,4},{4,0},{8,12},{12,8},{16,20},{20,16},{24,28},{28,24},{1,5},{5... | collective-permute-start | bytes 3145736 | tf_op jit(solution)/shard_map/ppermute | solution.py:558
  155.5 26.0 %collective-permute-start.31 = (bf16[128,4096]{1,0:T(8,128)(2,1)}, bf16[128,4096]{1,0:T(8,128)(2,1)S(1)}, u32[]{:S(2)}, u32[]{:S(2)}) collective-permute-start(bf16[128,4096]{1,0:T(8,128)(2,1)} %collective-permute-done.26.refs_7_.refs_15_), channel_id=1, source_target_pairs={{0,4},{4,0},{8,12},{12,8},{16,20},{20,16},{24,28},{28,24},{1,5},{5... | collective-permute-start | bytes 3145736 | tf_op jit(solution)/shard_map/ppermute | solution.py:558
  159.8 21.7 %collective-permute-start.29 = (bf16[128,2048]{1,0:T(8,128)(2,1)}, bf16[128,2048]{1,0:T(8,128)(2,1)S(1)}, u32[]{:S(2)}, u32[]{:S(2)}) collective-permute-start(bf16[128,2048]{1,0:T(8,128)(2,1)} %slice.445), channel_id=1, source_target_pairs={{0,1},{1,0},{2,3},{3,2},{4,5},{5,4},{6,7},{7,6},{8,9},{9,8},{10,11... | collective-permute-start | bytes 1572872 | tf_op jit(solution)/shard_map/ppermute | solution.py:558
  218.0 25.3 %collective-permute-start.34 = (bf16[512,4096]{1,0:T(8,128)(2,1)}, bf16[512,4096]{1,0:T(8,128)(2,1)}, u32[]{:S(2)}, u32[]{:S(2)}) collective-permute-start(bf16[512,4096]{1,0:T(8,128)(2,1)} %get-tuple-element.259), channel_id=1, source_target_pairs={{0,4},{4,0},{8,12},{12,8},{16,20},{20,16},{24,28},{28,24},{1,5},{5... | collective-permute-start | bytes 12582920 | tf_op jit(solution)/shard_map/ppermute | solution.py:558
  242.9 32.9 %collective-permute-start.37 = (bf16[512,5120]{1,0:T(8,128)(2,1)}, bf16[512,5120]{1,0:T(8,128)(2,1)}, u32[]{:S(2)}, u32[]{:S(2)}) collective-permute-start(bf16[512,5120]{1,0:T(8,128)(2,1)} %get-tuple-element.268), channel_id=1, source_target_pairs={{0,4},{4,0},{8,12},{12,8},{16,20},{20,16},{24,28},{28,24},{1,5},{5... | collective-permute-start | bytes 15728648 | tf_op jit(solution)/shard_map/ppermute | solution.py:558
  250.2 25.5 %collective-permute-start.36 = (bf16[256,2048]{1,0:T(8,128)(2,1)}, bf16[256,2048]{1,0:T(8,128)(2,1)}, u32[]{:S(2)}, u32[]{:S(2)}) collective-permute-start(bf16[256,2048]{1,0:T(8,128)(2,1)} %get-tuple-element.376), channel_id=1, source_target_pairs={{0,2},{1,3},{2,0},{3,1},{4,6},{5,7},{6,4},{7,5},{8,10},{9,11},{10,... | collective-permute-start | bytes 3145736 | tf_op jit(solution)/shard_map/ppermute | solution.py:558
  250.7 25.1 %collective-permute-start.35 = (bf16[256,2048]{1,0:T(8,128)(2,1)}, bf16[256,2048]{1,0:T(8,128)(2,1)S(1)}, u32[]{:S(2)}, u32[]{:S(2)}) collective-permute-start(bf16[256,2048]{1,0:T(8,128)(2,1)} %get-tuple-element.377), channel_id=1, source_target_pairs={{0,1},{1,0},{2,3},{3,2},{4,5},{5,4},{6,7},{7,6},{8,9},{9,8},{10,11... | collective-permute-start | bytes 3145736 | tf_op jit(solution)/shard_map/ppermute | solution.py:558
  277.4 23.6 %collective-permute-start.42 = (bf16[128,2048]{1,0:T(8,128)(2,1)S(1)}, bf16[128,2048]{1,0:T(8,128)(2,1)S(1)}, u32[]{:S(2)}, u32[]{:S(2)}) collective-permute-start(bf16[128,2048]{1,0:T(8,128)(2,1)S(1)} %get-tuple-element.388), channel_id=1, source_target_pairs={{0,1},{1,0},{2,3},{3,2},{4,5},{5,4},{6,7},{7,6},{8,9},{9,8},{10,11... | collective-permute-start | bytes 1572872 | tf_op jit(solution)/shard_map/ppermute | solution.py:558
  279.3 21.7 %collective-permute-start.41 = (bf16[128,2048]{1,0:T(8,128)(2,1)}, bf16[128,2048]{1,0:T(8,128)(2,1)}, u32[]{:S(2)}, u32[]{:S(2)}) collective-permute-start(bf16[128,2048]{1,0:T(8,128)(2,1)} %get-tuple-element.387), channel_id=1, source_target_pairs={{0,2},{1,3},{2,0},{3,1},{4,6},{5,7},{6,4},{7,5},{8,10},{9,11},{10,... | collective-permute-start | bytes 1572872 | tf_op jit(solution)/shard_map/ppermute | solution.py:558
  285.0 41.4 %collective-permute-start.38 = (bf16[256,3072]{1,0:T(8,128)(2,1)}, bf16[256,3072]{1,0:T(8,128)(2,1)}, u32[]{:S(2)}, u32[]{:S(2)}) collective-permute-start(bf16[256,3072]{1,0:T(8,128)(2,1)} %get-tuple-element.373), channel_id=1, source_target_pairs={{0,1},{1,0},{2,3},{3,2},{4,5},{5,4},{6,7},{7,6},{8,9},{9,8},{10,11... | collective-permute-start | bytes 4718600 | tf_op jit(solution)/shard_map/ppermute | solution.py:558
  297.0 29.4 %collective-permute-start.40 = (bf16[512,1536]{1,0:T(8,128)(2,1)}, bf16[512,1536]{1,0:T(8,128)(2,1)}, u32[]{:S(2)}, u32[]{:S(2)}) collective-permute-start(bf16[512,1536]{1,0:T(8,128)(2,1)} %get-tuple-element.285), channel_id=1, source_target_pairs={{0,4},{4,0},{8,12},{12,8},{16,20},{20,16},{24,28},{28,24},{1,5},{5... | collective-permute-start | bytes 4718600 | tf_op jit(solution)/shard_map/ppermute | solution.py:558
  300.5 25.9 %collective-permute-start.39 = (bf16[256,2048]{1,0:T(8,128)(2,1)}, bf16[256,2048]{1,0:T(8,128)(2,1)}, u32[]{:S(2)}, u32[]{:S(2)}) collective-permute-start(bf16[256,2048]{1,0:T(8,128)(2,1)} %get-tuple-element.371), channel_id=1, source_target_pairs={{0,2},{1,3},{2,0},{3,1},{4,6},{5,7},{6,4},{7,5},{8,10},{9,11},{10,... | collective-permute-start | bytes 3145736 | tf_op jit(solution)/shard_map/ppermute | solution.py:558
  303.4 23.0 %collective-permute-start.43 = (bf16[64,4096]{1,0:T(8,128)(2,1)}, bf16[64,4096]{1,0:T(8,128)(2,1)}, u32[]{:S(2)}, u32[]{:S(2)}) collective-permute-start(bf16[64,4096]{1,0:T(8,128)(2,1)} %pad_maximum_fusion.1), channel_id=1, source_target_pairs={{0,8},{4,12},{8,0},{12,4},{16,24},{20,28},{24,16},{28,20},{1,9},{5... | collective-permute-start | bytes 1572872 | tf_op jit(solution)/shard_map/ppermute | solution.py:558
  347.6 22.4 %collective-permute-start.47 = (bf16[512,2176]{1,0:T(8,128)(2,1)}, bf16[512,2176]{1,0:T(8,128)(2,1)S(1)}, u32[]{:S(2)}, u32[]{:S(2)}) collective-permute-start(bf16[512,2176]{1,0:T(8,128)(2,1)} %get-tuple-element.325), channel_id=1, source_target_pairs={{0,4},{4,0},{8,12},{12,8},{16,20},{20,16},{24,28},{28,24},{1,5},{5... | collective-permute-start | bytes 6684680 | tf_op jit(solution)/shard_map/ppermute | solution.py:558
  353.0 35.2 %collective-permute-start.53 = (bf16[128,512]{1,0:T(8,128)(2,1)S(1)}, bf16[128,512]{1,0:T(8,128)(2,1)S(1)}, u32[]{:S(2)}, u32[]{:S(2)}) collective-permute-start(bf16[128,512]{1,0:T(8,128)(2,1)S(1)} %get-tuple-element.419), channel_id=1, source_target_pairs={{0,1},{1,0},{2,3},{3,2},{4,5},{5,4},{6,7},{7,6},{8,9},{9,8},{10,11... | collective-permute-start | bytes 393224 | tf_op jit(solution)/shard_map/ppermute | solution.py:558
  354.3 33.9 %collective-permute-start.52 = (bf16[128,1024]{1,0:T(8,128)(2,1)S(1)}, bf16[128,1024]{1,0:T(8,128)(2,1)S(1)}, u32[]{:S(2)}, u32[]{:S(2)}) collective-permute-start(bf16[128,1024]{1,0:T(8,128)(2,1)S(1)} %get-tuple-element.403), channel_id=1, source_target_pairs={{0,2},{1,3},{2,0},{3,1},{4,6},{5,7},{6,4},{7,5},{8,10},{9,11},{10,... | collective-permute-start | bytes 786440 | tf_op jit(solution)/shard_map/ppermute | solution.py:558
  (88 other events, 1023.0 us)

commit v5 on v4

--- a/solution.py
+++ b/solution.py
@@ -354,21 +354,20 @@
     )(query, key, value, table, *[v.reshape(1, rows) for v in vectors], up_bias)
 
 
-def pack_second(out_weight, up, down):
+def pack_second(out_weight, up, down, cut):
     rows, ff = up.shape
     d = out_weight.shape[1]
-    cut = ff // 2
 
     def kernel(o_ref, u_ref, d_ref, a_ref, b_ref):
         down_t = d_ref[...].astype(BF)
         a_ref[:, 0:d] = o_ref[...].astype(BF)
         a_ref[:, d : d + cut] = u_ref[:, 0:cut].astype(BF)
         a_ref[:, d + cut : d + 2 * cut] = down_t[:, 0:cut]
-        b_ref[:, 0:cut] = u_ref[:, cut:ff].astype(BF)
-        b_ref[:, cut : 2 * cut] = down_t[:, cut:ff]
-
-    return pl.pallas_call(
-        kernel, out_shape=[jax.ShapeDtypeStruct((rows, d + 2 * cut), BF), jax.ShapeDtypeStruct((rows, 2 * cut), BF)],
+        b_ref[:, 0 : ff - cut] = u_ref[:, cut:ff].astype(BF)
+        b_ref[:, ff - cut : 2 * (ff - cut)] = down_t[:, cut:ff]
+
+    return pl.pallas_call(
+        kernel, out_shape=[jax.ShapeDtypeStruct((rows, d + 2 * cut), BF), jax.ShapeDtypeStruct((rows, 2 * (ff - cut)), BF)],
         cost_estimate=COST, compiler_params=pltpu.CompilerParams(vmem_limit_bytes=60 * 2**20),
     )(out_weight, up, down)
 
@@ -577,29 +576,25 @@
                 cur = join([cur, got])
         found = [{0: (cur, c)} for c in columns[:-1]]
         orders = [self.f_bits[::-1] if flipped else self.f_bits for _, flipped in sides]
-
-        def keep(keys, array, whole_row):
-            for s, i in keys:
-                found[s][i] = (array, columns[s] if whole_row else 0)
-
         every = range(len(sides))
+        pending = [([(s, 0) for s in every], True, cur)]
+        yield found, pending, columns
         sends = [([(s, bit) for s in every], True, (cur, "fsdp", bit)) for bit in self.f_bits]
-        cores = [([(s, self.nf) for s in every], True, (cur, "dp", 1))]
-        while sends or cores:
-            got = yield [x for _, _, x in sends + cores]
-            for (keys, whole_row, _), g in zip(sends + cores, got):
-                keep(keys, g, whole_row)
-            arrived, sends, cores = sends, [], []
+        while sends:
+            got = yield [x for _, _, x in sends]
+            arrived, sends = sends, []
+            for (keys, whole_row, _), g in zip(arrived, got):
+                for s, i in keys:
+                    found[s][i] = (g, columns[s] if whole_row else 0)
+                pending.append((keys, whole_row, g))
             for keys, whole_row, _ in arrived:
                 i = keys[0][1]
-                cores.append(([(s, self.nf + i) for s, _ in keys], whole_row, (found[keys[0][0]][i][0], "dp", 1)))
                 for s, _ in keys:
                     array, column = found[s][i]
                     last = max(at for at, bit in enumerate(orders[s]) if i & bit)
                     for bit in orders[s][last + 1 :]:
                         part = array[:, column : column + columns[s + 1] - columns[s]]
                         sends.append(([(s, i | bit)], False, (part, "fsdp", bit)))
-        return [[f[i] for i in range(2 * self.nf)] for f in found]
 
 
 class Job:
@@ -624,18 +619,20 @@
     def add(self, got):
         stage = self.stages.pop(0)
         more = bool(self.stages)
-        sums = lambda a, g: (a.astype(F32) + g.astype(F32)).astype(BF)
+        total = lambda *xs: sum(x.astype(F32) for x in xs)
+        sums = lambda *xs: total(*xs).astype(BF)
         if stage == "core":
             column = 0
             for side in self.sides:
-                r, n = side[0].shape
-                side[0] = sums(side[0], got[0][:r, column : column + n])
+                r, n = side[1].shape
+                side[0] = [side[0], got[0][:r, column : column + n]]
                 side[1] = sums(side[1], got[0][r:, column : column + n])
                 column += n
         elif isinstance(stage, int):
             for side, g in zip(self.sides, got):
-                r = side[0].shape[0] // 2
-                side[0], side[1] = sums(side[0][:r], g[:r]), sums(side[0][r:], g[r:])
+                known = side[0] if isinstance(side[0], list) else [side[0]]
+                r = g.shape[0] // 2
+                side[0], side[1] = sums(*[a[:r] for a in known], g[:r]), sums(*[a[r:] for a in known], g[r:])
             if not isinstance(self.stages[0], int):
                 cat = lambda xs: xs[0] if len(xs) == 1 else jnp.concatenate(xs, 1)
                 self.total = [cat([side[i] for side in self.sides]) for i in range(2)]
@@ -659,39 +656,76 @@
 
 
 class Flow:
-    def __init__(self, steps):
-        self.steps = steps
-        self.value = None
-        self.sends = next(steps)
+    def __init__(self, tree, cur, sides, direct=False):
+        self.tree = tree
+        self.steps = tree.gather(cur, sides, direct)
+        self.found = None
+        self.linked = False
+        self.next(None)
+
+    def next(self, got):
+        try:
+            out = self.steps.send(got)
+            if isinstance(out, tuple):
+                self.found, self.pending, self.columns = out
+                out = self.steps.send(None)
+            self.sends = out
+        except StopIteration:
+            self.sends, self.linked = [], True
 
     def wanted(self):
         return list(self.sends)
 
     def add(self, got):
-        try:
-            self.sends = self.steps.send(got)
-        except StopIteration as end:
-            self.sends, self.value = [], end.value
+        self.next(got)
 
     def hold(self, arrays):
         self.sends = [(a,) + rest[1:] for a, rest in zip(arrays, self.sends)]
 
-
-class Pair:
-    def __init__(self, *arrays):
-        self.arrays = arrays
-        self.value = None
+    def cores(self, most):
+        return Cores(self, most)
+
+    def rest(self):
+        return Rest(self)
+
+    @property
+    def value(self):
+        nf = self.tree.nf
+        if not self.linked or any(len(f) < 2 * nf for f in self.found):
+            return None
+        return [[f[i] for i in range(2 * nf)] for f in self.found]
+
+
+class Rest:
+    def __init__(self, flow):
+        self.flow = flow
 
     def wanted(self):
-        return [] if self.value is not None else [(a, "dp", 1) for a in self.arrays]
+        return [] if self.flow.found is None else [(array, "dp", 1) for _, _, array in self.flow.pending]
+
+    def hold(self, arrays):
+        self.flow.pending[:] = [p[:2] + (a,) for p, a in zip(self.flow.pending, arrays)]
+
+
+class Cores:
+    def __init__(self, flow, most):
+        self.flow = flow
+        self.taken = [] if flow.found is None else flow.pending[:most]
+        if self.taken:
+            del flow.pending[: len(self.taken)]
+
+    def wanted(self):
+        return [(array, "dp", 1) for _, _, array in self.taken]
 
     def add(self, got):
-        self.value = got
+        for (keys, whole_row, _), g in zip(self.taken, got):
+            for s, i in keys:
+                self.flow.found[s][self.flow.tree.nf + i] = (g, self.flow.columns[s] if whole_row else 0)
 
 
 def drain(tree, flow):
     while flow.value is None:
-        window(tree, [flow])
+        window(tree, [flow, flow.cores(5)])
 
 
 def window(tree, works, others=(), later=()):
@@ -722,41 +756,47 @@
     buckets = position_table.shape[0]
     scale = 1.0 / math.sqrt(3.0 * (d // HEADS))
     vectors = (query_bias, key_bias, value_bias, out_bias, attention_gain, attention_shift, down_bias, output_gain, output_shift)
-    cut = ff // 2
+    cut = ff * 5 // 8
+    late_cut = ff - cut
     lead = pack_first(query_weight, key_weight, value_weight, position_table.T, vectors, up_bias.reshape(spread, rows))
-    one = Flow(tree.gather(lead, [(2 * d, False), (d + buckets + 128, True)], True))
+    one = Flow(tree, lead, [(2 * d, False), (d + buckets + 128, True)], True)
     place = tree.place(False)
     place_t = tree.place(True)
     half = t // 2
     picked = lax.rev(rel_bucket[t - half : 2 * t - half], (0,))
     onehot = (picked[:, None] == lax.broadcasted_iota(jnp.int32, (t, buckets), 1)).astype(BF)
-    early, late = pack_second(out_weight.T, up_weight, down_weight.T)
+    early, late = pack_second(out_weight.T, up_weight, down_weight.T, cut)
     early, late, place, place_t, onehot = window(tree, [one], (early, late, place, place_t, onehot))
-    two = Flow(tree.gather(early, [(d + cut, False), (cut, True)]))
+    two = Flow(tree, early, [(d + cut, False), (cut, True)])
     arrange = lambda m: mm(m, place, 1, 0).astype(BF)
     x_p = arrange(x)
-    late, x_p = window(tree, [one, two], (late, x_p))
+    late, x_p = window(tree, [one, one.cores(1), two], (late, x_p))
+    three = Flow(tree, late, [(late_cut, False), (late_cut, True)])
     cot_p = arrange(cotangent[0])
-    late, cot_p = window(tree, [one, two], (late, cot_p))
-    three = Flow(tree.gather(late, [(cut, False), (cut, True)]))
+    (cot_p,) = window(tree, [one, one.cores(1), two], (cot_p,))
+    window(tree, [one, one.cores(3)], (), [two.rest()])
     drain(tree, one)
     low, high = one.value
 
     small = jnp.concatenate([a[:, c + d + buckets : c + d + buckets + 128] for a, c in high], 0)
     vec = mm(small, place, 0, 1)
-    vecs = small.T[3:11].astype(F32)
+    same = (lax.broadcasted_iota(jnp.int32, (d, d), 0) == lax.broadcasted_iota(jnp.int32, (d, d), 1)).astype(BF)
+    vecs = mm(small[:, 3:11], same, 0, 0)
     bias = vec[:3].reshape(1, 3 * d)
     bu = vec[SPLIT : SPLIT + spread].reshape(spread, tree.n, rows).transpose(1, 0, 2).reshape(1, ff)
     q, k, v, ek, eq = project(x_p, onehot, low, high, bias, TILE)
+    q, k, v, ek, eq, vecs, bu = window(tree, [three], (q, k, v, ek, eq, vecs, bu), [two.rest()])
     n_pairs = HEADS // 2
-    plan = (
-        (0, n_pairs // 4, [two, three], []),
-        (n_pairs // 4, n_pairs * 5 // 8, [two, three], []),
-        (n_pairs * 5 // 8, n_pairs, [two, three], []),
+    cuts = (0, n_pairs // 8, n_pairs // 2, n_pairs)
+    plans = (
+        lambda: ([two, two.cores(1), three], [two.rest()]),
+        lambda: ([two, two.cores(1)], [two.rest(), three.rest()]),
+        lambda: ([two.cores(3), three], [three.rest()]),
     )
     made = None
-    for begin, after, works, later in plan:
+    for begin, after, plan in zip(cuts, cuts[1:], plans):
         made = attend(q, k, v, ek, eq, seg, scale, made, begin, after - begin)
+        works, later = plan()
         made = window(tree, works, made, later)
     context, probs = made
 
@@ -764,51 +804,51 @@
     wo = two.value[0]
     shifted = lambda pieces, by: [(a, c + by) for a, c in pieces]
     up_a, dn_early = shifted(wo, d), two.value[1]
-    count = cut // WIDE
+    count, late_count = cut // WIDE, late_cut // WIDE
     act_a, slope_a, n1, r1, mixed, mixed_low, so_far = feed_forward(vecs, bu, up_a, dn_early, 0, count, (context, x_p, wo))
-    (so_far,) = window(tree, [three], (so_far,))
+    (so_far,) = window(tree, [three, three.cores(3)], (so_far,))
     drain(tree, three)
     up_b, dn_late = three.value
     act_b, slope_b, out_p, d_sum, d_ffn, sums2 = feed_forward(
-        vecs, bu, up_b, dn_late, count, count, (mixed, mixed_low, so_far), cot_p
+        vecs, bu, up_b, dn_late, count, late_count, (mixed, mixed_low, so_far), cot_p
     )
     back = feed_back(tree, d_ffn, mixed_low, act_a, slope_a, up_a, dn_early, d_sum, count)
     job_1 = Job(tree, back[0], (*back[1:3], False), (*back[3:5], True))
     d_bu_a, total = back[5:]
     back = feed_back(
-        tree, d_ffn, mixed_low, act_b, slope_b, up_b, dn_late, total, count, (context, wo, n1, r1, vecs[1:2])
+        tree, d_ffn, mixed_low, act_b, slope_b, up_b, dn_late, total, late_count, (context, wo, n1, r1, vecs[1:2])
     )
     job_2 = Job(tree, back[0], (*back[1:3], False), (*back[3:5], True))
     d_bu_b, d_attn, d_rest, d_context, sums1 = back[5:]
     (d_context,) = window(tree, [job_1], (d_context,))
 
     args = (q, k, v, ek, eq, d_context, probs, scale)
-    grads = attend_back(*args, None, 0, n_pairs // 2)
+    grads = attend_back(*args, None, 0, n_pairs * 3 // 4)
     grads = window(tree, [job_1, job_2], grads)
     split = attention_grads(tree, x_p, onehot, low, high, *grads, d // 2, 0)
     (*grads, d_table, sums) = window(tree, [job_1], (*grads, *split[5:]))
     job_3 = Job(tree, split[0], (*split[1:3], False), (*split[3:5], True))
-    grads = attend_back(*args, grads, n_pairs // 2, n_pairs // 2)
-    grads = window(tree, [job_2, job_3, job_1], grads)
+    grads = attend_back(*args, grads, n_pairs * 3 // 4, n_pairs // 4)
+    grads = window(tree, [job_3, job_1], grads)
     d_bu = jnp.concatenate([d_bu_a, d_bu_b], 1)
     lines = d_bu.reshape(tree.n, spread, rows).transpose(1, 0, 2).reshape(spread, d)
     ordered = jnp.concatenate([sums1[:3], sums2[:3]], 0)
     ordered = jnp.concatenate([ordered, jnp.zeros((2, d), F32)], 0)
     carried = (d_table, sums, lines, ordered, place_t)
     split = attention_grads(tree, x_p, onehot, low, high, *grads, d // 2, 1, carried)
-    split = window(tree, [job_3, job_1], split)
+    split = window(tree, [job_2, job_1], split)
     job_4 = Job(tree, split[0], (*split[1:3], False), (*split[3:5], True))
     dq, dk, dv, _, _ = grads
     d_attn, d_rest = window(tree, [job_4, job_2], (d_attn, d_rest))
     grad_layer = input_grads(d_attn, d_rest, low, high, dq, dk, dv, out_p, place_t, TILE)
-    input_grad, layer_out = window(tree, [job_4, job_3], grad_layer)
+    input_grad, layer_out = window(tree, [job_4, job_3, job_2], grad_layer)
     works = [job_4, job_3, job_2, job_1]
     while any(w.stages for w in works):
         window(tree, works)
     four, three, two, one = [w.total for w in works]
     h = d // 2
     up_a_grad, dn_a_grad = one[:, :cut], one[:, cut:]
-    up_b_grad, out_grad, dn_b_grad = two[:, :cut], two[:, cut : cut + d], two[:, cut + d :]
+    up_b_grad, out_grad, dn_b_grad = two[:, :late_cut], two[:, late_cut : late_cut + d], two[:, late_cut + d :]
     query_grad, key_grad, value_grad = [
         jnp.concatenate([three[:, i * h : (i + 1) * h], four[:, i * h : (i + 1) * h]], 1) for i in range(3)
     ]

time: 436 us -> 421 us (0.966)
  other arithmetic: 39.4 us -> 29.9 us
  waiting for transfers between devices: 110 us -> 105 us
    convert_element_type x27 -> x25, other arithmetic: 29.2 us -> 20.5 us  [add(): sums = lambda *xs: total(*xs).astype(BF)]
    ppermute x62, waiting for transfers between devices: 110 us -> 105 us  [swap(): return lax.ppermute(a, axis, [(i, i ^ bit) for i in range(size)])]
  transfers between devices with their start and end apart: 62 -> 62, of which waited for: 28 -> 26; matrix products, arithmetic and copies ran while one was open for 13% -> 10% of each run, Pallas kernels for 38% -> 39%
where the time goes in v5:
time: 421 us; the launch traced here: 415 us
  Pallas kernels  198 us (47%)
  waiting for transfers between devices  105 us (25%)
  starting transfers between devices  55.1 us (13%)
  other arithmetic  29.9 us (7%)
  local copies, waits for them, and re-layouts  18.7 us (4%)
  matrix products  6.37 us (2%)
    ppermute x62, waiting for transfers between devices, swap(): return lax.ppermute(a, axis, [(i, i ^ bit) for i in range(size)])  105 us
    ppermute x62, starting transfers between devices, swap(): return lax.ppermute(a, axis, [(i, i ^ bit) for i in range(size)])  55.1 us
    pallas_call x2, Pallas kernels, feed_back(): pl.pallas_call(kernel, grid=(count,), in_specs=specs, out_specs=[o[1] for...  42 us
    pallas_call x3, Pallas kernels, attend(): pl.pallas_call(lambda *r: attend_kernel(scale, *r[:7], *r[len(r) - 2:]),...  36.9 us
    pallas_call x2, Pallas kernels, attend_back(): pl.pallas_call(lambda *r: attend_back_kernel(scale, *r[:7], *r[len(r) - 5...  35.2 us
    pallas_call x2, Pallas kernels, feed_forward(): pl.pallas_call(kernel, grid=(count,), in_specs=specs, out_specs=[o[1] for...  30.3 us
    pallas_call x2, Pallas kernels, attention_grads(): pl.pallas_call(kernel, grid=(3,), in_specs=specs, out_specs=[o[1] for o i...  23 us
    convert_element_type x25, other arithmetic, add(): sums = lambda *xs: total(*xs).astype(BF)  20.5 us
  transfers between devices with their start and end apart: 62, of which 26 were waited for; matrix products, arithmetic and copies ran while one was open for 10% of the time, Pallas kernels for 39%

profile of v5, /device:TPU:0, one launch (start us, length us, event | category | flops | bytes accessed | tf_op | source)
XLA Modules:
  0.0 414.8 jit_solution(12935744839397363444)
XLA Ops:
  4.0 5.0 %collective-permute-start.2 = (bf16[32,3712]{1,0:T(8,128)(2,1)}, bf16[32,3712]{1,0:T(8,128)(2,1)S(1)}, u32[]{:S(2)}, u32[]{:S(2)}) collective-permute-start(bf16[32,3712]{1,0:T(8,128)(2,1)} %shard_map.348.refs_0_), channel_id=1, source_target_pairs={{0,24},{4,28},{8,16},{12,20},{16,8},{20,12},{24,0},{28,4},{1,25},{... | collective-permute-start | bytes 712712 | tf_op jit(solution)/shard_map/ppermute | solution.py:557
  16.0 13.5 %collective-permute-done.1.refs_1_ = bf16[32,3712]{1,0:T(8,128)(2,1)S(1)} collective-permute-done((bf16[32,3712]{1,0:T(8,128)(2,1)}, bf16[32,3712]{1,0:T(8,128)(2,1)S(1)}, u32[]{:S(2)}, u32[]{:S(2)}) %collective-permute-start.1) | collective-permute-done | bytes 237600 | tf_op jit(solution)/shard_map/ppermute | solution.py:557
  35.0 17.8 %collective-permute-done.6.refs_1_ = bf16[32,6144]{1,0:T(8,128)(2,1)S(1)} collective-permute-done((bf16[32,6144]{1,0:T(8,128)(2,1)S(1)}, bf16[32,6144]{1,0:T(8,128)(2,1)S(1)}, u32[]{:S(2)}, u32[]{:S(2)}) %collective-permute-start.6) | collective-permute-done | bytes 393248 | tf_op jit(solution)/shard_map/ppermute | solution.py:557
  59.3 10.5 %collective-permute-done.8.refs_11_.refs_19_.refs_18_ = bf16[128,1664]{1,0:T(8,128)(2,1)S(1)} collective-permute-done((bf16[128,1664]{1,0:T(8,128)(2,1)S(1)}, bf16[128,1664]{1,0:T(8,128)(2,1)S(1)}, u32[]{:S(2)}, u32[]{:S(2)}) %collective-permute-start.8) | collective-permute-done | bytes 426016 | tf_op jit(solution)/shard_map/ppermute | solution.py:557
  80.1 13.0 %shard_map.353 = (bf16[512,1024]{1,0:T(8,128)(2,1)}, bf16[512,1024]{1,0:T(8,128)(2,1)}, bf16[512,1024]{1,0:T(8,128)(2,1)}, bf16[512,1024]{1,0:T(8,128)(2,1)}, bf16[512,1024]{1,0:T(8,128)(2,1)}) custom-call(bf16[512,1024]{1,0:T(8,128)(2,1)} %fusion.3.x_ref.refs_1_.refs_0_, bf16[512,512]{1,0:T(8,128)(2,1)} %fusion.7.hot_ref.refs_1_, f32[1,3072]{1,0:T(1,128)} %bitcast.51, ...), custom_call_target="tpu_custom_call" | custom-call | flops 1000000000 | bytes 1000000 | tf_op jit(solution)/shard_map/pallas_call | solution.py:408
  95.8 5.6 %shard_map.355 = (bf16[512,1024]{1,0:T(8,128)(2,1)}, bf16[16,512,512]{2,1,0:T(8,128)(2,1)}) custom-call(bf16[512,1024]{1,0:T(8,128)(2,1)} %get-tuple-element.232.r_0_, bf16[512,1024]{1,0:T(8,128)(2,1)} %get-tuple-element.233.r_1_, bf16[512,1024]{1,0:T(8,128)(2,1)} %get-tuple-element.234.r_2_, bf16[512,1024]{1,0:T(8,128)(2,1)} %get-tuple-element.235.r_3_, ...), custom_call_target="tpu_custom_call" | custom-call | flops 1000000000 | bytes 1000000 | tf_op jit(solution)/shard_map/pallas_call | solution.py:41
  101.4 4.5 %collective-permute-done.18.refs_1_ = bf16[64,3072]{1,0:T(8,128)(2,1)S(1)} collective-permute-done((bf16[64,3072]{1,0:T(8,128)(2,1)S(1)}, bf16[64,3072]{1,0:T(8,128)(2,1)S(1)}, u32[]{:S(2)}, u32[]{:S(2)}) %collective-permute-start.18) | collective-permute-done | bytes 393248 | tf_op jit(solution)/shard_map/ppermute | solution.py:557
  105.9 5.7 %collective-permute-done.12.refs_4_.refs_14_.refs_22_.refs_7_.refs_15_.refs_27_ = bf16[128,6144]{1,0:T(8,128)(2,1)} collective-permute-done((bf16[128,6144]{1,0:T(8,128)(2,1)S(1)}, bf16[128,6144]{1,0:T(8,128)(2,1)}, u32[]{:S(2)}, u32[]{:S(2)}) %collective-permute-start.12) | collective-permute-done | bytes 1572896 | tf_op jit(solution)/shard_map/ppermute | solution.py:557
  119.1 13.6 %shard_map.357 = (bf16[512,1024]{1,0:T(8,128)(2,1)}, bf16[16,512,512]{2,1,0:T(8,128)(2,1)}) custom-call(bf16[512,1024]{1,0:T(8,128)(2,1)} %get-tuple-element.232.r_0_, bf16[512,1024]{1,0:T(8,128)(2,1)} %get-tuple-element.233.r_1_, bf16[512,1024]{1,0:T(8,128)(2,1)} %get-tuple-element.234.r_2_, ...), custom_call_target="tpu_custom_call", output_to_operand_aliasing={{0}: (7, {}), {1}: (8, {})} | custom-call | flops 1000000000 | bytes 1000000 | tf_op jit(solution)/shard_map/pallas_call | solution.py:41
  140.7 17.7 %shard_map.358 = (bf16[512,1024]{1,0:T(8,128)(2,1)}, bf16[16,512,512]{2,1,0:T(8,128)(2,1)}) custom-call(bf16[512,1024]{1,0:T(8,128)(2,1)} %get-tuple-element.232.r_0_, bf16[512,1024]{1,0:T(8,128)(2,1)} %get-tuple-element.233.r_1_, bf16[512,1024]{1,0:T(8,128)(2,1)} %get-tuple-element.234.r_2_, ...), custom_call_target="tpu_custom_call", output_to_operand_aliasing={{0}: (7, {}), {1}: (8, {})} | custom-call | flops 1000000000 | bytes 1000000 | tf_op jit(solution)/shard_map/pallas_call | solution.py:41
  162.2 17.0 %shard_map.359 = (bf16[512,2560]{1,0:T(8,128)(2,1)}, bf16[512,2560]{1,0:T(8,128)(2,1)}, f32[512,1024]{1,0:T(8,128)}, f32[512,1]{1,0:T(8,128)}, f32[512,1024]{1,0...) custom-call(bf16[512,1024]{1,0:T(8,128)(2,1)} %get-tuple-element.254.refs_0_.refs_21_, ...), custom_call_target="tpu_custom_call" | custom-call | flops 1000000000 | bytes 1000000 | tf_op jit(solution)/shard_map/pallas_call | solution.py:242
  182.4 13.3 %shard_map.360 = (bf16[512,1536]{1,0:T(8,128)(2,1)}, bf16[512,1536]{1,0:T(8,128)(2,1)}, bf16[512,1024]{1,0:T(8,128)(2,1)}, f32[512,1024]{1,0:T(8,128)}, bf16[512,1024]{1,0:T(8,128)(2,1)}, /*index=5*/f32[8,1024]{1,0:T(8,128)}) custom-call(f32[512,1024]{1,0:T(8,128)} %get-tuple-element.262.refs_0_, bf16[512,1024]{1,0:T(8,128)(2,1)} %get-tuple-element.263.refs_1_, ...), custom_call_target="tpu_custom_call" | custom-call | flops 1000000000 | bytes 1000000 | tf_op jit(solution)/shard_map/pallas_call | solution.py:242
  195.7 21.3 %shard_map.361 = (bf16[512,5120]{1,0:T(8,128)(2,1)}, bf16[256,2560]{1,0:T(8,128)(2,1)}, bf16[256,2560]{1,0:T(8,128)(2,1)}, bf16[256,2560]{1,0:T(8,128)(2,1)}, bf...) custom-call(bf16[512,1024]{1,0:T(8,128)(2,1)} %get-tuple-element.277.refs_0_, ...), custom_call_target="tpu_custom_call" | custom-call | flops 1000000000 | bytes 1000000 | tf_op jit(solution)/shard_map/pallas_call | solution.py:326
  218.6 20.7 %shard_map.362 = (bf16[512,4096]{1,0:T(8,128)(2,1)}, bf16[256,2560]{1,0:T(8,128)(2,1)}, bf16[256,2560]{1,0:T(8,128)(2,1)}, bf16[256,1536]{1,0:T(8,128)(2,1)}, bf...) custom-call(bf16[512,1024]{1,0:T(8,128)(2,1)} %get-tuple-element.277, ...), custom_call_target="tpu_custom_call" | custom-call | flops 1000000000 | bytes 1000000 | tf_op jit(solution)/shard_map/pallas_call | solution.py:326
  239.7 3.8 add_convert_fusion.1
  246.1 25.0 %shard_map.363 = (bf16[512,1024]{1,0:T(8,128)(2,1)}, bf16[512,1024]{1,0:T(8,128)(2,1)}, bf16[512,1024]{1,0:T(8,128)(2,1)}, bf16[512,1024]{1,0:T(8,128)(2,1)}, bf16[512,1024]{1,0:T(8,128)(2,1)}) custom-call(bf16[512,1024]{1,0:T(8,128)(2,1)} %get-tuple-element.232.r_0_, bf16[512,1024]{1,0:T(8,128)(2,1)} %get-tuple-element.233.r_1_, ...), custom_call_target="tpu_custom_call" | custom-call | flops 1000000000 | bytes 1000000 | tf_op jit(solution)/shard_map/pallas_call | solution.py:93
  284.8 10.6 %shard_map.364 = (bf16[512,1536]{1,0:T(8,128)(2,1)}, bf16[256,1024]{1,0:T(8,128)(2,1)}, bf16[256,1024]{1,0:T(8,128)(2,1)}, bf16[256,512]{1,0:T(8,128)(2,1)}, bf1...) custom-call(bf16[512,1024]{1,0:T(8,128)(2,1)} %fusion.3.x_ref.refs_1_.refs_0_, ...), custom_call_target="tpu_custom_call" | custom-call | flops 1000000000 | bytes 1000000 | tf_op jit(solution)/shard_map/pallas_call | solution.py:489
  303.9 10.2 %shard_map.365 = (bf16[512,1024]{1,0:T(8,128)(2,1)}, bf16[512,1024]{1,0:T(8,128)(2,1)}, bf16[512,1024]{1,0:T(8,128)(2,1)}, bf16[512,1024]{1,0:T(8,128)(2,1)}, bf16[512,1024]{1,0:T(8,128)(2,1)}) custom-call(bf16[512,1024]{1,0:T(8,128)(2,1)} %get-tuple-element.232.r_0_, ...), custom_call_target="tpu_custom_call", output_to_operand_aliasing={{0}: (7, {}), {1}: (8, {}), {2}: (9, {}), {3}: (10, {}), {4... | custom-call | flops 1000000000 | bytes 1000000 | tf_op jit(solution)/shard_map/pallas_call | solution.py:93
  319.1 12.4 %shard_map.366 = (bf16[512,2176]{1,0:T(8,128)(2,1)}, bf16[256,1024]{1,0:T(8,128)(2,1)}, bf16[256,1024]{1,0:T(8,128)(2,1)}, bf16[256,1152]{1,0:T(8,128)(2,1)}, bf16[256,1152]{1,0:T(8,128)(2,1)}) custom-call(bf16[512,1024]{1,0:T(8,128)(2,1)} %fusion.3.x_ref.refs_1_.refs_0_, bf16[512,512]{1,0:T(8,128)(2,1)} %fusion.7.hot_ref.refs_1_, ...), custom_call_target="tpu_custom_call" | custom-call | flops 1000000000 | bytes 1000000 | tf_op jit(solution)/shard_map/pallas_call | solution.py:489
  340.8 8.0 %collective-permute-done.47 = bf16[128,1536]{1,0:T(8,128)(2,1)S(1)} collective-permute-done((bf16[128,1536]{1,0:T(8,128)(2,1)S(1)}, bf16[128,1536]{1,0:T(8,128)(2,1)S(1)}, u32[]{:S(2)}, u32[]{:S(2)}) %collective-permute-start.47) | collective-permute-done | bytes 393248 | tf_op jit(solution)/shard_map/ppermute | solution.py:557
  356.5 13.6 %shard_map.367 = (bf16[512,1024]{1,0:T(8,128)(2,1)}, bf16[512,1024]{1,0:T(8,128)(2,1)}) custom-call(bf16[512,1024]{1,0:T(8,128)(2,1)} %get-tuple-element.359.refs_0_, bf16[512,1024]{1,0:T(8,128)(2,1)} %get-tuple-element.360.refs_1_, bf16[512,1024]{1,0:T(8,128)(2,1)} %get-tuple-element.327.refs_2_, bf16[512,1024]{1,0:T(8,128)(2,1)} %get-tuple-element.328.refs_3_, ...), custom_call_target="tpu_custom_call" | custom-call | flops 1000000000 | bytes 1000000 | tf_op jit(solution)/shard_map/pallas_call | solution.py:527
  378.9 6.2 %collective-permute-done.57 = bf16[32,4096]{1,0:T(8,128)(2,1)S(1)} collective-permute-done((bf16[32,4096]{1,0:T(8,128)(2,1)S(1)}, bf16[32,4096]{1,0:T(8,128)(2,1)S(1)}, u32[]{:S(2)}, u32[]{:S(2)}) %collective-permute-start.57) | collective-permute-done | bytes 262176 | tf_op jit(solution)/shard_map/ppermute | solution.py:557
  390.3 3.9 collective-permute-done.59
  401.5 6.9 %collective-permute-done.61 = bf16[32,1536]{1,0:T(8,128)(2,1)S(1)} collective-permute-done((bf16[32,1536]{1,0:T(8,128)(2,1)S(1)}, bf16[32,1536]{1,0:T(8,128)(2,1)S(1)}, u32[]{:S(2)}, u32[]{:S(2)}) %collective-permute-start.61) | collective-permute-done | bytes 98336 | tf_op jit(solution)/shard_map/ppermute | solution.py:557
  (330 shorter events, 133.1 us)
Async XLA Ops:
  9.0 20.4 %collective-permute-start.1 = (bf16[32,3712]{1,0:T(8,128)(2,1)}, bf16[32,3712]{1,0:T(8,128)(2,1)S(1)}, u32[]{:S(2)}, u32[]{:S(2)}) collective-permute-start(bf16[32,3712]{1,0:T(8,128)(2,1)} %shard_map.348.refs_0_), channel_id=1, source_target_pairs={{0,16},{4,20},{8,24},{12,28},{16,0},{20,4},{24,8},{28,12},{1,17},{... | collective-permute-start | bytes 712712 | tf_op jit(solution)/shard_map/ppermute | solution.py:557
  9.0 20.4 %collective-permute-start = (bf16[32,3712]{1,0:T(8,128)(2,1)}, bf16[32,3712]{1,0:T(8,128)(2,1)S(1)}, u32[]{:S(2)}, u32[]{:S(2)}) collective-permute-start(bf16[32,3712]{1,0:T(8,128)(2,1)} %shard_map.348.refs_0_), channel_id=1, source_target_pairs={{0,8},{4,12},{8,0},{12,4},{16,24},{20,28},{24,16},{28,20},{1,9},{5... | collective-permute-start | bytes 712712 | tf_op jit(solution)/shard_map/ppermute | solution.py:557
  29.6 23.2 %collective-permute-start.5 = (bf16[128,3712]{1,0:T(8,128)(2,1)S(1)}, bf16[128,3712]{1,0:T(8,128)(2,1)S(1)}, u32[]{:S(2)}, u32[]{:S(2)}) collective-permute-start(bf16[128,3712]{1,0:T(8,128)(2,1)S(1)} %shard_map.350.refs_0_.refs_8_.refs_16_.refs_7_.refs_15_), channel_id=1, source_target_pairs={{0,4},{4,0},{8,12},{12,8},{16,20},{20,16},{24,28},{28,24},{1,5},{5... | collective-permute-start | bytes 2850824 | tf_op jit(solution)/shard_map/ppermute | solution.py:557
  29.6 23.5 %collective-permute-start.4 = (bf16[128,3712]{1,0:T(8,128)(2,1)S(1)}, bf16[128,3712]{1,0:T(8,128)(2,1)S(1)}, u32[]{:S(2)}, u32[]{:S(2)}) collective-permute-start(bf16[128,3712]{1,0:T(8,128)(2,1)S(1)} %shard_map.350.refs_0_.refs_8_.refs_16_.refs_7_.refs_15_), channel_id=1, source_target_pairs={{0,2},{1,3},{2,0},{3,1},{4,6},{5,7},{6,4},{7,5},{8,10},{9,11},{10,... | collective-permute-start | bytes 2850824 | tf_op jit(solution)/shard_map/ppermute | solution.py:557
  31.2 23.1 %collective-permute-start.3 = (bf16[128,3712]{1,0:T(8,128)(2,1)S(1)}, bf16[128,3712]{1,0:T(8,128)(2,1)S(1)}, u32[]{:S(2)}, u32[]{:S(2)}) collective-permute-start(bf16[128,3712]{1,0:T(8,128)(2,1)S(1)} %shard_map.350.refs_0_.refs_8_.refs_16_.refs_7_.refs_15_), channel_id=1, source_target_pairs={{0,1},{1,0},{2,3},{3,2},{4,5},{5,4},{6,7},{7,6},{8,9},{9,8},{10,11... | collective-permute-start | bytes 2850824 | tf_op jit(solution)/shard_map/ppermute | solution.py:557
  69.8 24.4 %collective-permute-start.13 = (bf16[32,3072]{1,0:T(8,128)(2,1)S(1)}, bf16[32,3072]{1,0:T(8,128)(2,1)S(1)}, u32[]{:S(2)}, u32[]{:S(2)}) collective-permute-start(bf16[32,3072]{1,0:T(8,128)(2,1)S(1)} %copy-done.22), channel_id=1, source_target_pairs={{0,16},{4,20},{8,24},{12,28},{16,0},{20,4},{24,8},{28,12},{1,17},{... | collective-permute-start | bytes 589832 | tf_op jit(solution)/shard_map/ppermute | solution.py:557
  75.0 36.5 %collective-permute-start.12 = (bf16[128,6144]{1,0:T(8,128)(2,1)S(1)}, bf16[128,6144]{1,0:T(8,128)(2,1)}, u32[]{:S(2)}, u32[]{:S(2)}) collective-permute-start(bf16[128,6144]{1,0:T(8,128)(2,1)S(1)} %shard_map.352.refs_2_.refs_12_.refs_20_.refs_5_.refs_13_.refs_25_), channel_id=1, source_target_pairs={{0,2},{1,3},{2,0},{3,1},{4,6},{5,7},{6,4},{7,5},{8,10},{9,11},{10,... | collective-permute-start | bytes 4718600 | tf_op jit(solution)/shard_map/ppermute | solution.py:557
  75.4 36.4 %collective-permute-start.11 = (bf16[128,6144]{1,0:T(8,128)(2,1)S(1)}, bf16[128,6144]{1,0:T(8,128)(2,1)}, u32[]{:S(2)}, u32[]{:S(2)}) collective-permute-start(bf16[128,6144]{1,0:T(8,128)(2,1)S(1)} %shard_map.352.refs_2_.refs_12_.refs_20_.refs_5_.refs_13_.refs_25_), channel_id=1, source_target_pairs={{0,1},{1,0},{2,3},{3,2},{4,5},{5,4},{6,7},{7,6},{8,9},{9,8},{10,11... | collective-permute-start | bytes 4718600 | tf_op jit(solution)/shard_map/ppermute | solution.py:557
  111.7 25.2 %collective-permute-start.21 = (bf16[128,6144]{1,0:T(8,128)(2,1)}, bf16[128,6144]{1,0:T(8,128)(2,1)S(1)}, u32[]{:S(2)}, u32[]{:S(2)}) collective-permute-start(bf16[128,6144]{1,0:T(8,128)(2,1)} %collective-permute-done.11.refs_3_.refs_13_.refs_21_.refs_6_.refs_14_.refs_26_), channel_id=1, source_target_pairs={{0,4},{4,0},{8,12},{12,8},{16,20},{20,16},{24,28},{28,24},{1,5},{5... | collective-permute-start | bytes 4718600 | tf_op jit(solution)/shard_map/ppermute | solution.py:557
  113.9 23.1 %collective-permute-start.19 = (bf16[128,3584]{1,0:T(8,128)(2,1)}, bf16[128,3584]{1,0:T(8,128)(2,1)}, u32[]{:S(2)}, u32[]{:S(2)}) collective-permute-start(bf16[128,3584]{1,0:T(8,128)(2,1)} %slice.490), channel_id=1, source_target_pairs={{0,2},{1,3},{2,0},{3,1},{4,6},{5,7},{6,4},{7,5},{8,10},{9,11},{10,... | collective-permute-start | bytes 2752520 | tf_op jit(solution)/shard_map/ppermute | solution.py:557
  137.0 21.6 %collective-permute-start.22 = (bf16[128,6144]{1,0:T(8,128)(2,1)}, bf16[128,6144]{1,0:T(8,128)(2,1)}, u32[]{:S(2)}, u32[]{:S(2)}) collective-permute-start(bf16[128,6144]{1,0:T(8,128)(2,1)} %collective-permute-done.12.refs_4_.refs_14_.refs_22_.refs_7_.refs_15_.refs_27_), channel_id=1, source_target_pairs={{0,4},{4,0},{8,12},{12,8},{16,20},{20,16},{24,28},{28,24},{1,5},{5... | collective-permute-start | bytes 4718600 | tf_op jit(solution)/shard_map/ppermute | solution.py:557
  137.0 21.6 %collective-permute-start.23 = (bf16[128,3584]{1,0:T(8,128)(2,1)}, bf16[128,3584]{1,0:T(8,128)(2,1)}, u32[]{:S(2)}, u32[]{:S(2)}) collective-permute-start(bf16[128,3584]{1,0:T(8,128)(2,1)} %collective-permute-done.19.refs_5_.refs_15_.refs_8_.refs_28_), channel_id=1, source_target_pairs={{0,4},{4,0},{8,12},{12,8},{16,20},{20,16},{24,28},{28,24},{1,5},{5... | collective-permute-start | bytes 2752520 | tf_op jit(solution)/shard_map/ppermute | solution.py:557
  137.5 20.9 %collective-permute-start.26 = (bf16[128,3072]{1,0:T(8,128)(2,1)S(1)}, bf16[128,3072]{1,0:T(8,128)(2,1)S(1)}, u32[]{:S(2)}, u32[]{:S(2)}) collective-permute-start(bf16[128,3072]{1,0:T(8,128)(2,1)S(1)} %shard_map.356.refs_5_.refs_13_), channel_id=1, source_target_pairs={{0,2},{1,3},{2,0},{3,1},{4,6},{5,7},{6,4},{7,5},{8,10},{9,11},{10,... | collective-permute-start | bytes 2359304 | tf_op jit(solution)/shard_map/ppermute | solution.py:557
  158.6 20.6 %collective-permute-start.29 = (bf16[128,3072]{1,0:T(8,128)(2,1)S(1)}, bf16[128,3072]{1,0:T(8,128)(2,1)S(1)}, u32[]{:S(2)}, u32[]{:S(2)}) collective-permute-start(bf16[128,3072]{1,0:T(8,128)(2,1)S(1)} %shard_map.356.refs_5_.refs_13_), channel_id=1, source_target_pairs={{0,4},{4,0},{8,12},{12,8},{16,20},{20,16},{24,28},{28,24},{1,5},{5... | collective-permute-start | bytes 2359304 | tf_op jit(solution)/shard_map/ppermute | solution.py:557
  159.0 20.2 %collective-permute-start.30 = (bf16[128,3072]{1,0:T(8,128)(2,1)}, bf16[128,3072]{1,0:T(8,128)(2,1)S(1)}, u32[]{:S(2)}, u32[]{:S(2)}) collective-permute-start(bf16[128,3072]{1,0:T(8,128)(2,1)} %collective-permute-done.25.refs_6_.refs_14_), channel_id=1, source_target_pairs={{0,4},{4,0},{8,12},{12,8},{16,20},{20,16},{24,28},{28,24},{1,5},{5... | collective-permute-start | bytes 2359304 | tf_op jit(solution)/shard_map/ppermute | solution.py:557
  217.0 22.7 %collective-permute-start.34 = (bf16[512,5120]{1,0:T(8,128)(2,1)}, bf16[512,5120]{1,0:T(8,128)(2,1)}, u32[]{:S(2)}, u32[]{:S(2)}) collective-permute-start(bf16[512,5120]{1,0:T(8,128)(2,1)} %get-tuple-element.288), channel_id=1, source_target_pairs={{0,4},{4,0},{8,12},{12,8},{16,20},{20,16},{24,28},{28,24},{1,5},{5... | collective-permute-start | bytes 15728648 | tf_op jit(solution)/shard_map/ppermute | solution.py:557
  239.3 31.8 %collective-permute-start.37 = (bf16[512,4096]{1,0:T(8,128)(2,1)}, bf16[512,4096]{1,0:T(8,128)(2,1)}, u32[]{:S(2)}, u32[]{:S(2)}) collective-permute-start(bf16[512,4096]{1,0:T(8,128)(2,1)} %get-tuple-element.292), channel_id=1, source_target_pairs={{0,4},{4,0},{8,12},{12,8},{16,20},{20,16},{24,28},{28,24},{1,5},{5... | collective-permute-start | bytes 12582920 | tf_op jit(solution)/shard_map/ppermute | solution.py:557
  243.5 31.1 %collective-permute-start.36 = (bf16[256,2560]{1,0:T(8,128)(2,1)}, bf16[256,2560]{1,0:T(8,128)(2,1)}, u32[]{:S(2)}, u32[]{:S(2)}) collective-permute-start(bf16[256,2560]{1,0:T(8,128)(2,1)} %get-tuple-element.404), channel_id=1, source_target_pairs={{0,2},{1,3},{2,0},{3,1},{4,6},{5,7},{6,4},{7,5},{8,10},{9,11},{10,... | collective-permute-start | bytes 3932168 | tf_op jit(solution)/shard_map/ppermute | solution.py:557
  245.2 30.9 %collective-permute-start.35 = (bf16[256,2560]{1,0:T(8,128)(2,1)}, bf16[256,2560]{1,0:T(8,128)(2,1)}, u32[]{:S(2)}, u32[]{:S(2)}) collective-permute-start(bf16[256,2560]{1,0:T(8,128)(2,1)} %get-tuple-element.405), channel_id=1, source_target_pairs={{0,1},{1,0},{2,3},{3,2},{4,5},{5,4},{6,7},{7,6},{8,9},{9,8},{10,11... | collective-permute-start | bytes 3932168 | tf_op jit(solution)/shard_map/ppermute | solution.py:557
  283.1 48.4 %collective-permute-start.39 = (bf16[256,1536]{1,0:T(8,128)(2,1)}, bf16[256,1536]{1,0:T(8,128)(2,1)}, u32[]{:S(2)}, u32[]{:S(2)}) collective-permute-start(bf16[256,1536]{1,0:T(8,128)(2,1)} %add_convert_fusion.3), channel_id=1, source_target_pairs={{0,2},{1,3},{2,0},{3,1},{4,6},{5,7},{6,4},{7,5},{8,10},{9,11},{10,... | collective-permute-start | bytes 2359304 | tf_op jit(solution)/shard_map/ppermute | solution.py:557
  302.6 28.8 %collective-permute-start.38 = (bf16[256,2560]{1,0:T(8,128)(2,1)}, bf16[256,2560]{1,0:T(8,128)(2,1)}, u32[]{:S(2)}, u32[]{:S(2)}) collective-permute-start(bf16[256,2560]{1,0:T(8,128)(2,1)} %add_convert_fusion), channel_id=1, source_target_pairs={{0,1},{1,0},{2,3},{3,2},{4,5},{5,4},{6,7},{7,6},{8,9},{9,8},{10,11... | collective-permute-start | bytes 3932168 | tf_op jit(solution)/shard_map/ppermute | solution.py:557
  331.5 20.6 %collective-permute-start.45 = (bf16[512,2176]{1,0:T(8,128)(2,1)}, bf16[512,2176]{1,0:T(8,128)(2,1)S(1)}, u32[]{:S(2)}, u32[]{:S(2)}) collective-permute-start(bf16[512,2176]{1,0:T(8,128)(2,1)} %get-tuple-element.345), channel_id=1, source_target_pairs={{0,4},{4,0},{8,12},{12,8},{16,20},{20,16},{24,28},{28,24},{1,5},{5... | collective-permute-start | bytes 6684680 | tf_op jit(solution)/shard_map/ppermute | solution.py:557
  337.8 32.3 %collective-permute-start.51 = (bf16[256,512]{1,0:T(8,128)(2,1)S(1)}, bf16[256,512]{1,0:T(8,128)(2,1)}, u32[]{:S(2)}, u32[]{:S(2)}) collective-permute-start(bf16[256,512]{1,0:T(8,128)(2,1)S(1)} %add_convert_fusion.31), channel_id=1, source_target_pairs={{0,2},{1,3},{2,0},{3,1},{4,6},{5,7},{6,4},{7,5},{8,10},{9,11},{10,... | collective-permute-start | bytes 786440 | tf_op jit(solution)/shard_map/ppermute | solution.py:557
  339.8 30.4 %collective-permute-start.50 = (bf16[256,1024]{1,0:T(8,128)(2,1)S(1)}, bf16[256,1024]{1,0:T(8,128)(2,1)S(1)}, u32[]{:S(2)}, u32[]{:S(2)}) collective-permute-start(bf16[256,1024]{1,0:T(8,128)(2,1)S(1)} %add_convert_fusion.11), channel_id=1, source_target_pairs={{0,1},{1,0},{2,3},{3,2},{4,5},{5,4},{6,7},{7,6},{8,9},{9,8},{10,11... | collective-permute-start | bytes 1572872 | tf_op jit(solution)/shard_map/ppermute | solution.py:557
  (99 other events, 1093.0 us)

commit v6 on v5

--- a/solution.py
+++ b/solution.py
@@ -140,7 +140,7 @@
 
     return pl.pallas_call(
         kernel, out_shape=jax.ShapeDtypeStruct((rows * len(blocks), n), BF), cost_estimate=COST,
-        compiler_params=pltpu.CompilerParams(vmem_limit_bytes=32 * 2**20),
+        compiler_params=pltpu.CompilerParams(vmem_limit_bytes=16 * 2**20),
     )(*blocks)
 
 
@@ -242,7 +242,7 @@
     return pl.pallas_call(
         kernel, grid=(count,), in_specs=specs, out_specs=[o[1] for o in outs], out_shape=[o[0] for o in outs],
         scratch_shapes=[pltpu.VMEM((t, d), F32)], cost_estimate=COST,
-        compiler_params=pltpu.CompilerParams(vmem_limit_bytes=56 * 2**20),
+        compiler_params=pltpu.CompilerParams(vmem_limit_bytes=50 * 2**20),
     )(*ins)
 
 

time: 421 us -> 418 us (level)
  transfers between devices with their start and end apart: 62 -> 62, of which waited for: 26 -> 27; matrix products, arithmetic and copies ran while one was open for 10% -> 9% of each run, Pallas kernels for 39% -> 39%
where the time goes in v6:
time: 418 us; the launch traced here: 412 us
  Pallas kernels  199 us (48%)
  waiting for transfers between devices  103 us (25%)
  starting transfers between devices  55.1 us (13%)
  other arithmetic  32 us (8%)
  local copies, waits for them, and re-layouts  15.8 us (4%)
  matrix products  5.73 us (1%)
    ppermute x62, waiting for transfers between devices, swap(): return lax.ppermute(a, axis, [(i, i ^ bit) for i in range(size)])  103 us
    ppermute x62, starting transfers between devices, swap(): return lax.ppermute(a, axis, [(i, i ^ bit) for i in range(size)])  55.1 us
    pallas_call x2, Pallas kernels, feed_back(): pl.pallas_call(kernel, grid=(count,), in_specs=specs, out_specs=[o[1] for...  42 us
    pallas_call x3, Pallas kernels, attend(): pl.pallas_call(lambda *r: attend_kernel(scale, *r[:7], *r[len(r) - 2:]),...  36.7 us
    pallas_call x2, Pallas kernels, attend_back(): pl.pallas_call(lambda *r: attend_back_kernel(scale, *r[:7], *r[len(r) - 5...  35.1 us
    pallas_call x2, Pallas kernels, feed_forward(): pl.pallas_call(kernel, grid=(count,), in_specs=specs, out_specs=[o[1] for...  29.1 us
    pallas_call x2, Pallas kernels, attention_grads(): pl.pallas_call(kernel, grid=(3,), in_specs=specs, out_specs=[o[1] for o i...  23 us
    convert_element_type x25, other arithmetic, add(): sums = lambda *xs: total(*xs).astype(BF)  22.6 us
  transfers between devices with their start and end apart: 62, of which 27 were waited for; matrix products, arithmetic and copies ran while one was open for 9% of the time, Pallas kernels for 39%

profile of v6, /device:TPU:0, one launch (start us, length us, event | category | flops | bytes accessed | tf_op | source)
XLA Modules:
  0.0 412.1 jit_solution(6183684569000551708)
XLA Ops:
  4.0 5.0 %collective-permute-start.2 = (bf16[32,3712]{1,0:T(8,128)(2,1)}, bf16[32,3712]{1,0:T(8,128)(2,1)S(1)}, u32[]{:S(2)}, u32[]{:S(2)}) collective-permute-start(bf16[32,3712]{1,0:T(8,128)(2,1)} %shard_map.348.refs_0_), channel_id=1, source_target_pairs={{0,24},{4,28},{8,16},{12,20},{16,8},{20,12},{24,0},{28,4},{1,25},{... | collective-permute-start | bytes 712712 | tf_op jit(solution)/shard_map/ppermute | solution.py:557
  16.0 13.5 %collective-permute-done.1.refs_1_ = bf16[32,3712]{1,0:T(8,128)(2,1)S(1)} collective-permute-done((bf16[32,3712]{1,0:T(8,128)(2,1)}, bf16[32,3712]{1,0:T(8,128)(2,1)S(1)}, u32[]{:S(2)}, u32[]{:S(2)}) %collective-permute-start.1) | collective-permute-done | bytes 237600 | tf_op jit(solution)/shard_map/ppermute | solution.py:557
  35.0 17.8 %collective-permute-done.6.refs_1_ = bf16[32,6144]{1,0:T(8,128)(2,1)S(1)} collective-permute-done((bf16[32,6144]{1,0:T(8,128)(2,1)S(1)}, bf16[32,6144]{1,0:T(8,128)(2,1)S(1)}, u32[]{:S(2)}, u32[]{:S(2)}) %collective-permute-start.6) | collective-permute-done | bytes 393248 | tf_op jit(solution)/shard_map/ppermute | solution.py:557
  59.3 10.5 %collective-permute-done.8.refs_11_.refs_19_.refs_18_ = bf16[128,1664]{1,0:T(8,128)(2,1)S(1)} collective-permute-done((bf16[128,1664]{1,0:T(8,128)(2,1)S(1)}, bf16[128,1664]{1,0:T(8,128)(2,1)S(1)}, u32[]{:S(2)}, u32[]{:S(2)}) %collective-permute-start.8) | collective-permute-done | bytes 426016 | tf_op jit(solution)/shard_map/ppermute | solution.py:557
  79.3 13.1 %shard_map.353 = (bf16[512,1024]{1,0:T(8,128)(2,1)}, bf16[512,1024]{1,0:T(8,128)(2,1)}, bf16[512,1024]{1,0:T(8,128)(2,1)}, bf16[512,1024]{1,0:T(8,128)(2,1)}, bf16[512,1024]{1,0:T(8,128)(2,1)}) custom-call(bf16[512,1024]{1,0:T(8,128)(2,1)} %fusion.3.x_ref.refs_1_.refs_0_, bf16[512,512]{1,0:T(8,128)(2,1)} %fusion.7.hot_ref.refs_1_, f32[1,3072]{1,0:T(1,128)} %bitcast.51, ...), custom_call_target="tpu_custom_call" | custom-call | flops 1000000000 | bytes 1000000 | tf_op jit(solution)/shard_map/pallas_call | solution.py:408
  95.0 5.6 %shard_map.355 = (bf16[512,1024]{1,0:T(8,128)(2,1)}, bf16[16,512,512]{2,1,0:T(8,128)(2,1)}) custom-call(bf16[512,1024]{1,0:T(8,128)(2,1)} %get-tuple-element.232.r_0_, bf16[512,1024]{1,0:T(8,128)(2,1)} %get-tuple-element.233.r_1_, bf16[512,1024]{1,0:T(8,128)(2,1)} %get-tuple-element.234.r_2_, bf16[512,1024]{1,0:T(8,128)(2,1)} %get-tuple-element.235.r_3_, ...), custom_call_target="tpu_custom_call" | custom-call | flops 1000000000 | bytes 1000000 | tf_op jit(solution)/shard_map/pallas_call | solution.py:41
  100.6 4.9 %collective-permute-done.18.refs_1_ = bf16[64,3072]{1,0:T(8,128)(2,1)S(1)} collective-permute-done((bf16[64,3072]{1,0:T(8,128)(2,1)S(1)}, bf16[64,3072]{1,0:T(8,128)(2,1)S(1)}, u32[]{:S(2)}, u32[]{:S(2)}) %collective-permute-start.18) | collective-permute-done | bytes 393248 | tf_op jit(solution)/shard_map/ppermute | solution.py:557
  105.5 4.9 %collective-permute-done.12.refs_4_.refs_14_.refs_22_.refs_7_.refs_15_.refs_27_ = bf16[128,6144]{1,0:T(8,128)(2,1)} collective-permute-done((bf16[128,6144]{1,0:T(8,128)(2,1)S(1)}, bf16[128,6144]{1,0:T(8,128)(2,1)}, u32[]{:S(2)}, u32[]{:S(2)}) %collective-permute-start.12) | collective-permute-done | bytes 1572896 | tf_op jit(solution)/shard_map/ppermute | solution.py:557
  118.9 13.4 %shard_map.357 = (bf16[512,1024]{1,0:T(8,128)(2,1)}, bf16[16,512,512]{2,1,0:T(8,128)(2,1)}) custom-call(bf16[512,1024]{1,0:T(8,128)(2,1)} %get-tuple-element.232.r_0_, bf16[512,1024]{1,0:T(8,128)(2,1)} %get-tuple-element.233.r_1_, bf16[512,1024]{1,0:T(8,128)(2,1)} %get-tuple-element.234.r_2_, ...), custom_call_target="tpu_custom_call", output_to_operand_aliasing={{0}: (7, {}), {1}: (8, {})} | custom-call | flops 1000000000 | bytes 1000000 | tf_op jit(solution)/shard_map/pallas_call | solution.py:41
  140.2 17.7 %shard_map.358 = (bf16[512,1024]{1,0:T(8,128)(2,1)}, bf16[16,512,512]{2,1,0:T(8,128)(2,1)}) custom-call(bf16[512,1024]{1,0:T(8,128)(2,1)} %get-tuple-element.232.r_0_, bf16[512,1024]{1,0:T(8,128)(2,1)} %get-tuple-element.233.r_1_, bf16[512,1024]{1,0:T(8,128)(2,1)} %get-tuple-element.234.r_2_, ...), custom_call_target="tpu_custom_call", output_to_operand_aliasing={{0}: (7, {}), {1}: (8, {})} | custom-call | flops 1000000000 | bytes 1000000 | tf_op jit(solution)/shard_map/pallas_call | solution.py:41
  161.9 16.4 %shard_map.359 = (bf16[512,2560]{1,0:T(8,128)(2,1)}, bf16[512,2560]{1,0:T(8,128)(2,1)}, f32[512,1024]{1,0:T(8,128)}, f32[512,1]{1,0:T(8,128)S(1)}, f32[512,1024]...) custom-call(bf16[512,1024]{1,0:T(8,128)(2,1)} %get-tuple-element.254.refs_0_.refs_21_, ...), custom_call_target="tpu_custom_call" | custom-call | flops 1000000000 | bytes 1000000 | tf_op jit(solution)/shard_map/pallas_call | solution.py:242
  180.8 12.7 %shard_map.360 = (bf16[512,1536]{1,0:T(8,128)(2,1)}, bf16[512,1536]{1,0:T(8,128)(2,1)}, bf16[512,1024]{1,0:T(8,128)(2,1)}, f32[512,1024]{1,0:T(8,128)}, bf16[512...) custom-call(f32[512,1024]{1,0:T(8,128)} %get-tuple-element.262.refs_0_, bf16[512,1024]{1,0:T(8,128)(2,1)} %get-tuple-element.263.refs_1_, ...), custom_call_target="tpu_custom_call" | custom-call | flops 1000000000 | bytes 1000000 | tf_op jit(solution)/shard_map/pallas_call | solution.py:242
  193.6 21.3 %shard_map.361 = (bf16[512,5120]{1,0:T(8,128)(2,1)}, bf16[256,2560]{1,0:T(8,128)(2,1)}, bf16[256,2560]{1,0:T(8,128)(2,1)}, bf16[256,2560]{1,0:T(8,128)(2,1)}, bf...) custom-call(bf16[512,1024]{1,0:T(8,128)(2,1)} %get-tuple-element.277.refs_0_, ...), custom_call_target="tpu_custom_call" | custom-call | flops 1000000000 | bytes 1000000 | tf_op jit(solution)/shard_map/pallas_call | solution.py:326
  215.7 20.7 %shard_map.362 = (bf16[512,4096]{1,0:T(8,128)(2,1)}, bf16[256,2560]{1,0:T(8,128)(2,1)}, bf16[256,2560]{1,0:T(8,128)(2,1)}, bf16[256,1536]{1,0:T(8,128)(2,1)}, bf...) custom-call(bf16[512,1024]{1,0:T(8,128)(2,1)} %get-tuple-element.277, ...), custom_call_target="tpu_custom_call" | custom-call | flops 1000000000 | bytes 1000000 | tf_op jit(solution)/shard_map/pallas_call | solution.py:326
  242.2 25.0 %shard_map.363 = (bf16[512,1024]{1,0:T(8,128)(2,1)}, bf16[512,1024]{1,0:T(8,128)(2,1)}, bf16[512,1024]{1,0:T(8,128)(2,1)}, bf16[512,1024]{1,0:T(8,128)(2,1)}, bf16[512,1024]{1,0:T(8,128)(2,1)}) custom-call(bf16[512,1024]{1,0:T(8,128)(2,1)} %get-tuple-element.232.r_0_, bf16[512,1024]{1,0:T(8,128)(2,1)} %get-tuple-element.233.r_1_, ...), custom_call_target="tpu_custom_call" | custom-call | flops 1000000000 | bytes 1000000 | tf_op jit(solution)/shard_map/pallas_call | solution.py:93
  267.1 4.7 %collective-permute-done.36 = bf16[256,2560]{1,0:T(8,128)(2,1)} collective-permute-done((bf16[256,2560]{1,0:T(8,128)(2,1)}, bf16[256,2560]{1,0:T(8,128)(2,1)}, u32[]{:S(2)}, u32[]{:S(2)}) %collective-permute-start.36) | collective-permute-done | bytes 1310752 | tf_op jit(solution)/shard_map/ppermute | solution.py:557
  272.5 3.9 add_convert_fusion.6
  281.2 10.5 %shard_map.364 = (bf16[512,1536]{1,0:T(8,128)(2,1)}, bf16[256,1024]{1,0:T(8,128)(2,1)}, bf16[256,1024]{1,0:T(8,128)(2,1)}, bf16[256,512]{1,0:T(8,128)(2,1)}, bf1...) custom-call(bf16[512,1024]{1,0:T(8,128)(2,1)} %fusion.3.x_ref.refs_1_.refs_0_, ...), custom_call_target="tpu_custom_call" | custom-call | flops 1000000000 | bytes 1000000 | tf_op jit(solution)/shard_map/pallas_call | solution.py:489
  300.6 10.2 %shard_map.365 = (bf16[512,1024]{1,0:T(8,128)(2,1)}, bf16[512,1024]{1,0:T(8,128)(2,1)}, bf16[512,1024]{1,0:T(8,128)(2,1)}, bf16[512,1024]{1,0:T(8,128)(2,1)}, bf16[512,1024]{1,0:T(8,128)(2,1)}) custom-call(bf16[512,1024]{1,0:T(8,128)(2,1)} %get-tuple-element.232.r_0_, ...), custom_call_target="tpu_custom_call", output_to_operand_aliasing={{0}: (7, {}), {1}: (8, {}), {2}: (9, {}), {3}: (10, {}), {4... | custom-call | flops 1000000000 | bytes 1000000 | tf_op jit(solution)/shard_map/pallas_call | solution.py:93
  316.8 12.4 %shard_map.366 = (bf16[512,2176]{1,0:T(8,128)(2,1)}, bf16[256,1024]{1,0:T(8,128)(2,1)}, bf16[256,1024]{1,0:T(8,128)(2,1)}, bf16[256,1152]{1,0:T(8,128)(2,1)}, bf16[256,1152]{1,0:T(8,128)(2,1)}) custom-call(bf16[512,1024]{1,0:T(8,128)(2,1)} %fusion.3.x_ref.refs_1_.refs_0_, bf16[512,512]{1,0:T(8,128)(2,1)} %fusion.7.hot_ref.refs_1_, ...), custom_call_target="tpu_custom_call" | custom-call | flops 1000000000 | bytes 1000000 | tf_op jit(solution)/shard_map/pallas_call | solution.py:489
  339.2 7.3 %collective-permute-done.47 = bf16[128,1536]{1,0:T(8,128)(2,1)S(1)} collective-permute-done((bf16[128,1536]{1,0:T(8,128)(2,1)S(1)}, bf16[128,1536]{1,0:T(8,128)(2,1)S(1)}, u32[]{:S(2)}, u32[]{:S(2)}) %collective-permute-start.47) | collective-permute-done | bytes 393248 | tf_op jit(solution)/shard_map/ppermute | solution.py:557
  353.9 13.6 %shard_map.367 = (bf16[512,1024]{1,0:T(8,128)(2,1)}, bf16[512,1024]{1,0:T(8,128)(2,1)}) custom-call(bf16[512,1024]{1,0:T(8,128)(2,1)} %get-tuple-element.359.refs_0_, bf16[512,1024]{1,0:T(8,128)(2,1)} %get-tuple-element.360.refs_1_, bf16[512,1024]{1,0:T(8,128)(2,1)} %get-tuple-element.327.refs_2_, bf16[512,1024]{1,0:T(8,128)(2,1)} %get-tuple-element.328.refs_3_, ...), custom_call_target="tpu_custom_call" | custom-call | flops 1000000000 | bytes 1000000 | tf_op jit(solution)/shard_map/pallas_call | solution.py:527
  377.7 4.9 %collective-permute-done.57 = bf16[32,4096]{1,0:T(8,128)(2,1)S(1)} collective-permute-done((bf16[32,4096]{1,0:T(8,128)(2,1)S(1)}, bf16[32,4096]{1,0:T(8,128)(2,1)S(1)}, u32[]{:S(2)}, u32[]{:S(2)}) %collective-permute-start.57) | collective-permute-done | bytes 262176 | tf_op jit(solution)/shard_map/ppermute | solution.py:557
  398.8 6.9 %collective-permute-done.61 = bf16[32,1536]{1,0:T(8,128)(2,1)S(1)} collective-permute-done((bf16[32,1536]{1,0:T(8,128)(2,1)S(1)}, bf16[32,1536]{1,0:T(8,128)(2,1)S(1)}, u32[]{:S(2)}, u32[]{:S(2)}) %collective-permute-start.61) | collective-permute-done | bytes 98336 | tf_op jit(solution)/shard_map/ppermute | solution.py:557
  (334 shorter events, 133.1 us)
Async XLA Ops:
  9.0 20.4 %collective-permute-start.1 = (bf16[32,3712]{1,0:T(8,128)(2,1)}, bf16[32,3712]{1,0:T(8,128)(2,1)S(1)}, u32[]{:S(2)}, u32[]{:S(2)}) collective-permute-start(bf16[32,3712]{1,0:T(8,128)(2,1)} %shard_map.348.refs_0_), channel_id=1, source_target_pairs={{0,16},{4,20},{8,24},{12,28},{16,0},{20,4},{24,8},{28,12},{1,17},{... | collective-permute-start | bytes 712712 | tf_op jit(solution)/shard_map/ppermute | solution.py:557
  9.0 20.4 %collective-permute-start = (bf16[32,3712]{1,0:T(8,128)(2,1)}, bf16[32,3712]{1,0:T(8,128)(2,1)S(1)}, u32[]{:S(2)}, u32[]{:S(2)}) collective-permute-start(bf16[32,3712]{1,0:T(8,128)(2,1)} %shard_map.348.refs_0_), channel_id=1, source_target_pairs={{0,8},{4,12},{8,0},{12,4},{16,24},{20,28},{24,16},{28,20},{1,9},{5... | collective-permute-start | bytes 712712 | tf_op jit(solution)/shard_map/ppermute | solution.py:557
  29.6 23.2 %collective-permute-start.5 = (bf16[128,3712]{1,0:T(8,128)(2,1)S(1)}, bf16[128,3712]{1,0:T(8,128)(2,1)S(1)}, u32[]{:S(2)}, u32[]{:S(2)}) collective-permute-start(bf16[128,3712]{1,0:T(8,128)(2,1)S(1)} %shard_map.350.refs_0_.refs_8_.refs_16_.refs_7_.refs_15_), channel_id=1, source_target_pairs={{0,4},{4,0},{8,12},{12,8},{16,20},{20,16},{24,28},{28,24},{1,5},{5... | collective-permute-start | bytes 2850824 | tf_op jit(solution)/shard_map/ppermute | solution.py:557
  29.6 23.5 %collective-permute-start.4 = (bf16[128,3712]{1,0:T(8,128)(2,1)S(1)}, bf16[128,3712]{1,0:T(8,128)(2,1)S(1)}, u32[]{:S(2)}, u32[]{:S(2)}) collective-permute-start(bf16[128,3712]{1,0:T(8,128)(2,1)S(1)} %shard_map.350.refs_0_.refs_8_.refs_16_.refs_7_.refs_15_), channel_id=1, source_target_pairs={{0,2},{1,3},{2,0},{3,1},{4,6},{5,7},{6,4},{7,5},{8,10},{9,11},{10,... | collective-permute-start | bytes 2850824 | tf_op jit(solution)/shard_map/ppermute | solution.py:557
  31.2 23.1 %collective-permute-start.3 = (bf16[128,3712]{1,0:T(8,128)(2,1)S(1)}, bf16[128,3712]{1,0:T(8,128)(2,1)S(1)}, u32[]{:S(2)}, u32[]{:S(2)}) collective-permute-start(bf16[128,3712]{1,0:T(8,128)(2,1)S(1)} %shard_map.350.refs_0_.refs_8_.refs_16_.refs_7_.refs_15_), channel_id=1, source_target_pairs={{0,1},{1,0},{2,3},{3,2},{4,5},{5,4},{6,7},{7,6},{8,9},{9,8},{10,11... | collective-permute-start | bytes 2850824 | tf_op jit(solution)/shard_map/ppermute | solution.py:557
  32.7 20.1 %collective-permute-start.6 = (bf16[32,6144]{1,0:T(8,128)(2,1)S(1)}, bf16[32,6144]{1,0:T(8,128)(2,1)S(1)}, u32[]{:S(2)}, u32[]{:S(2)}) collective-permute-start(bf16[32,6144]{1,0:T(8,128)(2,1)S(1)} %copy-done.29), channel_id=1, source_target_pairs={{0,16},{4,20},{8,24},{12,28},{16,0},{20,4},{24,8},{28,12},{1,17},{... | collective-permute-start | bytes 1179656 | tf_op jit(solution)/shard_map/ppermute | solution.py:557
  69.8 23.0 %collective-permute-start.13 = (bf16[32,3072]{1,0:T(8,128)(2,1)}, bf16[32,3072]{1,0:T(8,128)(2,1)}, u32[]{:S(2)}, u32[]{:S(2)}) collective-permute-start(bf16[32,3072]{1,0:T(8,128)(2,1)} %get-tuple-element.214.refs_0_), channel_id=1, source_target_pairs={{0,16},{4,20},{8,24},{12,28},{16,0},{20,4},{24,8},{28,12},{1,17},{... | collective-permute-start | bytes 589832 | tf_op jit(solution)/shard_map/ppermute | solution.py:557
  73.9 36.5 %collective-permute-start.12 = (bf16[128,6144]{1,0:T(8,128)(2,1)S(1)}, bf16[128,6144]{1,0:T(8,128)(2,1)}, u32[]{:S(2)}, u32[]{:S(2)}) collective-permute-start(bf16[128,6144]{1,0:T(8,128)(2,1)S(1)} %shard_map.352.refs_2_.refs_12_.refs_20_.refs_5_.refs_13_.refs_25_), channel_id=1, source_target_pairs={{0,2},{1,3},{2,0},{3,1},{4,6},{5,7},{6,4},{7,5},{8,10},{9,11},{10,... | collective-permute-start | bytes 4718600 | tf_op jit(solution)/shard_map/ppermute | solution.py:557
  75.1 36.3 %collective-permute-start.11 = (bf16[128,6144]{1,0:T(8,128)(2,1)S(1)}, bf16[128,6144]{1,0:T(8,128)(2,1)}, u32[]{:S(2)}, u32[]{:S(2)}) collective-permute-start(bf16[128,6144]{1,0:T(8,128)(2,1)S(1)} %shard_map.352.refs_2_.refs_12_.refs_20_.refs_5_.refs_13_.refs_25_), channel_id=1, source_target_pairs={{0,1},{1,0},{2,3},{3,2},{4,5},{5,4},{6,7},{7,6},{8,9},{9,8},{10,11... | collective-permute-start | bytes 4718600 | tf_op jit(solution)/shard_map/ppermute | solution.py:557
  111.4 25.1 %collective-permute-start.21 = (bf16[128,6144]{1,0:T(8,128)(2,1)}, bf16[128,6144]{1,0:T(8,128)(2,1)S(1)}, u32[]{:S(2)}, u32[]{:S(2)}) collective-permute-start(bf16[128,6144]{1,0:T(8,128)(2,1)} %collective-permute-done.11.refs_3_.refs_13_.refs_21_.refs_6_.refs_14_.refs_26_), channel_id=1, source_target_pairs={{0,4},{4,0},{8,12},{12,8},{16,20},{20,16},{24,28},{28,24},{1,5},{5... | collective-permute-start | bytes 4718600 | tf_op jit(solution)/shard_map/ppermute | solution.py:557
  113.5 23.0 %collective-permute-start.19 = (bf16[128,3584]{1,0:T(8,128)(2,1)}, bf16[128,3584]{1,0:T(8,128)(2,1)S(1)}, u32[]{:S(2)}, u32[]{:S(2)}) collective-permute-start(bf16[128,3584]{1,0:T(8,128)(2,1)} %slice.490), channel_id=1, source_target_pairs={{0,2},{1,3},{2,0},{3,1},{4,6},{5,7},{6,4},{7,5},{8,10},{9,11},{10,... | collective-permute-start | bytes 2752520 | tf_op jit(solution)/shard_map/ppermute | solution.py:557
  136.5 22.0 %collective-permute-start.22 = (bf16[128,6144]{1,0:T(8,128)(2,1)}, bf16[128,6144]{1,0:T(8,128)(2,1)}, u32[]{:S(2)}, u32[]{:S(2)}) collective-permute-start(bf16[128,6144]{1,0:T(8,128)(2,1)} %collective-permute-done.12.refs_4_.refs_14_.refs_22_.refs_7_.refs_15_.refs_27_), channel_id=1, source_target_pairs={{0,4},{4,0},{8,12},{12,8},{16,20},{20,16},{24,28},{28,24},{1,5},{5... | collective-permute-start | bytes 4718600 | tf_op jit(solution)/shard_map/ppermute | solution.py:557
  137.7 20.9 %collective-permute-start.23 = (bf16[128,3584]{1,0:T(8,128)(2,1)S(1)}, bf16[128,3584]{1,0:T(8,128)(2,1)S(1)}, u32[]{:S(2)}, u32[]{:S(2)}) collective-permute-start(bf16[128,3584]{1,0:T(8,128)(2,1)S(1)} %collective-permute-done.19.refs_5_.refs_15_.refs_8_.refs_28_), channel_id=1, source_target_pairs={{0,4},{4,0},{8,12},{12,8},{16,20},{20,16},{24,28},{28,24},{1,5},{5... | collective-permute-start | bytes 2752520 | tf_op jit(solution)/shard_map/ppermute | solution.py:557
  137.7 20.2 %collective-permute-start.26 = (bf16[128,3072]{1,0:T(8,128)(2,1)}, bf16[128,3072]{1,0:T(8,128)(2,1)S(1)}, u32[]{:S(2)}, u32[]{:S(2)}) collective-permute-start(bf16[128,3072]{1,0:T(8,128)(2,1)} %shard_map.356.refs_5_.refs_13_), channel_id=1, source_target_pairs={{0,2},{1,3},{2,0},{3,1},{4,6},{5,7},{6,4},{7,5},{8,10},{9,11},{10,... | collective-permute-start | bytes 2359304 | tf_op jit(solution)/shard_map/ppermute | solution.py:557
  138.7 19.9 %collective-permute-start.25 = (bf16[128,3072]{1,0:T(8,128)(2,1)}, bf16[128,3072]{1,0:T(8,128)(2,1)S(1)}, u32[]{:S(2)}, u32[]{:S(2)}) collective-permute-start(bf16[128,3072]{1,0:T(8,128)(2,1)} %shard_map.356.refs_5_.refs_13_), channel_id=1, source_target_pairs={{0,1},{1,0},{2,3},{3,2},{4,5},{5,4},{6,7},{7,6},{8,9},{9,8},{10,11... | collective-permute-start | bytes 2359304 | tf_op jit(solution)/shard_map/ppermute | solution.py:557
  214.9 21.9 %collective-permute-start.34 = (bf16[512,5120]{1,0:T(8,128)(2,1)}, bf16[512,5120]{1,0:T(8,128)(2,1)}, u32[]{:S(2)}, u32[]{:S(2)}) collective-permute-start(bf16[512,5120]{1,0:T(8,128)(2,1)} %get-tuple-element.288), channel_id=1, source_target_pairs={{0,4},{4,0},{8,12},{12,8},{16,20},{20,16},{24,28},{28,24},{1,5},{5... | collective-permute-start | bytes 15728648 | tf_op jit(solution)/shard_map/ppermute | solution.py:557
  236.4 30.7 %collective-permute-start.37 = (bf16[512,4096]{1,0:T(8,128)(2,1)}, bf16[512,4096]{1,0:T(8,128)(2,1)}, u32[]{:S(2)}, u32[]{:S(2)}) collective-permute-start(bf16[512,4096]{1,0:T(8,128)(2,1)} %get-tuple-element.292), channel_id=1, source_target_pairs={{0,4},{4,0},{8,12},{12,8},{16,20},{20,16},{24,28},{28,24},{1,5},{5... | collective-permute-start | bytes 12582920 | tf_op jit(solution)/shard_map/ppermute | solution.py:557
  240.7 31.1 %collective-permute-start.36 = (bf16[256,2560]{1,0:T(8,128)(2,1)}, bf16[256,2560]{1,0:T(8,128)(2,1)}, u32[]{:S(2)}, u32[]{:S(2)}) collective-permute-start(bf16[256,2560]{1,0:T(8,128)(2,1)} %get-tuple-element.404), channel_id=1, source_target_pairs={{0,2},{1,3},{2,0},{3,1},{4,6},{5,7},{6,4},{7,5},{8,10},{9,11},{10,... | collective-permute-start | bytes 3932168 | tf_op jit(solution)/shard_map/ppermute | solution.py:557
  241.6 30.9 %collective-permute-start.35 = (bf16[256,2560]{1,0:T(8,128)(2,1)}, bf16[256,2560]{1,0:T(8,128)(2,1)}, u32[]{:S(2)}, u32[]{:S(2)}) collective-permute-start(bf16[256,2560]{1,0:T(8,128)(2,1)} %get-tuple-element.405), channel_id=1, source_target_pairs={{0,1},{1,0},{2,3},{3,2},{4,5},{5,4},{6,7},{7,6},{8,9},{9,8},{10,11... | collective-permute-start | bytes 3932168 | tf_op jit(solution)/shard_map/ppermute | solution.py:557
  280.3 49.0 %collective-permute-start.39 = (bf16[256,1536]{1,0:T(8,128)(2,1)}, bf16[256,1536]{1,0:T(8,128)(2,1)}, u32[]{:S(2)}, u32[]{:S(2)}) collective-permute-start(bf16[256,1536]{1,0:T(8,128)(2,1)} %add_convert_fusion.3), channel_id=1, source_target_pairs={{0,2},{1,3},{2,0},{3,1},{4,6},{5,7},{6,4},{7,5},{8,10},{9,11},{10,... | collective-permute-start | bytes 2359304 | tf_op jit(solution)/shard_map/ppermute | solution.py:557
  299.1 30.2 %collective-permute-start.38 = (bf16[256,2560]{1,0:T(8,128)(2,1)}, bf16[256,2560]{1,0:T(8,128)(2,1)}, u32[]{:S(2)}, u32[]{:S(2)}) collective-permute-start(bf16[256,2560]{1,0:T(8,128)(2,1)} %add_convert_fusion), channel_id=1, source_target_pairs={{0,1},{1,0},{2,3},{3,2},{4,5},{5,4},{6,7},{7,6},{8,9},{9,8},{10,11... | collective-permute-start | bytes 3932168 | tf_op jit(solution)/shard_map/ppermute | solution.py:557
  329.3 20.6 %collective-permute-start.45 = (bf16[512,2176]{1,0:T(8,128)(2,1)}, bf16[512,2176]{1,0:T(8,128)(2,1)S(1)}, u32[]{:S(2)}, u32[]{:S(2)}) collective-permute-start(bf16[512,2176]{1,0:T(8,128)(2,1)} %get-tuple-element.345), channel_id=1, source_target_pairs={{0,4},{4,0},{8,12},{12,8},{16,20},{20,16},{24,28},{28,24},{1,5},{5... | collective-permute-start | bytes 6684680 | tf_op jit(solution)/shard_map/ppermute | solution.py:557
  335.9 31.7 %collective-permute-start.51 = (bf16[256,512]{1,0:T(8,128)(2,1)}, bf16[256,512]{1,0:T(8,128)(2,1)}, u32[]{:S(2)}, u32[]{:S(2)}) collective-permute-start(bf16[256,512]{1,0:T(8,128)(2,1)} %add_convert_fusion.31), channel_id=1, source_target_pairs={{0,2},{1,3},{2,0},{3,1},{4,6},{5,7},{6,4},{7,5},{8,10},{9,11},{10,... | collective-permute-start | bytes 786440 | tf_op jit(solution)/shard_map/ppermute | solution.py:557
  337.6 30.0 %collective-permute-start.50 = (bf16[256,1024]{1,0:T(8,128)(2,1)S(1)}, bf16[256,1024]{1,0:T(8,128)(2,1)S(1)}, u32[]{:S(2)}, u32[]{:S(2)}) collective-permute-start(bf16[256,1024]{1,0:T(8,128)(2,1)S(1)} %add_convert_fusion.11), channel_id=1, source_target_pairs={{0,1},{1,0},{2,3},{3,2},{4,5},{5,4},{6,7},{7,6},{8,9},{9,8},{10,11... | collective-permute-start | bytes 1572872 | tf_op jit(solution)/shard_map/ppermute | solution.py:557
  (101 other events, 1149.0 us)
